TPU v7x, 32 devices: a whole 2x2x4 slice. The times are simulated.
32 devices in a mesh: tm: 8 (over y, x, core), inp: 4 (over z).
Axes of the slice: x: 2, y: 2, z: 4, core: 2. Of those that a mesh axis runs over, the one named last changes fastest.
Arguments:
- voltages: bfloat16 [1024, 32768], P('inp', 'tm'), may hold values from -6 to 6
- input_gain: float32 [1024], P('inp'), may hold values from 0.5 to 2
- input_feed: int32 [1024], replicated, may hold values from 0 to 511
- beam_grid: int32 [1024], replicated, may hold values from 0 to 511
Outputs:
- visibilities: bfloat16 [512, 2, 1024, 1024], P(('tm', 'inp'))
- beam_power: float32 [512, 1024], P(('tm', 'inp'))
All inputs are finite; a program needn't handle non-finite values.
Results may differ from a plain program's by a relative error of at most 0.0034.
Values may be sent and summed in bfloat16 or wider, within the bound.
No kernel may reach another device: no remote copies, remote signals or barrier semaphores. Data moves between devices by JAX's collectives and lax.ppermute only.
A program may use at most 128 MiB of HBM per device.

v0:
```python
import math

import jax
import jax.numpy as jnp
from jax import lax
from jax.sharding import PartitionSpec as P

L = 1024
CH = 512
TAPS = 4
GRID = 512


def passed_along(block, axis, distance):
    devices = range(lax.axis_size(axis))
    route = [(i - distance, i) for i in devices if i - distance in devices]
    return lax.ppermute(block, axis, route)


def window_table():
    span = TAPS * L
    sample_pos = jnp.arange(span).astype(jnp.float32)
    sinc_part = jnp.sinc((sample_pos - span / 2) / L)
    hann_part = 0.5 - 0.5 * jnp.cos(2.0 * jnp.pi * sample_pos / span)
    return (sinc_part * hann_part).reshape(TAPS, L)


def dft_table(channel):
    lag_index = jnp.arange(L)
    phase_step = lag_index[:, None] * channel[None, :] % L
    radians = 2.0 * jnp.pi * phase_step.astype(jnp.float32) / L
    factor = 1.0 / math.sqrt(L)
    stacked = jnp.stack([jnp.cos(radians), -jnp.sin(radians)], 2) * factor
    return stacked.astype(jnp.bfloat16).reshape(L, 2 * channel.shape[0])


def steer_table(input_feed, beam_grid):
    input_count = input_feed.shape[0]
    phase_step = input_feed[:, None] * beam_grid[None, :] % GRID
    radians = 2.0 * jnp.pi * phase_step.astype(jnp.float32) / GRID
    factor = 1.0 / math.sqrt(input_count)
    cosine = jnp.cos(radians) * factor
    sine_part = jnp.sin(radians) * factor
    top_rows = jnp.concatenate([cosine, sine_part], 1)
    low_rows = jnp.concatenate([-sine_part, cosine], 1)
    return jnp.concatenate([top_rows, low_rows], 0).astype(jnp.bfloat16)


def beam_power_of(spectrum, steer):
    input_count = spectrum.shape[1]
    frame_total = spectrum.shape[2]
    flat = spectrum.reshape(2 * input_count, frame_total)
    beams = lax.dot_general(
        steer, flat, (((0,), (0,)), ((), ())), preferred_element_type=jnp.float32
    )
    beam_count = beams.shape[0] // 2
    return jnp.mean(beams[:beam_count] ** 2 + beams[beam_count:] ** 2, axis=1)


def full_products(spectrum, steer):
    real_part = spectrum[0]
    imag_part = spectrum[1]
    input_count = real_part.shape[0]
    frame_total = real_part.shape[1]
    stacked = jnp.concatenate([real_part, imag_part], 1)
    rotated = jnp.concatenate([imag_part, -real_part], 1)
    both = jnp.concatenate([stacked, rotated], 0)
    products = lax.dot_general(
        both, stacked, (((1,), (1,)), ((), ())), preferred_element_type=jnp.float32
    )
    visible = (products / frame_total).reshape(2, input_count, input_count).astype(jnp.bfloat16)
    return (visible, beam_power_of(spectrum, steer))


def on_device(voltages, input_gain, input_feed, beam_grid):
    local_rows = voltages.shape[0]
    frame_count = voltages.shape[1] // L
    input_count = input_feed.shape[0]
    n_time = lax.axis_size("tm")
    n_input = lax.axis_size("inp")
    per_dev = CH // (n_time * n_input)
    head_part = voltages[:, : (TAPS - 1) * L]
    later = passed_along(head_part, "tm", -1)
    joined = jnp.concatenate([voltages, later], 1)
    window = window_table()
    summed = jnp.zeros((local_rows, frame_count, L), jnp.float32)
    for tap in range(TAPS):
        piece = joined[:, tap * L : tap * L + frame_count * L].reshape(local_rows, frame_count, L)
        summed = summed + piece.astype(jnp.float32) * window[tap]
    filtered = (summed * input_gain[:, None, None]).astype(jnp.bfloat16)
    channel_order = jnp.arange(CH).reshape(n_time, n_input, per_dev)
    table = dft_table(channel_order.reshape(CH))
    spectra = lax.dot_general(
        table, filtered, (((0,), (2,)), ((), ())), preferred_element_type=jnp.float32
    )
    spectra = spectra.astype(jnp.bfloat16)
    blocks = spectra.reshape(n_time, n_input, per_dev, 2, local_rows, frame_count)
    blocks = lax.all_to_all(
        lax.all_to_all(blocks, "tm", split_axis=0, concat_axis=5, tiled=True),
        "inp",
        split_axis=1,
        concat_axis=4,
        tiled=True,
    )
    owned = blocks.reshape(per_dev, 2, input_count, frame_count * n_time)
    steer = steer_table(input_feed, beam_grid)
    visible, power = lax.map(lambda spectrum: full_products(spectrum, steer), owned)
    return (visible, power)


def solution(mesh):
    return jax.shard_map(
        on_device,
        mesh=mesh,
        in_specs=(P("inp", "tm"), P("inp"), P(), P()),
        out_specs=(P(("tm", "inp"), None, None, None), P(("tm", "inp"), None)),
        check_vma=False,
    )
```

profile of v0, /device:TPU:1, one launch (start us, length us, event | category | flops | bytes accessed | tf_op | source)
XLA Modules:
  0.0 301.4 jit_solution(15083207187601768099)
XLA Ops:
  0.6 2.7 slice.43
  3.3 2.0 collective-permute-start
  5.4 8.2 %sine_negate_fusion = (f32[1024,512,1]{1,0,2:T(8,128)S(1)}, f32[1024,512,1]{1,0,2:T(8,128)S(1)}) fusion(), kind=kLoop, calls=%fused_computation.47 | loop fusion | flops 7864320 | bytes 4194304 | tf_op jit(solution)/shard_map/neg | solution.py:33
  13.7 1.9 fusion.16
  15.6 6.4 %copy.25 = bf16[1024,512,2]{0,2,1:T(2,128)(2,1)} copy(bf16[1024,512,2]{1,0,2:T(8,128)(2,1)} %fusion.16) | data formatting | bytes 4194304 | tf_op jit(solution)/shard_map/convert_element_type | solution.py:34
  22.0 4.1 %reshape.147 = bf16[1024,1024,1]{0,1,2:T(8,128)(2,1)} reshape(bf16[1024,512,2]{0,2,1:T(2,128)(2,1)} %copy.25) | data formatting | bytes 4194304 | tf_op jit(solution)/shard_map/convert_element_type | solution.py:34
  26.3 1.5 constant_dynamic-update-slice_fusion.1
  27.8 1.9 multiply_convert_fusion.2
  29.7 3.7 %fusion.27 = bf16[1024,256,4]{1,0,2:T(8,128)(2,1)} fusion(bf16[1024,1024,1]{0,1,2:T(8,128)(2,1)S(1)} %copy-done.1, bf16[32,4,8,1024]{3,2,1,0:T(8,128)(2,1)S(1)} %bitcast.75), kind=kOutput, calls=%fused_computation.51 | convolution fusion | flops 2148532224 | bytes 6291456 | tf_op jit(solution)/shard_map/dot_general | solution.py:93
  33.4 2.7 reshape.145
  36.6 31.5 %all_to_all.33 = bf16[8,4,16,2,256,4]{4,2,5,3,1,0:T(8,128)(2,1)S(1)} all-to-all(bf16[8,4,16,2,256,4]{4,2,5,3,1,0:T(8,128)(2,1)S(1)} %copy.27), channel_id=1, replica_groups=mesh['tm'=8,'inp'=4] {'tm'}, dimensions={0} | all-to-all | bytes 4194304 | tf_op jit(solution)/shard_map/all_to_all | solution.py:99
  68.2 1.6 copy.28
  69.8 4.6 %all-to-all-start.1 = ((bf16[1,4,16,2,256,32]{4,2,5,3,0,1:T(8,128)(2,1)}), bf16[1,4,16,2,256,32]{4,2,5,3,0,1:T(8,128)(2,1)S(1)}, u32[]{:S(2)}, u32[]{:S(2)}) async-start(bf16[1,4,16,2,256,32]{4,2,5,3,0,1:T(8,128)(2,1)} %bitcast.74), calls=%async_computation.1 | async-start | bytes 4194304 | tf_op jit(solution)/shard_map/all_to_all | solution.py:98
  74.4 17.8 %fusion.17 = (bf16[1024,1024]{1,0:T(8,128)(2,1)S(1)}, bf16[1024,1024]{1,0:T(8,128)(2,1)S(1)}, bf16[1024,1024]{1,0:T(8,128)(2,1)S(1)}) fusion(s32[1024]{0:T(1024)S(1)} %copy-done.2, s32[1024]{0:T(1024)S(1)} %copy-done.3), kind=kLoop, calls=%fused_computation.37 | loop fusion | flops 20971520 | bytes 6299648 | tf_op jit(solution)/shard_map/convert.5
  92.1 36.7 %maximum_maximum_fusion = bf16[2048,2048]{1,0:T(8,128)(2,1)} fusion(bf16[1024,1024]{1,0:T(8,128)(2,1)S(1)} %get-tuple-element.70, bf16[1024,1024]{1,0:T(8,128)(2,1)S(1)} %get-tuple-element.69, bf16[1024,1024]{1,0:T(8,128)(2,1)S(1)} %get-tuple-element.68), kind=kLoop, calls=%fused_computation.22 | loop fusion | flops 33554432 | bytes 14680064 | tf_op jit(solution)/shard_map/concatenate | solution.py:46
  128.8 6.1 %copy.32 = bf16[1,1,16,2,4,256,32]{6,5,4,3,2,1,0:T(8,128)(2,1)} copy(bf16[1,1,16,2,4,256,32]{5,2,6,3,4,1,0:T(8,128)(2,1)S(1)} %bitcast.73) | data formatting | bytes 4194304 | tf_op jit(solution)/shard_map/while | solution.py:107
  134.9 166.5 %while.12 = (s32[]{:T(128)}, bf16[16,2,1024,1024]{3,2,1,0:T(8,128)(2,1)}, f32[16,1024]{1,0:T(8,128)}, bf16[16,2,1024,32]{3,2,1,0:T(8,128)(2,1)}, bf16[2048,2048]{1,0:T(8,128)(2,1)}, /*index=5*/s32[]{:T(128)}, s32[]{:T(128)}, s32[]{}) while((s32[]{:T(128)}, bf16[16,2,1024,1024]{3,2,1,0:T(8,128)(2,1)}, f32[16,1024]{1,0:T(8,128)}, ...), condition=%wide.region_2.3_spmd, body=%wide.region_0.2_spmd.sunk | while | flops 542539776 | bytes 47600292 | solution.py:107
  138.4 2.6 constant_dynamic-update-slice_fusion.4
  142.3 1.6 convolution_bitcast_fusion.2
  143.9 1.4 dynamic_update_slice.12
  148.8 2.6 constant_dynamic-update-slice_fusion.4
  152.7 1.6 convolution_bitcast_fusion.2
  154.3 1.4 dynamic_update_slice.12
  159.2 2.6 constant_dynamic-update-slice_fusion.4
  163.1 1.6 convolution_bitcast_fusion.2
  164.8 1.4 dynamic_update_slice.12
  169.7 2.6 constant_dynamic-update-slice_fusion.4
  173.5 1.6 convolution_bitcast_fusion.2
  175.2 1.4 dynamic_update_slice.12
  180.1 2.6 constant_dynamic-update-slice_fusion.4
  183.9 1.6 convolution_bitcast_fusion.2
  190.5 2.6 constant_dynamic-update-slice_fusion.4
  194.3 1.6 convolution_bitcast_fusion.2
  196.0 1.4 dynamic_update_slice.12
  200.9 2.6 constant_dynamic-update-slice_fusion.4
  204.7 1.6 convolution_bitcast_fusion.2
  206.4 1.4 dynamic_update_slice.12
  211.3 2.6 constant_dynamic-update-slice_fusion.4
  215.1 1.6 convolution_bitcast_fusion.2
  216.8 1.4 dynamic_update_slice.12
  221.7 2.6 constant_dynamic-update-slice_fusion.4
  225.5 1.6 convolution_bitcast_fusion.2
  227.2 1.4 dynamic_update_slice.12
  232.1 2.6 constant_dynamic-update-slice_fusion.4
  236.0 1.6 convolution_bitcast_fusion.2
  237.6 1.4 dynamic_update_slice.12
  242.5 2.6 constant_dynamic-update-slice_fusion.4
  246.4 1.6 convolution_bitcast_fusion.2
  248.0 1.4 dynamic_update_slice.12
  252.9 2.6 constant_dynamic-update-slice_fusion.4
  256.8 1.6 convolution_bitcast_fusion.2
  258.4 1.4 dynamic_update_slice.12
  263.3 2.6 constant_dynamic-update-slice_fusion.4
  267.2 1.6 convolution_bitcast_fusion.2
  268.8 1.4 dynamic_update_slice.12
  273.7 2.6 constant_dynamic-update-slice_fusion.4
  277.6 1.6 convolution_bitcast_fusion.2
  279.2 1.4 dynamic_update_slice.12
  284.1 2.6 constant_dynamic-update-slice_fusion.4
  288.0 1.6 convolution_bitcast_fusion.2
  289.6 1.4 dynamic_update_slice.12
  294.5 2.6 constant_dynamic-update-slice_fusion.4
  298.4 1.6 convolution_bitcast_fusion.2
  300.0 1.4 dynamic_update_slice.12
  (201 shorter events, 78.5 us)
Async XLA Ops:
  3.3 23.0 %collective-permute-start = (bf16[256,3072]{1,0:T(8,128)(2,1)}, bf16[256,3072]{1,0:T(8,128)(2,1)}, u32[]{:S(2)}, u32[]{:S(2)}) collective-permute-start(bf16[256,3072]{1,0:T(8,128)(2,1)} %slice.43), channel_id=1, source_target_pairs={{4,0},{8,4},{12,8},{16,12},{20,16},{24,20},{28,24},{5,1},{9,5},{13... | collective-permute-start | bytes 4718600 | tf_op jit(solution)/shard_map/ppermute | solution.py:17
  15.6 10.5 %copy-start = (bf16[256,4096]{1,0:T(8,128)(2,1)S(1)}, bf16[256,4096]{1,0:T(8,128)(2,1)}, u32[]{:S(2)}) copy-start(bf16[256,4096]{1,0:T(8,128)(2,1)} %param.6) | copy-start | bytes 6291460
  26.1 1.7 copy-start.4
  27.8 1.9 copy-start.1
  68.1 6.2 %copy-start.2 = (s32[1024]{0:T(1024)S(1)}, s32[1024]{0:T(1024)}, u32[]{:S(2)}) copy-start(s32[1024]{0:T(1024)} %param.9) | copy-start | bytes 12292
  68.2 6.2 %copy-start.3 = (s32[1024]{0:T(1024)S(1)}, s32[1024]{0:T(1024)}, u32[]{:S(2)}) copy-start(s32[1024]{0:T(1024)} %param.8) | copy-start | bytes 12292
  69.8 59.0 %all-to-all-start.1 = ((bf16[1,4,16,2,256,32]{4,2,5,3,0,1:T(8,128)(2,1)}), bf16[1,4,16,2,256,32]{4,2,5,3,0,1:T(8,128)(2,1)S(1)}, u32[]{:S(2)}, u32[]{:S(2)}) async-start(bf16[1,4,16,2,256,32]{4,2,5,3,0,1:T(8,128)(2,1)} %bitcast.74), calls=%async_computation.1 | async-start | bytes 4194304 | tf_op jit(solution)/shard_map/all_to_all | solution.py:98
  135.9 6.3 %slice-start = ((s8[8388608]{0:T(1024)(128)(4,1)}), s8[4194304]{0:T(1024)(128)(4,1)S(1)}, s32[]{:S(2)}) async-start(s8[8388608]{0:T(1024)(128)(4,1)} %bitcast.68), calls=%async_computation.2 | async-start | bytes 8388608 | tf_op jit(solution)/shard_map/while
  138.4 3.9 %slice-start.1 = ((s8[8388608]{0:T(1024)(128)(4,1)}), s8[4194304]{0:T(1024)(128)(4,1)S(1)}, s32[]{:S(2)}) async-start(s8[8388608]{0:T(1024)(128)(4,1)} %bitcast.68), calls=%async_computation.3 | async-start | bytes 8388608 | tf_op jit(solution)/shard_map/while
  146.3 6.3 %slice-start = ((s8[8388608]{0:T(1024)(128)(4,1)}), s8[4194304]{0:T(1024)(128)(4,1)S(1)}, s32[]{:S(2)}) async-start(s8[8388608]{0:T(1024)(128)(4,1)} %bitcast.68), calls=%async_computation.2 | async-start | bytes 8388608 | tf_op jit(solution)/shard_map/while
  148.8 3.9 %slice-start.1 = ((s8[8388608]{0:T(1024)(128)(4,1)}), s8[4194304]{0:T(1024)(128)(4,1)S(1)}, s32[]{:S(2)}) async-start(s8[8388608]{0:T(1024)(128)(4,1)} %bitcast.68), calls=%async_computation.3 | async-start | bytes 8388608 | tf_op jit(solution)/shard_map/while
  156.8 6.3 %slice-start = ((s8[8388608]{0:T(1024)(128)(4,1)}), s8[4194304]{0:T(1024)(128)(4,1)S(1)}, s32[]{:S(2)}) async-start(s8[8388608]{0:T(1024)(128)(4,1)} %bitcast.68), calls=%async_computation.2 | async-start | bytes 8388608 | tf_op jit(solution)/shard_map/while
  159.2 3.9 %slice-start.1 = ((s8[8388608]{0:T(1024)(128)(4,1)}), s8[4194304]{0:T(1024)(128)(4,1)S(1)}, s32[]{:S(2)}) async-start(s8[8388608]{0:T(1024)(128)(4,1)} %bitcast.68), calls=%async_computation.3 | async-start | bytes 8388608 | tf_op jit(solution)/shard_map/while
  167.2 6.3 %slice-start = ((s8[8388608]{0:T(1024)(128)(4,1)}), s8[4194304]{0:T(1024)(128)(4,1)S(1)}, s32[]{:S(2)}) async-start(s8[8388608]{0:T(1024)(128)(4,1)} %bitcast.68), calls=%async_computation.2 | async-start | bytes 8388608 | tf_op jit(solution)/shard_map/while
  169.6 3.9 %slice-start.1 = ((s8[8388608]{0:T(1024)(128)(4,1)}), s8[4194304]{0:T(1024)(128)(4,1)S(1)}, s32[]{:S(2)}) async-start(s8[8388608]{0:T(1024)(128)(4,1)} %bitcast.68), calls=%async_computation.3 | async-start | bytes 8388608 | tf_op jit(solution)/shard_map/while
  177.6 6.3 %slice-start = ((s8[8388608]{0:T(1024)(128)(4,1)}), s8[4194304]{0:T(1024)(128)(4,1)S(1)}, s32[]{:S(2)}) async-start(s8[8388608]{0:T(1024)(128)(4,1)} %bitcast.68), calls=%async_computation.2 | async-start | bytes 8388608 | tf_op jit(solution)/shard_map/while
  180.0 3.9 %slice-start.1 = ((s8[8388608]{0:T(1024)(128)(4,1)}), s8[4194304]{0:T(1024)(128)(4,1)S(1)}, s32[]{:S(2)}) async-start(s8[8388608]{0:T(1024)(128)(4,1)} %bitcast.68), calls=%async_computation.3 | async-start | bytes 8388608 | tf_op jit(solution)/shard_map/while
  188.0 6.3 %slice-start = ((s8[8388608]{0:T(1024)(128)(4,1)}), s8[4194304]{0:T(1024)(128)(4,1)S(1)}, s32[]{:S(2)}) async-start(s8[8388608]{0:T(1024)(128)(4,1)} %bitcast.68), calls=%async_computation.2 | async-start | bytes 8388608 | tf_op jit(solution)/shard_map/while
  190.5 3.9 %slice-start.1 = ((s8[8388608]{0:T(1024)(128)(4,1)}), s8[4194304]{0:T(1024)(128)(4,1)S(1)}, s32[]{:S(2)}) async-start(s8[8388608]{0:T(1024)(128)(4,1)} %bitcast.68), calls=%async_computation.3 | async-start | bytes 8388608 | tf_op jit(solution)/shard_map/while
  198.4 6.3 %slice-start = ((s8[8388608]{0:T(1024)(128)(4,1)}), s8[4194304]{0:T(1024)(128)(4,1)S(1)}, s32[]{:S(2)}) async-start(s8[8388608]{0:T(1024)(128)(4,1)} %bitcast.68), calls=%async_computation.2 | async-start | bytes 8388608 | tf_op jit(solution)/shard_map/while
  200.9 3.9 %slice-start.1 = ((s8[8388608]{0:T(1024)(128)(4,1)}), s8[4194304]{0:T(1024)(128)(4,1)S(1)}, s32[]{:S(2)}) async-start(s8[8388608]{0:T(1024)(128)(4,1)} %bitcast.68), calls=%async_computation.3 | async-start | bytes 8388608 | tf_op jit(solution)/shard_map/while
  208.8 6.3 %slice-start = ((s8[8388608]{0:T(1024)(128)(4,1)}), s8[4194304]{0:T(1024)(128)(4,1)S(1)}, s32[]{:S(2)}) async-start(s8[8388608]{0:T(1024)(128)(4,1)} %bitcast.68), calls=%async_computation.2 | async-start | bytes 8388608 | tf_op jit(solution)/shard_map/while
  211.3 3.9 %slice-start.1 = ((s8[8388608]{0:T(1024)(128)(4,1)}), s8[4194304]{0:T(1024)(128)(4,1)S(1)}, s32[]{:S(2)}) async-start(s8[8388608]{0:T(1024)(128)(4,1)} %bitcast.68), calls=%async_computation.3 | async-start | bytes 8388608 | tf_op jit(solution)/shard_map/while
  219.2 6.3 %slice-start = ((s8[8388608]{0:T(1024)(128)(4,1)}), s8[4194304]{0:T(1024)(128)(4,1)S(1)}, s32[]{:S(2)}) async-start(s8[8388608]{0:T(1024)(128)(4,1)} %bitcast.68), calls=%async_computation.2 | async-start | bytes 8388608 | tf_op jit(solution)/shard_map/while
  221.7 3.9 %slice-start.1 = ((s8[8388608]{0:T(1024)(128)(4,1)}), s8[4194304]{0:T(1024)(128)(4,1)S(1)}, s32[]{:S(2)}) async-start(s8[8388608]{0:T(1024)(128)(4,1)} %bitcast.68), calls=%async_computation.3 | async-start | bytes 8388608 | tf_op jit(solution)/shard_map/while
  229.6 6.3 %slice-start = ((s8[8388608]{0:T(1024)(128)(4,1)}), s8[4194304]{0:T(1024)(128)(4,1)S(1)}, s32[]{:S(2)}) async-start(s8[8388608]{0:T(1024)(128)(4,1)} %bitcast.68), calls=%async_computation.2 | async-start | bytes 8388608 | tf_op jit(solution)/shard_map/while
  232.1 3.9 %slice-start.1 = ((s8[8388608]{0:T(1024)(128)(4,1)}), s8[4194304]{0:T(1024)(128)(4,1)S(1)}, s32[]{:S(2)}) async-start(s8[8388608]{0:T(1024)(128)(4,1)} %bitcast.68), calls=%async_computation.3 | async-start | bytes 8388608 | tf_op jit(solution)/shard_map/while
  240.0 6.3 %slice-start = ((s8[8388608]{0:T(1024)(128)(4,1)}), s8[4194304]{0:T(1024)(128)(4,1)S(1)}, s32[]{:S(2)}) async-start(s8[8388608]{0:T(1024)(128)(4,1)} %bitcast.68), calls=%async_computation.2 | async-start | bytes 8388608 | tf_op jit(solution)/shard_map/while
  242.5 3.9 %slice-start.1 = ((s8[8388608]{0:T(1024)(128)(4,1)}), s8[4194304]{0:T(1024)(128)(4,1)S(1)}, s32[]{:S(2)}) async-start(s8[8388608]{0:T(1024)(128)(4,1)} %bitcast.68), calls=%async_computation.3 | async-start | bytes 8388608 | tf_op jit(solution)/shard_map/while
  250.4 6.3 %slice-start = ((s8[8388608]{0:T(1024)(128)(4,1)}), s8[4194304]{0:T(1024)(128)(4,1)S(1)}, s32[]{:S(2)}) async-start(s8[8388608]{0:T(1024)(128)(4,1)} %bitcast.68), calls=%async_computation.2 | async-start | bytes 8388608 | tf_op jit(solution)/shard_map/while
  252.9 3.9 %slice-start.1 = ((s8[8388608]{0:T(1024)(128)(4,1)}), s8[4194304]{0:T(1024)(128)(4,1)S(1)}, s32[]{:S(2)}) async-start(s8[8388608]{0:T(1024)(128)(4,1)} %bitcast.68), calls=%async_computation.3 | async-start | bytes 8388608 | tf_op jit(solution)/shard_map/while
  260.8 6.3 %slice-start = ((s8[8388608]{0:T(1024)(128)(4,1)}), s8[4194304]{0:T(1024)(128)(4,1)S(1)}, s32[]{:S(2)}) async-start(s8[8388608]{0:T(1024)(128)(4,1)} %bitcast.68), calls=%async_computation.2 | async-start | bytes 8388608 | tf_op jit(solution)/shard_map/while
  263.3 3.9 %slice-start.1 = ((s8[8388608]{0:T(1024)(128)(4,1)}), s8[4194304]{0:T(1024)(128)(4,1)S(1)}, s32[]{:S(2)}) async-start(s8[8388608]{0:T(1024)(128)(4,1)} %bitcast.68), calls=%async_computation.3 | async-start | bytes 8388608 | tf_op jit(solution)/shard_map/while
  271.2 6.3 %slice-start = ((s8[8388608]{0:T(1024)(128)(4,1)}), s8[4194304]{0:T(1024)(128)(4,1)S(1)}, s32[]{:S(2)}) async-start(s8[8388608]{0:T(1024)(128)(4,1)} %bitcast.68), calls=%async_computation.2 | async-start | bytes 8388608 | tf_op jit(solution)/shard_map/while
  273.7 3.9 %slice-start.1 = ((s8[8388608]{0:T(1024)(128)(4,1)}), s8[4194304]{0:T(1024)(128)(4,1)S(1)}, s32[]{:S(2)}) async-start(s8[8388608]{0:T(1024)(128)(4,1)} %bitcast.68), calls=%async_computation.3 | async-start | bytes 8388608 | tf_op jit(solution)/shard_map/while
  281.6 6.3 %slice-start = ((s8[8388608]{0:T(1024)(128)(4,1)}), s8[4194304]{0:T(1024)(128)(4,1)S(1)}, s32[]{:S(2)}) async-start(s8[8388608]{0:T(1024)(128)(4,1)} %bitcast.68), calls=%async_computation.2 | async-start | bytes 8388608 | tf_op jit(solution)/shard_map/while
  284.1 3.9 %slice-start.1 = ((s8[8388608]{0:T(1024)(128)(4,1)}), s8[4194304]{0:T(1024)(128)(4,1)S(1)}, s32[]{:S(2)}) async-start(s8[8388608]{0:T(1024)(128)(4,1)} %bitcast.68), calls=%async_computation.3 | async-start | bytes 8388608 | tf_op jit(solution)/shard_map/while
  292.0 6.3 %slice-start = ((s8[8388608]{0:T(1024)(128)(4,1)}), s8[4194304]{0:T(1024)(128)(4,1)S(1)}, s32[]{:S(2)}) async-start(s8[8388608]{0:T(1024)(128)(4,1)} %bitcast.68), calls=%async_computation.2 | async-start | bytes 8388608 | tf_op jit(solution)/shard_map/while
  294.5 3.9 %slice-start.1 = ((s8[8388608]{0:T(1024)(128)(4,1)}), s8[4194304]{0:T(1024)(128)(4,1)S(1)}, s32[]{:S(2)}) async-start(s8[8388608]{0:T(1024)(128)(4,1)} %bitcast.68), calls=%async_computation.3 | async-start | bytes 8388608 | tf_op jit(solution)/shard_map/while
where the time goes:
time: 305 us; the launch traced here: 301 us
  local copies, waits for them, and re-layouts  128 us (42%)
  other arithmetic  83.2 us (27%)
  matrix products  50.3 us (16%)
  blocking collectives  31.5 us (10%)
  starting transfers between devices  6.54 us (2%)
    dynamic_update_slice x32, local copies, waits for them, and re-layouts, on_device(): lax.map(lambda spectrum: full_products(spectrum, steer), owned)  63.8 us
    concatenate x1, other arithmetic, steer_table(): return jnp.concatenate([top_rows, low_rows], 0).astype(jnp.bfloat16)  36.7 us
    all_to_all x1, blocking collectives, on_device(): lax.all_to_all(blocks, 'tm', split_axis=0, concat_axis=5, tiled=True)  31.5 us
    dot_general x16, matrix products, beam_power_of(): lax.dot_general(steer, flat, (((0,), (0,)), ((), ())), preferred_element_...  25.2 us
    dot_general x16, matrix products, full_products(): lax.dot_general(both, stacked, (((1,), (1,)), ((), ())), preferred_elemen...  21.4 us
    dynamic_slice x16, local copies, waits for them, and re-layouts, on_device(): lax.map(lambda spectrum: full_products(spectrum, steer), owned)  20.1 us
    squeeze x16, local copies, waits for them, and re-layouts, full_products(): imag_part = spectrum[1]  18 us
    another operation x1, other arithmetic  17.8 us
  transfers between devices with their start and end apart: 2, of which 0 were waited for; matrix products, arithmetic and copies ran while one was open for 25% of the time, Pallas kernels for 0%

commit v1 on v0

v1 whole, which is shorter than its diff:
```python
import functools
import math

import jax
import jax.numpy as jnp
import numpy as np
from jax import lax
from jax.experimental import pallas as pl
from jax.experimental.pallas import tpu as pltpu
from jax.sharding import PartitionSpec as P

L = 1024
CH = 512
TAPS = 4
GRID = 512
SUB = 4
AXES = ("tm", "inp")
MIB = 2**20


def window_table():
    span = TAPS * L
    pos = np.arange(span, dtype=np.float64)
    window = np.sinc((pos - span / 2) / L) * (0.5 - 0.5 * np.cos(2.0 * np.pi * pos / span))
    return window.astype(np.float32).reshape(TAPS, L)


def dft_rows():
    step = np.arange(CH)[:, None] * np.arange(L)[None, :] % L
    radians = 2.0 * np.pi * step / L
    both = np.stack([np.cos(radians), -np.sin(radians)], 1) / math.sqrt(L)
    return both.reshape(2 * CH, L).astype(jnp.bfloat16)


def steer_grid(input_count):
    step = np.arange(GRID)[:, None] * np.arange(GRID)[None, :] % GRID
    radians = 2.0 * np.pi * step / GRID
    both = np.stack([np.cos(radians), np.sin(radians)], 0) / math.sqrt(input_count)
    return both.astype(jnp.bfloat16)


def sort_rows(slots):
    order = np.arange(slots * SUB * 2).reshape(slots, SUB, 2).transpose(1, 2, 0).reshape(-1)
    return np.eye(slots * SUB * 2, dtype=np.float32)[order].astype(jnp.bfloat16)


def channelize_kernel(frames, cuts, v_ref, later_ref, gain_ref, window_ref, table_ref, *out_refs):
    frame_count = v_ref.shape[1] // L
    dests = out_refs[0].shape[0]
    for at, frame in enumerate(frames):
        total = None
        for tap in range(TAPS):
            source = frame + tap
            if source < frame_count:
                piece = v_ref[:, source * L : (source + 1) * L]
            else:
                piece = later_ref[:, (source - frame_count) * L : (source - frame_count + 1) * L]
            term = piece.astype(jnp.float32) * window_ref[tap : tap + 1, :]
            total = term if total is None else total + term
        filtered = (total * gain_ref[...]).astype(jnp.bfloat16)
        spectra = lax.dot_general(
            table_ref[...], filtered, (((1,), (1,)), ((), ())), preferred_element_type=jnp.float32
        ).astype(jnp.bfloat16)
        spectra = spectra.reshape(dests, spectra.shape[0] // dests, spectra.shape[1])
        row = 0
        for out_ref, rows in zip(out_refs, cuts):
            out_ref[:, at * rows : (at + 1) * rows, :] = spectra[:, row : row + rows, :]
            row += rows


def channelize(frames, cuts, dests, voltages, later, gain, window, table):
    rows = voltages.shape[0]
    cost = pl.CostEstimate(
        flops=2 * len(frames) * rows * L * 2 * CH,
        bytes_accessed=2 * (voltages.size + table.size + len(frames) * rows * 2 * CH),
        transcendentals=0,
    )
    return pl.pallas_call(
        functools.partial(channelize_kernel, frames, cuts),
        out_shape=[
            jax.ShapeDtypeStruct((dests, len(frames) * cut, rows), jnp.bfloat16) for cut in cuts
        ],
        compiler_params=pltpu.CompilerParams(vmem_limit_bytes=32 * MIB),
        cost_estimate=cost,
        name="channelize",
    )(voltages, later, gain, window, table)


def steer_kernel(feed_ref, beam_ref, table_ref, out_ref):
    inputs = feed_ref.shape[0]
    beams = beam_ref.shape[1]
    feed = lax.rem(feed_ref[...], GRID)
    beam = lax.rem(beam_ref[...], GRID)
    pick_feed = (lax.broadcasted_iota(jnp.int32, (inputs, GRID), 1) == feed)
    pick_feed = pick_feed.astype(jnp.float32).astype(jnp.bfloat16)
    pick_beam = (lax.broadcasted_iota(jnp.int32, (GRID, beams), 0) == beam)
    pick_beam = pick_beam.astype(jnp.float32).astype(jnp.bfloat16)
    for part in range(2):
        rows = jnp.dot(pick_feed, table_ref[part], preferred_element_type=jnp.float32)
        out_ref[part] = jnp.dot(
            rows.astype(jnp.bfloat16), pick_beam, preferred_element_type=jnp.float32
        ).astype(jnp.bfloat16)


def steering(input_feed, beam_grid, table):
    inputs, beams = input_feed.shape[0], beam_grid.shape[0]
    cost = pl.CostEstimate(
        flops=4 * inputs * GRID * (GRID + beams), bytes_accessed=4 * inputs * beams, transcendentals=0
    )
    return pl.pallas_call(
        steer_kernel,
        out_shape=jax.ShapeDtypeStruct((2, inputs, beams), jnp.bfloat16),
        compiler_params=pltpu.CompilerParams(vmem_limit_bytes=32 * MIB),
        cost_estimate=cost,
        name="steering",
    )(input_feed.reshape(inputs, 1), beam_grid.reshape(1, beams), table)


def products_kernel(
    n_time, n_input, frame_count, first, count, x0_ref, xl_ref, sort_ref, steer_ref, *rest
):
    vis_ref, power_ref, arrived, ordered = rest[-4:]
    step = pl.program_id(0)
    half = n_time * frame_count
    rows_per = 2 * half
    width = x0_ref.shape[2]
    inputs = n_input * width
    tile = 2 * SUB

    @pl.when(step % SUB == 0)
    def _():
        sub = step // SUB
        for t in range(n_time):
            for i in range(n_input):
                source = t * n_input + i
                lanes = slice(i * width, (i + 1) * width)
                for f in range(frame_count):
                    slot = (t * frame_count + f) * tile
                    if f == 0:
                        at = pl.multiple_of((first // SUB + sub) * tile, tile)
                        piece = x0_ref[source, pl.ds(at, tile), :]
                    else:
                        at = pl.multiple_of(((f - 1) * (count // SUB) + sub) * tile, tile)
                        piece = xl_ref[source, pl.ds(at, tile), :]
                    arrived[slot : slot + tile, lanes] = piece
        sorted_rows = jnp.dot(sort_ref[...], arrived[...], preferred_element_type=jnp.float32)
        ordered[...] = sorted_rows.astype(jnp.bfloat16)
        beams = steer_ref.shape[2]
        chunk = min(beams, 256)
        for b in range(0, beams, chunk):
            lanes = slice(b, b + chunk)
            cos_part = jnp.dot(ordered[...], steer_ref[0, :, lanes], preferred_element_type=jnp.float32)
            sin_part = jnp.dot(ordered[...], steer_ref[1, :, lanes], preferred_element_type=jnp.float32)
            for c in range(SUB):
                re = slice(c * rows_per, c * rows_per + half)
                im = slice(c * rows_per + half, (c + 1) * rows_per)
                beam_re = cos_part[re] - sin_part[im]
                beam_im = sin_part[re] + cos_part[im]
                power = jnp.sum(beam_re * beam_re + beam_im * beam_im, axis=0, keepdims=True)
                power_ref[0, c : c + 1, lanes] = power * (1.0 / half)

    at = pl.multiple_of((step % SUB) * rows_per, rows_per)
    both = ordered[pl.ds(at, rows_per), :]
    re, im = both[:half], both[half:]
    left = jnp.concatenate([re, im, im, -re], 0).T
    right = both * jnp.asarray(1.0 / half, jnp.bfloat16)
    zero = jnp.zeros_like(right)
    chunk = min(inputs, 256)
    for part in range(2):
        against = jnp.concatenate([right, zero] if part == 0 else [zero, right], 0)
        for b in range(0, inputs, chunk):
            lanes = slice(b, b + chunk)
            vis_ref[0, part, :, lanes] = jnp.dot(
                left, against[:, lanes], preferred_element_type=jnp.float32
            ).astype(jnp.bfloat16)


def products(sizes, first, count, x0, xl, sort, steer, so_far):
    n_time, n_input, frame_count, per_dev = sizes
    inputs = n_input * x0.shape[2]
    beams = steer.shape[2]
    whole = pl.BlockSpec(memory_space=pltpu.VMEM)
    rows = 2 * n_time * frame_count * SUB
    cost = pl.CostEstimate(
        flops=count * 2 * rows // SUB * inputs * (2 * inputs + 2 * beams),
        bytes_accessed=count * 4 * inputs * inputs + 4 * inputs * beams,
        transcendentals=0,
    )
    operands = [x0, xl, sort, steer]
    specs = [whole] * 4
    aliases = {}
    if so_far is not None:
        aliases = {len(operands): 0}
        operands.append(so_far)
        specs.append(pl.BlockSpec(memory_space=pl.ANY))
    vis, power = pl.pallas_call(
        functools.partial(products_kernel, n_time, n_input, frame_count, first, count),
        grid=(count,),
        in_specs=specs,
        out_specs=[
            pl.BlockSpec((1, 2, inputs, inputs), lambda c: (first + c, 0, 0, 0)),
            pl.BlockSpec((1, SUB, beams), lambda c: (c // SUB, 0, 0)),
        ],
        out_shape=[
            jax.ShapeDtypeStruct((per_dev, 2, inputs, inputs), jnp.bfloat16),
            jax.ShapeDtypeStruct((count // SUB, SUB, beams), jnp.float32),
        ],
        scratch_shapes=[
            pltpu.VMEM((rows, inputs), jnp.bfloat16),
            pltpu.VMEM((rows, inputs), jnp.bfloat16),
        ],
        input_output_aliases=aliases,
        compiler_params=pltpu.CompilerParams(vmem_limit_bytes=40 * MIB),
        cost_estimate=cost,
        name="products",
    )(*operands)
    return vis, power.reshape(count, beams)


def exchanged(block):
    return lax.all_to_all(block, AXES, 0, 0, tiled=True)


def in_pieces(voltages, input_gain, input_feed, beam_grid):
    frame_count = voltages.shape[1] // L
    n_time = lax.axis_size("tm")
    n_input = lax.axis_size("inp")
    dests = n_time * n_input
    per_dev = CH // dests
    last = max(SUB, per_dev // 4 // SUB * SUB)
    counts = (per_dev - last, last)

    later = lax.ppermute(
        voltages[:, : (TAPS - 1) * L], "tm", [(i + 1, i) for i in range(n_time - 1)]
    )
    window = jnp.asarray(window_table())
    table = jnp.asarray(dft_rows())
    gain = input_gain.reshape(-1, 1)
    sort = jnp.asarray(sort_rows(n_time * frame_count))

    (first_frame,) = channelize(
        (0,), (2 * per_dev,), dests, voltages, voltages[:8, :128], gain, window, table
    )
    x0 = exchanged(first_frame)
    parts = channelize(
        tuple(range(1, frame_count)),
        tuple(2 * c for c in counts),
        dests,
        voltages,
        later,
        gain,
        window,
        table,
    )
    steer = steering(input_feed, beam_grid, jnp.asarray(steer_grid(input_feed.shape[0])))
    send_a, x0, steer = lax.optimization_barrier((parts[0], x0, steer))
    xa = exchanged(send_a)
    send_b, xa = lax.optimization_barrier((parts[1], xa))
    xb = exchanged(send_b)
    sizes = (n_time, n_input, frame_count, per_dev)
    vis, power_a = products(sizes, 0, counts[0], x0, xa, sort, steer, None)
    vis, power_b = products(sizes, counts[0], counts[1], x0, xb, sort, steer, vis)
    return vis, jnp.concatenate([power_a, power_b], 0)


def whole_channel(spectrum, steer):
    real_part, imag_part = spectrum[0], spectrum[1]
    input_count, frame_total = real_part.shape
    stacked = jnp.concatenate([real_part, imag_part], 1)
    rotated = jnp.concatenate([imag_part, -real_part], 1)
    both = jnp.concatenate([stacked, rotated], 0)
    found = lax.dot_general(
        both, stacked, (((1,), (1,)), ((), ())), preferred_element_type=jnp.float32
    )
    visible = (found / frame_total).reshape(2, input_count, input_count).astype(jnp.bfloat16)
    cos_part, sin_part = [
        lax.dot_general(
            spectrum, part, (((1,), (0,)), ((), ())), preferred_element_type=jnp.float32
        )
        for part in steer
    ]
    beam_re = cos_part[0] - sin_part[1]
    beam_im = sin_part[0] + cos_part[1]
    return visible, jnp.mean(beam_re**2 + beam_im**2, axis=0)


def at_once(voltages, input_gain, input_feed, beam_grid):
    rows = voltages.shape[0]
    frame_count = voltages.shape[1] // L
    n_time = lax.axis_size("tm")
    n_input = lax.axis_size("inp")
    dests = n_time * n_input
    per_dev = CH // dests
    later = lax.ppermute(
        voltages[:, : (TAPS - 1) * L], "tm", [(i + 1, i) for i in range(n_time - 1)]
    )
    joined = jnp.concatenate([voltages, later], 1)
    window = jnp.asarray(window_table())
    summed = jnp.zeros((rows, frame_count, L), jnp.float32)
    for tap in range(TAPS):
        piece = joined[:, tap * L : (tap + frame_count) * L].reshape(rows, frame_count, L)
        summed = summed + piece.astype(jnp.float32) * window[tap]
    filtered = (summed * input_gain[:, None, None]).astype(jnp.bfloat16)
    spectra = lax.dot_general(
        jnp.asarray(dft_rows()),
        filtered,
        (((1,), (2,)), ((), ())),
        preferred_element_type=jnp.float32,
    ).astype(jnp.bfloat16)
    blocks = exchanged(spectra.reshape(dests, per_dev * 2, rows, frame_count))
    blocks = blocks.reshape(n_time, n_input, per_dev, 2, rows, frame_count)
    owned = blocks.transpose(2, 3, 1, 4, 0, 5)
    owned = owned.reshape(per_dev, 2, n_input * rows, n_time * frame_count)
    steer = steering(input_feed, beam_grid, jnp.asarray(steer_grid(input_feed.shape[0])))
    return lax.map(lambda spectrum: whole_channel(spectrum, steer), owned)


def on_device(voltages, input_gain, input_feed, beam_grid):
    per_dev = CH // (lax.axis_size("tm") * lax.axis_size("inp"))
    slots = lax.axis_size("tm") * (voltages.shape[1] // L)
    if per_dev % SUB == 0 and per_dev >= 2 * SUB and slots % 16 == 0 and slots & (slots - 1) == 0:
        return in_pieces(voltages, input_gain, input_feed, beam_grid)
    return at_once(voltages, input_gain, input_feed, beam_grid)


def solution(mesh):
    return jax.shard_map(
        on_device,
        mesh=mesh,
        in_specs=(P("inp", "tm"), P("inp"), P(), P()),
        out_specs=(P(("tm", "inp"), None, None, None), P(("tm", "inp"), None)),
        check_vma=False,
    )
```

time: 305 us -> 116 us (0.38)
  local copies, waits for them, and re-layouts: 128 us -> 13.3 us
  other arithmetic: 83.2 us -> 0.64 us
  matrix products: 50.3 us -> 0 us
  Pallas kernels: 0 us -> 44.4 us
  waiting for transfers between devices: 0.01 us -> 6.43 us
  starting transfers between devices: 6.54 us -> 12.7 us
  blocking collectives: 31.5 us -> 36.9 us
    dynamic_update_slice x32 -> x0, local copies, waits for them, and re-layouts: 63.8 us -> none  [on_device(): lax.map(lambda spectrum: full_products(spectrum, steer), owned)]
    dot_general x33 -> x0, matrix products: 50.3 us -> none  [the longest x16 25.2 us: beam_power_of(): lax.dot_general(steer, flat, (((0,), (0,)), ((), ())), preferred_element_...]
    pallas_call x0 -> x5, Pallas kernels: none -> 44.4 us  [the longest x2 34.7 us: products(): pl.pallas_call(functools.partial(products_kernel, n_time, n_input, frame_...]
    concatenate x1, other arithmetic: 36.7 us -> 0.64 us  [in_pieces(): return (vis, jnp.concatenate([power_a, power_b], 0))]
    neg x17 -> x0, other arithmetic: 24.2 us -> none  [the longest x16 16 us: full_products(): rotated = jnp.concatenate([imag_part, -real_part], 1)]
    dynamic_slice x16 -> x0, local copies, waits for them, and re-layouts: 20.1 us -> none  [on_device(): lax.map(lambda spectrum: full_products(spectrum, steer), owned)]
    squeeze x16 -> x0, local copies, waits for them, and re-layouts: 18 us -> none  [full_products(): imag_part = spectrum[1]]
    another operation x1 -> x0, other arithmetic: 17.8 us -> none
  transfers between devices with their start and end apart: 2 -> 3, of which waited for: 0 -> 1; matrix products, arithmetic and copies ran while one was open for 25% -> 0% of each run, Pallas kernels for 0% -> 30%
where the time goes in v1:
time: 116 us; the launch traced here: 115 us
  Pallas kernels  44.4 us (38%)
  blocking collectives  36.9 us (32%)
  local copies, waits for them, and re-layouts  13.3 us (11%)
  starting transfers between devices  12.7 us (11%)
  waiting for transfers between devices  6.43 us (6%)
    all_to_all x1, blocking collectives, exchanged(): return lax.all_to_all(block, AXES, 0, 0, tiled=True)  36.9 us
    pallas_call x2, Pallas kernels, products(): pl.pallas_call(functools.partial(products_kernel, n_time, n_input, frame_...  34.7 us
    all_to_all x2, starting transfers between devices, exchanged(): return lax.all_to_all(block, AXES, 0, 0, tiled=True)  10.7 us
    unnamed x26, local copies, waits for them, and re-layouts  10.2 us
    ppermute x1, waiting for transfers between devices, in_pieces(): lax.ppermute(voltages[:, :(TAPS - 1) * L], 'tm', [(i + 1, i) for i in ran...  6.42 us
    pallas_call x2, Pallas kernels, channelize(): pl.pallas_call(functools.partial(channelize_kernel, frames, cuts), out_sh...  6.16 us
    pallas_call x1, Pallas kernels, steering(): pl.pallas_call(steer_kernel, out_shape=jax.ShapeDtypeStruct((2, inputs, b...  3.54 us
    slice x1, local copies, waits for them, and re-layouts, in_pieces(): voltages[:, :(TAPS - 1) * L]  2.8 us
  transfers between devices with their start and end apart: 3, of which 1 were waited for; matrix products, arithmetic and copies ran while one was open for 0% of the time, Pallas kernels for 30%

profile of v1, /device:TPU:1, one launch (start us, length us, event | category | flops | bytes accessed | tf_op | source)
XLA Modules:
  0.0 115.2 jit_solution(2608743882711752953)
XLA Ops:
  0.6 0.0 copy-start.8
  0.6 0.0 copy-start
  0.7 0.0 copy-start.12
  0.7 2.8 %slice.6 = bf16[256,3072]{1,0:T(8,128)(2,1)} slice(bf16[256,4096]{1,0:T(8,128)(2,1)} %v_ref.3), slice={[0:256], [0:3072]} | slice | bytes 3145728 | tf_op jit(solution)/shard_map/slice | solution.py:234
  3.5 2.0 %collective-permute-start = (bf16[256,3072]{1,0:T(8,128)(2,1)}, bf16[256,3072]{1,0:T(8,128)(2,1)}, u32[]{:S(2)}, u32[]{:S(2)}) collective-permute-start(bf16[256,3072]{1,0:T(8,128)(2,1)} %slice.6), channel_id=1, source_target_pairs={{4,0},{8,4},{12,8},{16,12},{20,16},{24,20},{28,24},{5,1},{9,5},{13... | collective-permute-start | bytes 4718600 | tf_op jit(solution)/shard_map/ppermute | solution.py:233
  5.4 0.0 copy-done
  5.4 0.0 copy-done.12
  5.5 0.1 copy.11.gain_ref
  5.6 0.0 copy-done.8
  5.6 0.0 copy-start.4
  5.6 1.6 %copy-done.4 = bf16[1024,1024]{1,0:T(8,128)(2,1)S(1)} copy-done((bf16[1024,1024]{1,0:T(8,128)(2,1)S(1)}, bf16[1024,1024]{1,0:T(8,128)(2,1)}, u32[]{:S(2)}) %copy-start.4) | copy-done | bytes 2097176
  7.2 0.0 copy-start.11
  7.2 0.0 copy-start.9
  7.2 1.8 %channelize.3 = bf16[32,32,256]{2,1,0:T(8,128)(2,1)} custom-call(bf16[256,4096]{1,0:T(8,128)(2,1)S(1)} %copy-done, bf16[8,128]{1,0:T(8,128)(2,1)S(1)} %slice.7.later_ref, f32[256,1]{1,0:T(8,128)S(1)} %copy.11.gain_ref, f32[4,1024]{1,0:T(4,128)S(1)} %copy-done.8, bf16[1024,1024]{1,0:T(8,128)(2,1)S(1)} %copy-done.4), custom_call_target="tpu_custom_call" | custom-call | flops 536870912 | bytes 4718592 | tf_op jit(solution)/shard_map/channelize/pallas_call | solution.py:78
  9.0 8.3 %all-to-all-start = ((bf16[32,32,256]{2,1,0:T(8,128)(2,1)}), bf16[32,32,256]{2,1,0:T(8,128)(2,1)S(1)}, u32[]{:S(2)}, u32[]{:S(2)}) async-start(bf16[32,32,256]{2,1,0:T(8,128)(2,1)} %channelize.3), calls=%async_computation | async-start | bytes 1048576 | tf_op jit(solution)/shard_map/all_to_all | solution.py:221
  17.4 0.0 copy-done.11
  17.4 0.2 copy.13.feed_ref
  17.6 0.0 copy-done.9
  17.6 0.0 copy-start.10
  17.6 1.2 %copy-done.10 = bf16[2,512,512]{2,1,0:T(8,128)(2,1)S(1)} copy-done((bf16[2,512,512]{2,1,0:T(8,128)(2,1)S(1)}, bf16[2,512,512]{2,1,0:T(8,128)(2,1)}, u32[]{:S(2)}) %copy-start.10) | copy-done | bytes 1048600
  18.9 0.0 copy-start.5
  18.9 3.5 %steering.1.steer_ref = bf16[2,1024,1024]{2,1,0:T(8,128)(2,1)S(1)} custom-call(s32[1024,1]{1,0:T(8,128)S(1)} %copy.13.feed_ref, s32[1,1024]{1,0:T(1,128)S(1)} %bitcast.5, bf16[2,512,512]{2,1,0:T(8,128)(2,1)S(1)} %copy-done.10), custom_call_target="tpu_custom_call" | custom-call | flops 3221225472 | bytes 4194304 | tf_op jit(solution)/shard_map/steering/pallas_call | solution.py:110
  22.4 0.0 copy-start.1
  22.4 1.9 %copy-done.1 = bf16[2,1024,1024]{2,1,0:T(8,128)(2,1)} copy-done((bf16[2,1024,1024]{2,1,0:T(8,128)(2,1)}, bf16[2,1024,1024]{2,1,0:T(8,128)(2,1)S(1)}, u32[]{:S(2)}) %copy-start.1) | copy-done | bytes 4194328
  24.4 6.4 %collective-permute-done.later_ref = bf16[256,3072]{1,0:T(8,128)(2,1)} collective-permute-done((bf16[256,3072]{1,0:T(8,128)(2,1)}, bf16[256,3072]{1,0:T(8,128)(2,1)}, u32[]{:S(2)}, u32[]{:S(2)}) %collective-permute-start) | collective-permute-done | bytes 1572896 | tf_op jit(solution)/shard_map/ppermute | solution.py:233
  30.8 0.0 copy-done.5
  30.8 4.3 %channelize.2 = (bf16[32,72,256]{2,1,0:T(8,128)(2,1)S(1)}, bf16[32,24,256]{2,1,0:T(8,128)(2,1)}) custom-call(bf16[256,4096]{1,0:T(8,128)(2,1)S(1)} %copy-done, bf16[256,3072]{1,0:T(8,128)(2,1)} %collective-permute-done.later_ref, f32[256,1]{1,0:T(8,128)S(1)} %copy.11.gain_ref, f32[4,1024]{1,0:T(4,128)S(1)} %copy-done.8, bf16[1024,1024]{1,0:T(8,128)(2,1)S(1)} %copy-done.5), custom_call_target="tpu_custom_call" | custom-call | flops 1610612736 | bytes 5767168 | tf_op jit(solution)/shard_map/channelize/pallas_call | solution.py:78
  35.1 0.0 copy-start.6
  35.1 1.0 copy-done.6
  36.1 0.0 copy-start.7
  36.1 0.0 all-to-all-done.x0_ref
  36.1 36.9 %all_to_all.15.xl_ref = bf16[32,72,256]{2,1,0:T(8,128)(2,1)S(1)} all-to-all(bf16[32,72,256]{2,1,0:T(8,128)(2,1)} %copy-done.6), channel_id=1, replica_groups=mesh['tm'=8,'inp'=4] {'tm','inp'}, dimensions={0} | all-to-all | bytes 2359296 | tf_op jit(solution)/shard_map/all_to_all | solution.py:221
  73.0 2.4 %all-to-all-start.2 = ((bf16[32,24,256]{2,1,0:T(8,128)(2,1)}), bf16[32,24,256]{2,1,0:T(8,128)(2,1)S(1)}, u32[]{:S(2)}, u32[]{:S(2)}) async-start(bf16[32,24,256]{2,1,0:T(8,128)(2,1)} %get-tuple-element.17), calls=%async_computation.2 | async-start | bytes 786432 | tf_op jit(solution)/shard_map/all_to_all | solution.py:221
  75.4 0.0 copy-done.7
  75.5 0.0 copy-start.2
  75.5 2.2 %copy-done.2 = bf16[2,1024,1024]{2,1,0:T(8,128)(2,1)S(1)} copy-done((bf16[2,1024,1024]{2,1,0:T(8,128)(2,1)S(1)}, bf16[2,1024,1024]{2,1,0:T(8,128)(2,1)}, u32[]{:S(2)}) %copy-start.2) | copy-done | bytes 4194328
  77.6 25.4 %products.2 = (bf16[16,2,1024,1024]{3,2,1,0:T(8,128)(2,1)}, f32[3,4,1024]{2,1,0:T(4,128)S(1)}) custom-call(bf16[32,32,256]{2,1,0:T(8,128)(2,1)S(1)} %all-to-all-done.x0_ref, bf16[32,72,256]{2,1,0:T(8,128)(2,1)S(1)} %all_to_all.15.xl_ref, bf16[256,256]{1,0:T(8,128)(2,1)S(1)} %copy-done.7, bf16[2,1024,1024]{2,1,0:T(8,128)(2,1)S(1)} %copy-done.2), custom_call_target="tpu_custom_call" | custom-call | flops 6442450944 | bytes 54525952 | tf_op jit(solution)/shard_map/products/pallas_call | solution.py:196
  103.0 0.0 all-to-all-done.2.xl_ref
  103.0 0.0 copy-start.3
  103.0 2.2 %copy-done.3 = bf16[2,1024,1024]{2,1,0:T(8,128)(2,1)S(1)} copy-done((bf16[2,1024,1024]{2,1,0:T(8,128)(2,1)S(1)}, bf16[2,1024,1024]{2,1,0:T(8,128)(2,1)}, u32[]{:S(2)}) %copy-start.3) | copy-done | bytes 4194328
  105.2 9.4 %products.3 = (bf16[16,2,1024,1024]{3,2,1,0:T(8,128)(2,1)}, f32[1,4,1024]{2,1,0:T(4,128)S(1)}) custom-call(bf16[32,32,256]{2,1,0:T(8,128)(2,1)S(1)} %all-to-all-done.x0_ref, bf16[32,24,256]{2,1,0:T(8,128)(2,1)S(1)} %all-to-all-done.2.xl_ref, bf16[256,256]{1,0:T(8,128)(2,1)S(1)} %copy-done.7, ...), custom_call_target="tpu_custom_call", output_to_operand_aliasing={{0}: (4, {})} | custom-call | flops 2147483648 | bytes 20971520 | tf_op jit(solution)/shard_map/products/pallas_call | solution.py:196
  114.6 0.6 pad_maximum_fusion
  (2 shorter events, 0.0 us)
Async XLA Ops:
  0.6 5.0 %copy-start.8 = (f32[4,1024]{1,0:T(4,128)S(1)}, f32[4,1024]{1,0:T(4,128)}, u32[]{:S(2)}) copy-start(f32[4,1024]{1,0:T(4,128)} %constant.8.clone.window_ref) | copy-start | bytes 49156
  0.6 4.8 %copy-start = (bf16[256,4096]{1,0:T(8,128)(2,1)S(1)}, bf16[256,4096]{1,0:T(8,128)(2,1)}, u32[]{:S(2)}) copy-start(bf16[256,4096]{1,0:T(8,128)(2,1)} %v_ref.3) | copy-start | bytes 6291460
  0.7 4.8 %copy-start.12 = (f32[256]{0:T(256)S(1)}, f32[256]{0:T(256)}, u32[]{:S(2)}) copy-start(f32[256]{0:T(256)} %param.9) | copy-start | bytes 3076
  3.5 27.3 %collective-permute-start = (bf16[256,3072]{1,0:T(8,128)(2,1)}, bf16[256,3072]{1,0:T(8,128)(2,1)}, u32[]{:S(2)}, u32[]{:S(2)}) collective-permute-start(bf16[256,3072]{1,0:T(8,128)(2,1)} %slice.6), channel_id=1, source_target_pairs={{4,0},{8,4},{12,8},{16,12},{20,16},{24,20},{28,24},{5,1},{9,5},{13... | collective-permute-start | bytes 4718600 | tf_op jit(solution)/shard_map/ppermute | solution.py:233
  5.6 1.6 %copy-start.4 = (bf16[1024,1024]{1,0:T(8,128)(2,1)S(1)}, bf16[1024,1024]{1,0:T(8,128)(2,1)}, u32[]{:S(2)}) copy-start(bf16[1024,1024]{1,0:T(8,128)(2,1)} %constant.9.clone.table_ref) | copy-start | bytes 6291460
  7.2 10.2 %copy-start.11 = (s32[1024]{0:T(1024)S(1)}, s32[1024]{0:T(1024)}, u32[]{:S(2)}) copy-start(s32[1024]{0:T(1024)} %param.10) | copy-start | bytes 12292
  7.2 10.4 %copy-start.9 = (s32[1024]{0:T(1024)S(1)}, s32[1024]{0:T(1024)}, u32[]{:S(2)}) copy-start(s32[1024]{0:T(1024)} %param.11) | copy-start | bytes 12292
  9.0 27.1 %all-to-all-start = ((bf16[32,32,256]{2,1,0:T(8,128)(2,1)}), bf16[32,32,256]{2,1,0:T(8,128)(2,1)S(1)}, u32[]{:S(2)}, u32[]{:S(2)}) async-start(bf16[32,32,256]{2,1,0:T(8,128)(2,1)} %channelize.3), calls=%async_computation | async-start | bytes 1048576 | tf_op jit(solution)/shard_map/all_to_all | solution.py:221
  17.6 1.2 %copy-start.10 = (bf16[2,512,512]{2,1,0:T(8,128)(2,1)S(1)}, bf16[2,512,512]{2,1,0:T(8,128)(2,1)}, u32[]{:S(2)}) copy-start(bf16[2,512,512]{2,1,0:T(8,128)(2,1)} %constant.11.clone.table_ref) | copy-start | bytes 3145732
  18.9 11.9 %copy-start.5 = (bf16[1024,1024]{1,0:T(8,128)(2,1)S(1)}, bf16[1024,1024]{1,0:T(8,128)(2,1)}, u32[]{:S(2)}) copy-start(bf16[1024,1024]{1,0:T(8,128)(2,1)} %constant.9.clone.table_ref) | copy-start | bytes 6291460
  22.4 1.9 %copy-start.1 = (bf16[2,1024,1024]{2,1,0:T(8,128)(2,1)}, bf16[2,1024,1024]{2,1,0:T(8,128)(2,1)S(1)}, u32[]{:S(2)}) copy-start(bf16[2,1024,1024]{2,1,0:T(8,128)(2,1)S(1)} %steering.1.steer_ref) | copy-start | bytes 12582916
  35.1 1.0 copy-start.6
  36.1 39.3 %copy-start.7 = (bf16[256,256]{1,0:T(8,128)(2,1)S(1)}, bf16[256,256]{1,0:T(8,128)(2,1)}, u32[]{:S(2)}) copy-start(bf16[256,256]{1,0:T(8,128)(2,1)} %constant.10.clone.sort_ref) | copy-start | bytes 393220
  73.0 30.0 %all-to-all-start.2 = ((bf16[32,24,256]{2,1,0:T(8,128)(2,1)}), bf16[32,24,256]{2,1,0:T(8,128)(2,1)S(1)}, u32[]{:S(2)}, u32[]{:S(2)}) async-start(bf16[32,24,256]{2,1,0:T(8,128)(2,1)} %get-tuple-element.17), calls=%async_computation.2 | async-start | bytes 786432 | tf_op jit(solution)/shard_map/all_to_all | solution.py:221
  75.5 2.2 %copy-start.2 = (bf16[2,1024,1024]{2,1,0:T(8,128)(2,1)S(1)}, bf16[2,1024,1024]{2,1,0:T(8,128)(2,1)}, u32[]{:S(2)}) copy-start(bf16[2,1024,1024]{2,1,0:T(8,128)(2,1)} %copy-done.1) | copy-start | bytes 12582916
  103.0 2.2 %copy-start.3 = (bf16[2,1024,1024]{2,1,0:T(8,128)(2,1)S(1)}, bf16[2,1024,1024]{2,1,0:T(8,128)(2,1)}, u32[]{:S(2)}) copy-start(bf16[2,1024,1024]{2,1,0:T(8,128)(2,1)} %copy-done.1) | copy-start | bytes 12582916

commit v2 on v1

v2 whole, which is shorter than its diff:
```python
import functools
import math

import jax
import jax.numpy as jnp
import numpy as np
from jax import lax
from jax.experimental import pallas as pl
from jax.experimental.pallas import tpu as pltpu
from jax.sharding import PartitionSpec as P

L = 1024
CH = 512
TAPS = 4
GRID = 512
SUB = 4
AXES = ("tm", "inp")
MIB = 2**20


def window_table():
    span = TAPS * L
    pos = np.arange(span, dtype=np.float64)
    window = np.sinc((pos - span / 2) / L) * (0.5 - 0.5 * np.cos(2.0 * np.pi * pos / span))
    return window.astype(np.float32).reshape(TAPS, L)


def dft_rows():
    step = np.arange(CH)[:, None] * np.arange(L)[None, :] % L
    radians = 2.0 * np.pi * step / L
    both = np.stack([np.cos(radians), -np.sin(radians)], 1) / math.sqrt(L)
    return both.reshape(2 * CH, L).astype(jnp.bfloat16)


def steer_grid(input_count):
    step = np.arange(GRID)[:, None] * np.arange(GRID)[None, :] % GRID
    radians = 2.0 * np.pi * step / GRID
    both = np.stack([np.cos(radians), np.sin(radians)], 0) / math.sqrt(input_count)
    return both.astype(jnp.bfloat16)


def filtered_frame(pieces, gain_ref, window_ref):
    total = None
    for tap, piece in enumerate(pieces):
        term = piece.astype(jnp.float32) * window_ref[tap : tap + 1, :]
        total = term if total is None else total + term
    rows = total.shape[0]
    gain = jnp.broadcast_to(gain_ref[...], (128, rows)).T[:, :1]
    return (total * gain).astype(jnp.bfloat16)


def put_spectra(filtered, table_ref, outs):
    spectra = lax.dot_general(
        table_ref[...], filtered, (((1,), (1,)), ((), ())), preferred_element_type=jnp.float32
    ).astype(jnp.bfloat16)
    dests = outs[0].shape[0]
    spectra = spectra.reshape(dests, spectra.shape[0] // dests, spectra.shape[1])
    row = 0
    for out in outs:
        rows = out.shape[-2]
        if len(out.shape) == 4:
            out[:, 0] = spectra[:, row : row + rows]
        else:
            out[...] = spectra[:, row : row + rows]
        row += rows


def frame_of(ref, frame):
    return ref[:, frame * L : (frame + 1) * L]


def heads_kernel(v_ref, *refs):
    head_refs, held, sems = refs[:-2], refs[-2], refs[-1]
    into, out, start = [], [], 0
    for at, head_ref in enumerate(head_refs):
        lanes = slice(start, start + head_ref.shape[1])
        into.append(pltpu.make_async_copy(v_ref.at[:, lanes], held.at[:, lanes], sems.at[0, at]))
        out.append(pltpu.make_async_copy(held.at[:, lanes], head_ref, sems.at[1, at]))
        into[-1].start()
        start = lanes.stop
    for first, second in zip(into, out):
        first.wait()
        second.start()
    for copy in out:
        copy.wait()


def heads_of(voltages, widths):
    rows, span = voltages.shape[0], sum(widths)
    far = pl.BlockSpec(memory_space=pltpu.HBM)
    return pl.pallas_call(
        heads_kernel,
        in_specs=[far],
        out_specs=[far] * len(widths),
        out_shape=[jax.ShapeDtypeStruct((rows, width), jnp.bfloat16) for width in widths],
        scratch_shapes=[
            pltpu.VMEM((rows, span), jnp.bfloat16),
            pltpu.SemaphoreType.DMA((2, len(widths))),
        ],
        compiler_params=pltpu.CompilerParams(vmem_limit_bytes=58 * MIB),
        cost_estimate=pl.CostEstimate(flops=0, bytes_accessed=4 * rows * span, transcendentals=0),
        name="heads",
    )(voltages)


def first_kernel(v_ref, gain_ref, window_ref, table_ref, out_ref, held, gain, window, table, sems):
    copies = [
        pltpu.make_async_copy(frame_of(v_ref.at, tap), frame_of(held.at, tap), sems.at[tap])
        for tap in range(TAPS)
    ]
    copies.append(pltpu.make_async_copy(window_ref, window, sems.at[TAPS]))
    copies.append(pltpu.make_async_copy(gain_ref, gain, sems.at[TAPS + 1]))
    for copy in copies:
        copy.start()
    table_copy = pltpu.make_async_copy(table_ref, table, sems.at[TAPS + 2])
    table_copy.start()
    for copy in copies:
        copy.wait()
    filtered = filtered_frame([frame_of(held, tap) for tap in range(TAPS)], gain, window)
    table_copy.wait()
    put_spectra(filtered, table, [out_ref])


def first_frame(dests, voltages, gain, window, table):
    rows = voltages.shape[0]
    far = pl.BlockSpec(memory_space=pltpu.HBM)
    return pl.pallas_call(
        first_kernel,
        in_specs=[far] * 4,
        out_shape=jax.ShapeDtypeStruct((dests, 2 * CH // dests, rows), jnp.bfloat16),
        scratch_shapes=[
            pltpu.VMEM((rows, TAPS * L), jnp.bfloat16),
            pltpu.VMEM(gain.shape, jnp.float32),
            pltpu.VMEM(window.shape, jnp.float32),
            pltpu.VMEM(table.shape, jnp.bfloat16),
            pltpu.SemaphoreType.DMA((TAPS + 3,)),
        ],
        compiler_params=pltpu.CompilerParams(vmem_limit_bytes=58 * MIB),
        cost_estimate=pl.CostEstimate(
            flops=2 * rows * L * 2 * CH, bytes_accessed=4 * voltages.size, transcendentals=0
        ),
        name="first_frame",
    )(voltages, gain, window, table)


def later_kernel(frame, n_later, n_out, v_ref, gain_ref, window_ref, table_ref, *refs):
    frame_count = v_ref.shape[1] // L
    later_refs, out_refs = refs[:n_later], refs[-n_out:]
    frames = [frame_of(v_ref, source) for source in range(frame_count)]
    for ref in later_refs:
        frames += [frame_of(ref, source) for source in range(ref.shape[1] // L)]
    pieces = frames[frame : frame + TAPS]
    put_spectra(filtered_frame(pieces, gain_ref, window_ref), table_ref, out_refs)


def later_frame(frame, dests, cuts, voltages, later, gain, window, table, so_far):
    rows = voltages.shape[0]
    frame_count = voltages.shape[1] // L
    needed = frame + TAPS - frame_count
    later = [block for at, block in enumerate(later) if sum(b.shape[1] for b in later[:at]) < needed * L]
    whole = pl.BlockSpec(memory_space=pltpu.VMEM)
    operands = [voltages, gain, window, table, *later]
    specs = [whole] * len(operands)
    aliases = {}
    for at, block in enumerate(so_far):
        aliases[len(operands)] = at
        operands.append(block)
        specs.append(pl.BlockSpec(memory_space=pl.ANY))
    return pl.pallas_call(
        functools.partial(later_kernel, frame, len(later), len(cuts)),
        grid=(1,),
        in_specs=specs,
        out_specs=[
            pl.BlockSpec((dests, 1, cut, rows), lambda g: (0, frame - 1, 0, 0)) for cut in cuts
        ],
        out_shape=[
            jax.ShapeDtypeStruct((dests, frame_count - 1, cut, rows), jnp.bfloat16) for cut in cuts
        ],
        input_output_aliases=aliases,
        compiler_params=pltpu.CompilerParams(vmem_limit_bytes=24 * MIB),
        cost_estimate=pl.CostEstimate(
            flops=2 * rows * L * 2 * CH, bytes_accessed=3 * voltages.size, transcendentals=0
        ),
        name="later_frame",
    )(*operands)


def steer_kernel(feed_ref, beam_ref, table_ref, out_ref):
    inputs = feed_ref.shape[0]
    chunks, width = out_ref.shape[0], out_ref.shape[2] // 2
    beams = chunks * width
    feed = lax.rem(feed_ref[...], GRID)
    beam = lax.rem(beam_ref[...], GRID)
    pick_feed = (lax.broadcasted_iota(jnp.int32, (inputs, GRID), 1) == feed)
    pick_feed = pick_feed.astype(jnp.float32).astype(jnp.bfloat16)
    pick_beam = (lax.broadcasted_iota(jnp.int32, (GRID, beams), 0) == beam)
    pick_beam = pick_beam.astype(jnp.float32).astype(jnp.bfloat16)
    for part in range(2):
        rows = jnp.dot(pick_feed, table_ref[part], preferred_element_type=jnp.float32)
        found = jnp.dot(rows.astype(jnp.bfloat16), pick_beam, preferred_element_type=jnp.float32)
        for c in range(chunks):
            out_ref[c, :, part * width : (part + 1) * width] = found[
                :, c * width : (c + 1) * width
            ].astype(jnp.bfloat16)


def steering(input_feed, beam_grid, table, chunks):
    inputs, beams = input_feed.shape[0], beam_grid.shape[0]
    cost = pl.CostEstimate(
        flops=4 * inputs * GRID * (GRID + beams), bytes_accessed=4 * inputs * beams, transcendentals=0
    )
    return pl.pallas_call(
        steer_kernel,
        out_shape=jax.ShapeDtypeStruct((chunks, inputs, 2 * beams // chunks), jnp.bfloat16),
        compiler_params=pltpu.CompilerParams(vmem_limit_bytes=32 * MIB),
        cost_estimate=cost,
        name="steering",
    )(input_feed.reshape(inputs, 1), beam_grid.reshape(1, beams), table)


def products_kernel(
    n_time, n_input, frame_count, first, count, x0_ref, xl_ref, steer_ref, *rest
):
    vis_ref, power_ref, arrived, ordered, held, ring, sems, ring_sems = rest[-8:]
    step, steps = pl.program_id(0), pl.num_programs(0)
    chunk = step % SUB
    slots = ring.shape[0]

    def vis_copy(at, part):
        slot = at % slots
        return pltpu.make_async_copy(
            ring.at[slot, part], vis_ref.at[first + at, part], ring_sems.at[slot, part]
        )

    def steer_copy(c):
        return pltpu.make_async_copy(steer_ref.at[c], held.at[c], sems.at[c])

    @pl.when(step == 0)
    def _():
        steer_copy(0).start()

    half = n_time * frame_count
    rows_per = 2 * half
    width = x0_ref.shape[2]
    inputs = n_input * width
    tile = 2 * SUB

    @pl.when(step % SUB == 0)
    def _():
        sub = step // SUB
        at = pl.multiple_of((first // SUB + sub) * tile, tile)
        at_later = pl.multiple_of(sub * tile, tile)
        for t in range(n_time):
            for i in range(n_input):
                source = t * n_input + i
                lanes = slice(i * width, (i + 1) * width)
                for f in range(frame_count):
                    slot = (t * frame_count + f) * tile
                    if f == 0:
                        piece = x0_ref[source, pl.ds(at, tile), :]
                    else:
                        piece = xl_ref[source, f - 1, pl.ds(at_later, tile), :]
                    arrived[slot : slot + tile, lanes] = piece
        total = SUB * rows_per
        row = lax.broadcasted_iota(jnp.int32, (total, total), 0)
        column = lax.broadcasted_iota(jnp.int32, (total, total), 1)
        source = (row % half) * tile + (row // rows_per) * 2 + (row // half) % 2
        pick = jnp.where(column == source, 1.0, 0.0).astype(jnp.bfloat16)
        sorted_rows = jnp.dot(pick, arrived[...], preferred_element_type=jnp.float32)
        ordered[...] = sorted_rows.astype(jnp.bfloat16)

    @pl.when(step < SUB)
    def _():
        steer_copy(chunk).wait()

    @pl.when(step == 0)
    def _():
        for c in range(1, SUB):
            steer_copy(c).start()

    @pl.when(step >= slots)
    def _():
        for part in range(2):
            vis_copy(step - slots, part).wait()

    at = pl.multiple_of((step % SUB) * rows_per, rows_per)
    both = ordered[pl.ds(at, rows_per), :]
    re, im = both[:half], both[half:]
    right = both * jnp.asarray(1.0 / half, jnp.bfloat16)
    wide = steer_ref.shape[2] // 2
    turned = jnp.dot(ordered[...], held[chunk], preferred_element_type=jnp.float32)
    cos_part, sin_part = turned[:, :wide], turned[:, wide:]
    lanes = pl.ds(pl.multiple_of(chunk * wide, wide), wide)
    for c in range(SUB):
        rows_re = slice(c * rows_per, c * rows_per + half)
        rows_im = slice(c * rows_per + half, (c + 1) * rows_per)
        beam_re = cos_part[rows_re] - sin_part[rows_im]
        beam_im = sin_part[rows_re] + cos_part[rows_im]
        power = jnp.sum(beam_re * beam_re + beam_im * beam_im, axis=0, keepdims=True)
        row = (step // SUB) % 2 * SUB + c
        power_ref[pl.ds(row, 1), lanes] = power * (1.0 / half)

    block = min(inputs, 256)
    slot = step % slots
    for part in range(2):
        left = (both if part == 0 else jnp.concatenate([im, -re], 0)).T
        for j in range(0, inputs, block):
            lanes = slice(j, j + block)
            upper = jnp.dot(
                left[: j + block], right[:, lanes], preferred_element_type=jnp.float32
            ).astype(jnp.bfloat16)
            ring[slot, part, : j + block, lanes] = upper
            for i in range(0, j, block):
                mirror = upper[i : i + block].T
                ring[slot, part, lanes, i : i + block] = mirror if part == 0 else -mirror
        vis_copy(step, part).start()

    @pl.when(step == steps - 1)
    def _():
        for at in range(count - min(slots, count), count):
            for part in range(2):
                vis_copy(at, part).wait()


def products(sizes, first, count, x0, xl, steer, so_far):
    n_time, n_input, frame_count, per_dev = sizes
    inputs = n_input * x0.shape[2]
    beams = steer.shape[0] * steer.shape[2] // 2
    whole = pl.BlockSpec(memory_space=pltpu.VMEM)
    rows = 2 * n_time * frame_count * SUB
    slots = min(3, count)
    cost = pl.CostEstimate(
        flops=count * 2 * rows // SUB * inputs * (2 * inputs + 2 * beams),
        bytes_accessed=count * 4 * inputs * inputs + 4 * inputs * beams,
        transcendentals=0,
    )
    operands = [x0, xl, steer]
    specs = [whole] * 2 + [pl.BlockSpec(memory_space=pltpu.HBM)]
    aliases = {}
    for at, block in enumerate(so_far):
        aliases[len(operands)] = at
        operands.append(block)
        specs.append(pl.BlockSpec(memory_space=pl.ANY))
    return pl.pallas_call(
        functools.partial(products_kernel, n_time, n_input, frame_count, first, count),
        grid=(count,),
        in_specs=specs,
        out_specs=[
            pl.BlockSpec(memory_space=pltpu.HBM),
            pl.BlockSpec((2 * SUB, beams), lambda c: ((first + c) // (2 * SUB), 0)),
        ],
        out_shape=[
            jax.ShapeDtypeStruct((per_dev, 2, inputs, inputs), jnp.bfloat16),
            jax.ShapeDtypeStruct((per_dev, beams), jnp.float32),
        ],
        scratch_shapes=[
            pltpu.VMEM((rows, inputs), jnp.bfloat16),
            pltpu.VMEM((rows, inputs), jnp.bfloat16),
            pltpu.VMEM(steer.shape, jnp.bfloat16),
            pltpu.VMEM((slots, 2, inputs, inputs), jnp.bfloat16),
            pltpu.SemaphoreType.DMA((SUB,)),
            pltpu.SemaphoreType.DMA((slots, 2)),
        ],
        input_output_aliases=aliases,
        compiler_params=pltpu.CompilerParams(vmem_limit_bytes=58 * MIB),
        cost_estimate=cost,
        name="products",
    )(*operands)


def exchanged(block):
    return lax.all_to_all(block, AXES, 0, 0, tiled=True)


def in_pieces(voltages, input_gain, input_feed, beam_grid):
    frame_count = voltages.shape[1] // L
    n_time = lax.axis_size("tm")
    n_input = lax.axis_size("inp")
    dests = n_time * n_input
    per_dev = CH // dests
    last = per_dev // 2 // (2 * SUB) * (2 * SUB)
    counts = (per_dev - last, last)
    back = [(i + 1, i) for i in range(n_time - 1)]

    window = jnp.asarray(window_table())
    table = jnp.asarray(dft_rows())
    gain = input_gain.reshape(1, -1)

    widths = ((TAPS - 2) * L, L)
    later = [lax.ppermute(head, "tm", back) for head in heads_of(voltages, widths)]
    first = first_frame(dests, voltages, gain, window, table)
    x0 = exchanged(first)
    parts = ()
    for frame in range(1, frame_count):
        cuts = [2 * count for count in counts]
        parts = later_frame(frame, dests, cuts, voltages, later, gain, window, table, parts)
    steer = steering(input_feed, beam_grid, jnp.asarray(steer_grid(input_feed.shape[0])), SUB)
    send_a, x0, steer = lax.optimization_barrier((parts[0], x0, steer))
    xa = exchanged(send_a)
    send_b, xa = lax.optimization_barrier((parts[1], xa))
    xb = exchanged(send_b)
    sizes = (n_time, n_input, frame_count, per_dev)
    found = products(sizes, 0, counts[0], x0, xa, steer, ())
    return products(sizes, counts[0], counts[1], x0, xb, steer, found)


def whole_channel(spectrum, steer):
    real_part, imag_part = spectrum[0], spectrum[1]
    input_count, frame_total = real_part.shape
    stacked = jnp.concatenate([real_part, imag_part], 1)
    rotated = jnp.concatenate([imag_part, -real_part], 1)
    both = jnp.concatenate([stacked, rotated], 0)
    found = lax.dot_general(
        both, stacked, (((1,), (1,)), ((), ())), preferred_element_type=jnp.float32
    )
    visible = (found / frame_total).reshape(2, input_count, input_count).astype(jnp.bfloat16)
    cos_part, sin_part = [
        lax.dot_general(
            spectrum, part, (((1,), (0,)), ((), ())), preferred_element_type=jnp.float32
        )
        for part in steer
    ]
    beam_re = cos_part[0] - sin_part[1]
    beam_im = sin_part[0] + cos_part[1]
    return visible, jnp.mean(beam_re**2 + beam_im**2, axis=0)


def at_once(voltages, input_gain, input_feed, beam_grid):
    rows = voltages.shape[0]
    frame_count = voltages.shape[1] // L
    n_time = lax.axis_size("tm")
    n_input = lax.axis_size("inp")
    dests = n_time * n_input
    per_dev = CH // dests
    later = lax.ppermute(
        voltages[:, : (TAPS - 1) * L], "tm", [(i + 1, i) for i in range(n_time - 1)]
    )
    joined = jnp.concatenate([voltages, later], 1)
    window = jnp.asarray(window_table())
    summed = jnp.zeros((rows, frame_count, L), jnp.float32)
    for tap in range(TAPS):
        piece = joined[:, tap * L : (tap + frame_count) * L].reshape(rows, frame_count, L)
        summed = summed + piece.astype(jnp.float32) * window[tap]
    filtered = (summed * input_gain[:, None, None]).astype(jnp.bfloat16)
    spectra = lax.dot_general(
        jnp.asarray(dft_rows()),
        filtered,
        (((1,), (2,)), ((), ())),
        preferred_element_type=jnp.float32,
    ).astype(jnp.bfloat16)
    blocks = exchanged(spectra.reshape(dests, per_dev * 2, rows, frame_count))
    blocks = blocks.reshape(n_time, n_input, per_dev, 2, rows, frame_count)
    owned = blocks.transpose(2, 3, 1, 4, 0, 5)
    owned = owned.reshape(per_dev, 2, n_input * rows, n_time * frame_count)
    steer = steering(input_feed, beam_grid, jnp.asarray(steer_grid(input_feed.shape[0])), 1)[0]
    steer = jnp.split(steer, 2, axis=1)
    return lax.map(lambda spectrum: whole_channel(spectrum, steer), owned)


def on_device(voltages, input_gain, input_feed, beam_grid):
    per_dev = CH // (lax.axis_size("tm") * lax.axis_size("inp"))
    slots = lax.axis_size("tm") * (voltages.shape[1] // L)
    whole_tiles = per_dev % (4 * SUB) == 0 and slots % 16 == 0 and beam_grid.shape[0] % (SUB * 128) == 0
    if whole_tiles and slots & (slots - 1) == 0:
        return in_pieces(voltages, input_gain, input_feed, beam_grid)
    return at_once(voltages, input_gain, input_feed, beam_grid)


def solution(mesh):
    return jax.shard_map(
        on_device,
        mesh=mesh,
        in_specs=(P("inp", "tm"), P("inp"), P(), P()),
        out_specs=(P(("tm", "inp"), None, None, None), P(("tm", "inp"), None)),
        check_vma=False,
    )
```

time: 116 us -> 101 us (0.87)
  local copies, waits for them, and re-layouts: 13.3 us -> 1.17 us
  blocking collectives: 36.9 us -> 26.8 us
  waiting for transfers between devices: 6.43 us -> 10.6 us
  Pallas kernels: 44.4 us -> 46.4 us
  starting transfers between devices: 12.7 us -> 14.6 us
    all_to_all x1, blocking collectives: 36.9 us -> 26.8 us  [exchanged(): return lax.all_to_all(block, AXES, 0, 0, tiled=True)]
    unnamed x26 -> x18, local copies, waits for them, and re-layouts: 10.2 us -> 0.95 us
    pallas_call x3 -> x6, Pallas kernels: 9.7 us -> 15.5 us  [the longest x3 5.59 us: later_frame(): pl.pallas_call(functools.partial(later_kernel, frame, len(later), len(cut...]
    all_to_all x2, waiting for transfers between devices: 0.01 us -> 5.34 us  [exchanged(): return lax.all_to_all(block, AXES, 0, 0, tiled=True)]
    pallas_call x2, Pallas kernels: 34.7 us -> 30.9 us  [products(): pl.pallas_call(functools.partial(products_kernel, n_time, n_input, frame_...]
    slice x2 -> x0, local copies, waits for them, and re-layouts: 2.8 us -> none  [the longest x1 2.8 us: in_pieces(): voltages[:, :(TAPS - 1) * L]]
    ppermute x1 -> x2, starting transfers between devices: 1.96 us -> 4.21 us  [in_pieces(): lax.ppermute(head, 'tm', back)]
    ppermute x1 -> x2, waiting for transfers between devices: 6.42 us -> 5.25 us  [in_pieces(): lax.ppermute(head, 'tm', back)]
  transfers between devices with their start and end apart: 3 -> 4, of which waited for: 1 -> 3; matrix products, arithmetic and copies ran while one was open for 0% -> 0% of each run, Pallas kernels for 30% -> 28%
where the time goes in v2:
time: 101 us; the launch traced here: 100 us
  Pallas kernels  46.4 us (46%)
  blocking collectives  26.8 us (27%)
  starting transfers between devices  14.6 us (14%)
  waiting for transfers between devices  10.6 us (10%)
  local copies, waits for them, and re-layouts  1.17 us (1%)
    pallas_call x2, Pallas kernels, products(): pl.pallas_call(functools.partial(products_kernel, n_time, n_input, frame_...  30.9 us
    all_to_all x1, blocking collectives, exchanged(): return lax.all_to_all(block, AXES, 0, 0, tiled=True)  26.8 us
    all_to_all x2, starting transfers between devices, exchanged(): return lax.all_to_all(block, AXES, 0, 0, tiled=True)  10.4 us
    pallas_call x3, Pallas kernels, later_frame(): pl.pallas_call(functools.partial(later_kernel, frame, len(later), len(cut...  5.59 us
    all_to_all x2, waiting for transfers between devices, exchanged(): return lax.all_to_all(block, AXES, 0, 0, tiled=True)  5.34 us
    ppermute x2, waiting for transfers between devices, in_pieces(): lax.ppermute(head, 'tm', back)  5.25 us
    ppermute x2, starting transfers between devices, in_pieces(): lax.ppermute(head, 'tm', back)  4.21 us
    pallas_call x1, Pallas kernels, first_frame(): pl.pallas_call(first_kernel, in_specs=[far] * 4, out_shape=jax.ShapeDtype...  3.88 us
  transfers between devices with their start and end apart: 4, of which 3 were waited for; matrix products, arithmetic and copies ran while one was open for 0% of the time, Pallas kernels for 28%

profile of v2, /device:TPU:1, one launch (start us, length us, event | category | flops | bytes accessed | tf_op | source)
XLA Modules:
  0.0 100.4 jit_solution(11143781823572608788)
XLA Ops:
  0.6 0.0 copy-start.6
  0.6 0.0 copy-start.8
  0.7 0.0 copy-start.5
  0.7 2.5 %heads.1 = (bf16[256,2048]{1,0:T(8,128)(2,1)}, bf16[256,1024]{1,0:T(8,128)(2,1)}) custom-call(bf16[256,4096]{1,0:T(8,128)(2,1)} %v_ref.9), custom_call_target="tpu_custom_call" | custom-call | bytes 3145728 | tf_op jit(solution)/shard_map/heads/pallas_call | solution.py:91
  3.2 2.0 %collective-permute-start = (bf16[256,2048]{1,0:T(8,128)(2,1)}, bf16[256,2048]{1,0:T(8,128)(2,1)S(1)}, u32[]{:S(2)}, u32[]{:S(2)}) collective-permute-start(bf16[256,2048]{1,0:T(8,128)(2,1)} %get-tuple-element.17), channel_id=1, source_target_pairs={{4,0},{8,4},{12,8},{16,12},{20,16},{24,20},{28,24},{5,1},{9,5},{13... | collective-permute-start | bytes 3145736 | tf_op jit(solution)/shard_map/ppermute | solution.py:390
  5.1 3.9 %first_frame.1 = bf16[32,32,256]{2,1,0:T(8,128)(2,1)} custom-call(bf16[256,4096]{1,0:T(8,128)(2,1)} %v_ref.9, f32[1,256]{1,0:T(1,128)} %bitcast.3, f32[4,1024]{1,0:T(4,128)} %constant.6.clone.window_ref, bf16[1024,1024]{1,0:T(8,128)(2,1)} %constant.7.clone.table_ref), custom_call_target="tpu_custom_call" | custom-call | flops 536870912 | bytes 4194304 | tf_op jit(solution)/shard_map/first_frame/pallas_call | solution.py:127
  9.0 7.3 %all-to-all-start = ((bf16[32,32,256]{2,1,0:T(8,128)(2,1)}), bf16[32,32,256]{2,1,0:T(8,128)(2,1)}, u32[]{:S(2)}, u32[]{:S(2)}) async-start(bf16[32,32,256]{2,1,0:T(8,128)(2,1)} %first_frame.1), calls=%async_computation | async-start | bytes 1048576 | tf_op jit(solution)/shard_map/all_to_all | solution.py:372
  16.3 2.2 %collective-permute-start.1 = (bf16[256,1024]{1,0:T(8,128)(2,1)}, bf16[256,1024]{1,0:T(8,128)(2,1)S(1)}, u32[]{:S(2)}, u32[]{:S(2)}) collective-permute-start(bf16[256,1024]{1,0:T(8,128)(2,1)} %get-tuple-element.18), channel_id=1, source_target_pairs={{4,0},{8,4},{12,8},{16,12},{20,16},{24,20},{28,24},{5,1},{9,5},{13... | collective-permute-start | bytes 1572872 | tf_op jit(solution)/shard_map/ppermute | solution.py:390
  18.6 0.0 copy-done.8
  18.6 0.2 copy.15.feed_ref
  18.8 0.0 copy-done.6
  18.8 0.0 copy-done.5
  18.8 0.0 copy-start
  18.8 0.0 copy-start.1
  18.8 0.0 copy-start.3
  18.8 0.0 copy-start.4
  18.9 3.6 %steering.1.steer_ref = bf16[4,1024,512]{2,1,0:T(8,128)(2,1)S(1)} custom-call(s32[1024,1]{1,0:T(8,128)S(1)} %copy.15.feed_ref, s32[1,1024]{1,0:T(1,128)S(1)} %bitcast.7, bf16[2,512,512]{2,1,0:T(8,128)(2,1)S(1)} %copy-done.6), custom_call_target="tpu_custom_call" | custom-call | flops 3221225472 | bytes 4194304 | tf_op jit(solution)/shard_map/steering/pallas_call | solution.py:212
  22.4 0.0 copy-start.2
  22.4 0.7 collective-permute-done.refs_0_
  23.1 0.0 copy-done
  23.2 0.0 copy-done.1
  23.2 0.0 copy-done.3
  23.2 0.0 copy-done.4
  23.2 1.8 %later_frame.3 = (bf16[32,3,16,256]{3,2,1,0:T(8,128)(2,1)S(1)}, bf16[32,3,16,256]{3,2,1,0:T(8,128)(2,1)}) custom-call(bf16[256,4096]{1,0:T(8,128)(2,1)S(1)} %copy-done, f32[1,256]{1,0:T(1,128)S(1)} %bitcast.4, f32[4,1024]{1,0:T(4,128)S(1)} %copy-done.3, bf16[1024,1024]{1,0:T(8,128)(2,1)S(1)} %copy-done.1, bf16[256,2048]{1,0:T(8,128)(2,1)S(1)} %collective-permute-done.refs_0_), custom_call_target="tpu_custom_call" | custom-call | flops 536870912 | bytes 3145728 | tf_op jit(solution)/shard_map/later_frame/pallas_call | solution.py:169
  25.0 1.9 %later_frame.4 = (bf16[32,3,16,256]{3,2,1,0:T(8,128)(2,1)S(1)}, bf16[32,3,16,256]{3,2,1,0:T(8,128)(2,1)}) custom-call(bf16[256,4096]{1,0:T(8,128)(2,1)S(1)} %copy-done, f32[1,256]{1,0:T(1,128)S(1)} %bitcast.5, f32[4,1024]{1,0:T(4,128)S(1)} %copy-done.3, bf16[1024,1024]{1,0:T(8,128)(2,1)S(1)} %copy-done.1, ...), custom_call_target="tpu_custom_call", output_to_operand_aliasing={{0}: (5, {}), {1}: (6, {})} | custom-call | flops 536870912 | bytes 3145728 | tf_op jit(solution)/shard_map/later_frame/pallas_call | solution.py:169
  26.9 0.0 copy-done.2
  26.9 4.5 %collective-permute-done.1.refs_1_ = bf16[256,1024]{1,0:T(8,128)(2,1)S(1)} collective-permute-done((bf16[256,1024]{1,0:T(8,128)(2,1)}, bf16[256,1024]{1,0:T(8,128)(2,1)S(1)}, u32[]{:S(2)}, u32[]{:S(2)}) %collective-permute-start.1) | collective-permute-done | bytes 524320 | tf_op jit(solution)/shard_map/ppermute | solution.py:390
  31.4 1.9 %later_frame.5 = (bf16[32,3,16,256]{3,2,1,0:T(8,128)(2,1)S(1)}, bf16[32,3,16,256]{3,2,1,0:T(8,128)(2,1)}) custom-call(bf16[256,4096]{1,0:T(8,128)(2,1)S(1)} %copy-done, f32[1,256]{1,0:T(1,128)S(1)} %bitcast.6, f32[4,1024]{1,0:T(4,128)S(1)} %copy-done.3, bf16[1024,1024]{1,0:T(8,128)(2,1)S(1)} %copy-done.1, ...), custom_call_target="tpu_custom_call", output_to_operand_aliasing={{0}: (6, {}), {1}: (7, {})} | custom-call | flops 536870912 | bytes 3145728 | tf_op jit(solution)/shard_map/later_frame/pallas_call | solution.py:169
  33.3 0.0 all-to-all-done.x0_ref
  33.3 26.8 %all_to_all.15.xl_ref = bf16[32,3,16,256]{3,2,1,0:T(8,128)(2,1)} all-to-all(bf16[32,3,16,256]{3,2,1,0:T(8,128)(2,1)S(1)} %get-tuple-element.26), channel_id=1, replica_groups=mesh['tm'=8,'inp'=4] {'tm','inp'}, dimensions={0} | all-to-all | bytes 1572864 | tf_op jit(solution)/shard_map/all_to_all | solution.py:372
  60.1 3.2 %all-to-all-start.2 = ((bf16[32,3,16,256]{3,2,1,0:T(8,128)(2,1)}), bf16[32,3,16,256]{3,2,1,0:T(8,128)(2,1)S(1)}, u32[]{:S(2)}, u32[]{:S(2)}) async-start(bf16[32,3,16,256]{3,2,1,0:T(8,128)(2,1)} %get-tuple-element.27), calls=%async_computation.2 | async-start | bytes 1572864 | tf_op jit(solution)/shard_map/all_to_all | solution.py:372
  63.2 15.5 %products.2 = (bf16[16,2,1024,1024]{3,2,1,0:T(8,128)(2,1)}, f32[16,1024]{1,0:T(8,128)}) custom-call(bf16[32,32,256]{2,1,0:T(8,128)(2,1)} %all-to-all-done.x0_ref, bf16[32,3,16,256]{3,2,1,0:T(8,128)(2,1)} %all_to_all.15.xl_ref, bf16[4,1024,512]{2,1,0:T(8,128)(2,1)} %copy-done.2), custom_call_target="tpu_custom_call" | custom-call | flops 4294967296 | bytes 37748736 | tf_op jit(solution)/shard_map/products/pallas_call | solution.py:344
  78.7 5.3 %all-to-all-done.2.xl_ref = bf16[32,3,16,256]{3,2,1,0:T(8,128)(2,1)S(1)} async-done(((bf16[32,3,16,256]{3,2,1,0:T(8,128)(2,1)}), bf16[32,3,16,256]{3,2,1,0:T(8,128)(2,1)S(1)}, u32[]{:S(2)}, u32[]{:S(2)}) %all-to-all-start.2) | async-done | bytes 786464 | tf_op jit(solution)/shard_map/all_to_all | solution.py:372
  84.0 0.0 copy-start.7
  84.0 0.9 copy-done.7
  84.9 15.4 %products.3 = (bf16[16,2,1024,1024]{3,2,1,0:T(8,128)(2,1)}, f32[16,1024]{1,0:T(8,128)}) custom-call(bf16[32,32,256]{2,1,0:T(8,128)(2,1)} %all-to-all-done.x0_ref, bf16[32,3,16,256]{3,2,1,0:T(8,128)(2,1)} %copy-done.7, bf16[4,1024,512]{2,1,0:T(8,128)(2,1)} %copy-done.2, ...), custom_call_target="tpu_custom_call", output_to_operand_aliasing={{0}: (3, {}), {1}: (4, {})} | custom-call | flops 4294967296 | bytes 37748736 | tf_op jit(solution)/shard_map/products/pallas_call | solution.py:344
Async XLA Ops:
  0.6 18.2 %copy-start.6 = (bf16[2,512,512]{2,1,0:T(8,128)(2,1)S(1)}, bf16[2,512,512]{2,1,0:T(8,128)(2,1)}, u32[]{:S(2)}) copy-start(bf16[2,512,512]{2,1,0:T(8,128)(2,1)} %constant.8.clone.table_ref) | copy-start | bytes 3145732
  0.6 17.9 %copy-start.8 = (s32[1024]{0:T(1024)S(1)}, s32[1024]{0:T(1024)}, u32[]{:S(2)}) copy-start(s32[1024]{0:T(1024)} %param.9) | copy-start | bytes 12292
  0.7 18.1 %copy-start.5 = (s32[1024]{0:T(1024)S(1)}, s32[1024]{0:T(1024)}, u32[]{:S(2)}) copy-start(s32[1024]{0:T(1024)} %param.10) | copy-start | bytes 12292
  3.2 20.0 %collective-permute-start = (bf16[256,2048]{1,0:T(8,128)(2,1)}, bf16[256,2048]{1,0:T(8,128)(2,1)S(1)}, u32[]{:S(2)}, u32[]{:S(2)}) collective-permute-start(bf16[256,2048]{1,0:T(8,128)(2,1)} %get-tuple-element.17), channel_id=1, source_target_pairs={{4,0},{8,4},{12,8},{16,12},{20,16},{24,20},{28,24},{5,1},{9,5},{13... | collective-permute-start | bytes 3145736 | tf_op jit(solution)/shard_map/ppermute | solution.py:390
  9.0 24.3 %all-to-all-start = ((bf16[32,32,256]{2,1,0:T(8,128)(2,1)}), bf16[32,32,256]{2,1,0:T(8,128)(2,1)}, u32[]{:S(2)}, u32[]{:S(2)}) async-start(bf16[32,32,256]{2,1,0:T(8,128)(2,1)} %first_frame.1), calls=%async_computation | async-start | bytes 1048576 | tf_op jit(solution)/shard_map/all_to_all | solution.py:372
  16.3 15.1 %collective-permute-start.1 = (bf16[256,1024]{1,0:T(8,128)(2,1)}, bf16[256,1024]{1,0:T(8,128)(2,1)S(1)}, u32[]{:S(2)}, u32[]{:S(2)}) collective-permute-start(bf16[256,1024]{1,0:T(8,128)(2,1)} %get-tuple-element.18), channel_id=1, source_target_pairs={{4,0},{8,4},{12,8},{16,12},{20,16},{24,20},{28,24},{5,1},{9,5},{13... | collective-permute-start | bytes 1572872 | tf_op jit(solution)/shard_map/ppermute | solution.py:390
  18.8 4.3 %copy-start = (bf16[256,4096]{1,0:T(8,128)(2,1)S(1)}, bf16[256,4096]{1,0:T(8,128)(2,1)}, u32[]{:S(2)}) copy-start(bf16[256,4096]{1,0:T(8,128)(2,1)} %v_ref.9) | copy-start | bytes 6291460
  18.8 4.3 %copy-start.1 = (bf16[1024,1024]{1,0:T(8,128)(2,1)S(1)}, bf16[1024,1024]{1,0:T(8,128)(2,1)}, u32[]{:S(2)}) copy-start(bf16[1024,1024]{1,0:T(8,128)(2,1)} %constant.7.clone.table_ref) | copy-start | bytes 6291460
  18.8 4.3 %copy-start.3 = (f32[4,1024]{1,0:T(4,128)S(1)}, f32[4,1024]{1,0:T(4,128)}, u32[]{:S(2)}) copy-start(f32[4,1024]{1,0:T(4,128)} %constant.6.clone.window_ref) | copy-start | bytes 49156
  18.8 4.3 %copy-start.4 = (f32[256]{0:T(256)S(1)}, f32[256]{0:T(256)}, u32[]{:S(2)}) copy-start(f32[256]{0:T(256)} %param.8) | copy-start | bytes 3076
  22.4 4.5 %copy-start.2 = (bf16[4,1024,512]{2,1,0:T(8,128)(2,1)}, bf16[4,1024,512]{2,1,0:T(8,128)(2,1)S(1)}, u32[]{:S(2)}) copy-start(bf16[4,1024,512]{2,1,0:T(8,128)(2,1)S(1)} %steering.1.steer_ref) | copy-start | bytes 12582916
  60.1 24.0 %all-to-all-start.2 = ((bf16[32,3,16,256]{3,2,1,0:T(8,128)(2,1)}), bf16[32,3,16,256]{3,2,1,0:T(8,128)(2,1)S(1)}, u32[]{:S(2)}, u32[]{:S(2)}) async-start(bf16[32,3,16,256]{3,2,1,0:T(8,128)(2,1)} %get-tuple-element.27), calls=%async_computation.2 | async-start | bytes 1572864 | tf_op jit(solution)/shard_map/all_to_all | solution.py:372
  84.0 0.9 copy-start.7

commit v3 on v2

--- a/solution.py
+++ b/solution.py
@@ -14,6 +14,7 @@
 TAPS = 4
 GRID = 512
 SUB = 4
+LAST_GROUP = 2 * SUB
 AXES = ("tm", "inp")
 MIB = 2**20
 
@@ -143,21 +144,71 @@
     )(voltages, gain, window, table)
 
 
-def later_kernel(frame, n_later, n_out, v_ref, gain_ref, window_ref, table_ref, *refs):
-    frame_count = v_ref.shape[1] // L
-    later_refs, out_refs = refs[:n_later], refs[-n_out:]
-    frames = [frame_of(v_ref, source) for source in range(frame_count)]
+def frames_with(v_ref, later_refs):
+    frames = [frame_of(v_ref, source) for source in range(v_ref.shape[1] // L)]
     for ref in later_refs:
         frames += [frame_of(ref, source) for source in range(ref.shape[1] // L)]
-    pieces = frames[frame : frame + TAPS]
+    return frames
+
+
+def needed_of(frame, frame_count, later):
+    needed = frame + TAPS - frame_count
+    return [block for at, block in enumerate(later) if sum(b.shape[1] for b in later[:at]) < needed * L]
+
+
+def to_tm_kernel(n_input, spectra_ref, *outs):
+    n_time = len(outs)
+    frames, rows = spectra_ref.shape[1], spectra_ref.shape[2]
+    for t, out in enumerate(outs):
+        row = lax.rem(lax.axis_index("tm") + t, n_time) * n_input
+        for z in range(n_input):
+            dest = row + lax.rem(lax.axis_index("inp") + z, n_input)
+            for f in range(frames):
+                out[z, f * rows : (f + 1) * rows] = spectra_ref[dest, f]
+
+
+def to_tm(n_time, n_input, spectra):
+    _, frames, cut, rows = spectra.shape
+    return pl.pallas_call(
+        functools.partial(to_tm_kernel, n_input),
+        out_shape=[jax.ShapeDtypeStruct((n_input, frames * cut, rows), jnp.bfloat16)] * n_time,
+        compiler_params=pltpu.CompilerParams(vmem_limit_bytes=24 * MIB),
+        cost_estimate=pl.CostEstimate(flops=0, bytes_accessed=4 * spectra.size, transcendentals=0),
+        name="to_tm",
+    )(spectra)
+
+
+def to_inp_kernel(n_time, *refs):
+    blocks, outs = refs[:n_time], refs[n_time:]
+    for z, out in enumerate(outs):
+        for t in range(n_time):
+            out[t] = blocks[t][z]
+
+
+def to_inp(blocks):
+    n_time = len(blocks)
+    n_input, cut, rows = blocks[0].shape
+    return pl.pallas_call(
+        functools.partial(to_inp_kernel, n_time),
+        out_shape=[jax.ShapeDtypeStruct((n_time, cut, rows), jnp.bfloat16)] * n_input,
+        compiler_params=pltpu.CompilerParams(vmem_limit_bytes=24 * MIB),
+        cost_estimate=pl.CostEstimate(
+            flops=0, bytes_accessed=4 * n_time * blocks[0].size, transcendentals=0
+        ),
+        name="to_inp",
+    )(*blocks)
+
+
+def later_kernel(frame, n_later, n_out, v_ref, gain_ref, window_ref, table_ref, *refs):
+    later_refs, out_refs = refs[:n_later], refs[-n_out:]
+    pieces = frames_with(v_ref, later_refs)[frame : frame + TAPS]
     put_spectra(filtered_frame(pieces, gain_ref, window_ref), table_ref, out_refs)
 
 
-def later_frame(frame, dests, cuts, voltages, later, gain, window, table, so_far):
+def later_frame(frame, n_early, dests, cuts, voltages, later, gain, window, table, so_far):
     rows = voltages.shape[0]
     frame_count = voltages.shape[1] // L
-    needed = frame + TAPS - frame_count
-    later = [block for at, block in enumerate(later) if sum(b.shape[1] for b in later[:at]) < needed * L]
+    later = needed_of(frame, frame_count, later)
     whole = pl.BlockSpec(memory_space=pltpu.VMEM)
     operands = [voltages, gain, window, table, *later]
     specs = [whole] * len(operands)
@@ -171,10 +222,12 @@
         grid=(1,),
         in_specs=specs,
         out_specs=[
-            pl.BlockSpec((dests, 1, cut, rows), lambda g: (0, frame - 1, 0, 0)) for cut in cuts
+            pl.BlockSpec((dests, 1, cut, rows), lambda g: (0, frame - n_early, 0, 0))
+            for cut in cuts
         ],
         out_shape=[
-            jax.ShapeDtypeStruct((dests, frame_count - 1, cut, rows), jnp.bfloat16) for cut in cuts
+            jax.ShapeDtypeStruct((dests, frame_count - n_early, cut, rows), jnp.bfloat16)
+            for cut in cuts
         ],
         input_output_aliases=aliases,
         compiler_params=pltpu.CompilerParams(vmem_limit_bytes=24 * MIB),
@@ -186,22 +239,21 @@
 
 
 def steer_kernel(feed_ref, beam_ref, table_ref, out_ref):
-    inputs = feed_ref.shape[0]
-    chunks, width = out_ref.shape[0], out_ref.shape[2] // 2
-    beams = chunks * width
-    feed = lax.rem(feed_ref[...], GRID)
+    inputs = feed_ref.shape[1]
+    chunks, wide = out_ref.shape[0], out_ref.shape[2] // 2
+    feed = lax.rem(feed_ref[...], GRID).astype(jnp.float32)
+    feed = jnp.broadcast_to(feed, (128, inputs)).T[:, :1].astype(jnp.int32)
     beam = lax.rem(beam_ref[...], GRID)
-    pick_feed = (lax.broadcasted_iota(jnp.int32, (inputs, GRID), 1) == feed)
-    pick_feed = pick_feed.astype(jnp.float32).astype(jnp.bfloat16)
-    pick_beam = (lax.broadcasted_iota(jnp.int32, (GRID, beams), 0) == beam)
-    pick_beam = pick_beam.astype(jnp.float32).astype(jnp.bfloat16)
+    pick_feed = lax.broadcasted_iota(jnp.int32, (inputs, GRID), 1) == feed
+    pick_feed = jnp.where(pick_feed, 1.0, 0.0).astype(jnp.bfloat16)
+    pick_beam = lax.broadcasted_iota(jnp.int32, (GRID, chunks * wide), 0) == beam
+    pick_beam = jnp.where(pick_beam, 1.0, 0.0).astype(jnp.bfloat16)
     for part in range(2):
         rows = jnp.dot(pick_feed, table_ref[part], preferred_element_type=jnp.float32)
         found = jnp.dot(rows.astype(jnp.bfloat16), pick_beam, preferred_element_type=jnp.float32)
+        found = found.astype(jnp.bfloat16)
         for c in range(chunks):
-            out_ref[c, :, part * width : (part + 1) * width] = found[
-                :, c * width : (c + 1) * width
-            ].astype(jnp.bfloat16)
+            out_ref[c, :, part * wide : (part + 1) * wide] = found[:, c * wide : (c + 1) * wide]
 
 
 def steering(input_feed, beam_grid, table, chunks):
@@ -215,13 +267,17 @@
         compiler_params=pltpu.CompilerParams(vmem_limit_bytes=32 * MIB),
         cost_estimate=cost,
         name="steering",
-    )(input_feed.reshape(inputs, 1), beam_grid.reshape(1, beams), table)
+    )(input_feed.reshape(1, inputs), beam_grid.reshape(1, beams), table)
 
 
 def products_kernel(
-    n_time, n_input, frame_count, first, count, x0_ref, xl_ref, steer_ref, *rest
+    n_time, n_input, frame_count, first, count, n_late, steer_ref, *rest
 ):
-    vis_ref, power_ref, arrived, ordered, held, ring, sems, ring_sems = rest[-8:]
+    early_ref, late_refs, rest = rest[0], rest[1 : n_late + 1], rest[n_late + 1 :]
+    earlier_ref = rest[1] if first else None
+    vis_ref, power_ref, arrived, ordered, held, ring, sems, ring_sems, in_sems, early, *late = rest[
+        2 if first else 0 :
+    ]
     step, steps = pl.program_id(0), pl.num_programs(0)
     chunk = step % SUB
     slots = ring.shape[0]
@@ -232,42 +288,62 @@
             ring.at[slot, part], vis_ref.at[first + at, part], ring_sems.at[slot, part]
         )
 
+    half = n_time * frame_count
+    rows_per = 2 * half
+    width = early.shape[2]
+    inputs = n_input * width
+    tile = 2 * SUB
+    start = early_start(first)
+
     def steer_copy(c):
         return pltpu.make_async_copy(steer_ref.at[c], held.at[c], sems.at[c])
 
     @pl.when(step == 0)
     def _():
+        rows = slice(start, start + early.shape[1])
+        copies = [pltpu.make_async_copy(early_ref.at[:, rows], early, in_sems.at[0])]
+        copies += [
+            pltpu.make_async_copy(ref, late[z], in_sems.at[1 + z]) for z, ref in enumerate(late_refs)
+        ]
+        for copy in copies:
+            copy.start()
         steer_copy(0).start()
-
-    half = n_time * frame_count
-    rows_per = 2 * half
-    width = x0_ref.shape[2]
-    inputs = n_input * width
-    tile = 2 * SUB
+        if first:
+            power_ref[...] = earlier_ref[...]
+        for copy in copies:
+            copy.wait()
+
+    def assemble(sub):
+        at = sub * tile
+        at_early = first * 2 - start + sub * tile
+        for t in range(n_time):
+            for z in range(n_input):
+                source = lax.rem(lax.axis_index("inp") + n_input - z, n_input)
+                slot = t * frame_count * tile
+                piece = early[t * n_input + z, at_early : at_early + tile, :]
+                arrived[z, slot : slot + tile, :] = piece
+                for f in range(1, frame_count):
+                    slot = (t * frame_count + f) * tile
+                    if n_late == 1:
+                        piece = late[0][t * n_input + z, f - 1, at : at + tile, :]
+                        arrived[z, slot : slot + tile, :] = piece
+                    else:
+                        row = (f - 1) * 2 * count + at
+                        arrived[source, slot : slot + tile, :] = late[z][t, row : row + tile, :]
+
+    for sub in range(count // SUB):
+        pl.when(step == sub * SUB)(functools.partial(assemble, sub))
 
     @pl.when(step % SUB == 0)
     def _():
-        sub = step // SUB
-        at = pl.multiple_of((first // SUB + sub) * tile, tile)
-        at_later = pl.multiple_of(sub * tile, tile)
-        for t in range(n_time):
-            for i in range(n_input):
-                source = t * n_input + i
-                lanes = slice(i * width, (i + 1) * width)
-                for f in range(frame_count):
-                    slot = (t * frame_count + f) * tile
-                    if f == 0:
-                        piece = x0_ref[source, pl.ds(at, tile), :]
-                    else:
-                        piece = xl_ref[source, f - 1, pl.ds(at_later, tile), :]
-                    arrived[slot : slot + tile, lanes] = piece
         total = SUB * rows_per
         row = lax.broadcasted_iota(jnp.int32, (total, total), 0)
         column = lax.broadcasted_iota(jnp.int32, (total, total), 1)
         source = (row % half) * tile + (row // rows_per) * 2 + (row // half) % 2
         pick = jnp.where(column == source, 1.0, 0.0).astype(jnp.bfloat16)
-        sorted_rows = jnp.dot(pick, arrived[...], preferred_element_type=jnp.float32)
-        ordered[...] = sorted_rows.astype(jnp.bfloat16)
+        for z in range(n_input):
+            sorted_rows = jnp.dot(pick, arrived[z], preferred_element_type=jnp.float32)
+            ordered[:, z * width : (z + 1) * width] = sorted_rows.astype(jnp.bfloat16)
 
     @pl.when(step < SUB)
     def _():
@@ -297,7 +373,7 @@
         beam_re = cos_part[rows_re] - sin_part[rows_im]
         beam_im = sin_part[rows_re] + cos_part[rows_im]
         power = jnp.sum(beam_re * beam_re + beam_im * beam_im, axis=0, keepdims=True)
-        row = (step // SUB) % 2 * SUB + c
+        row = (first // SUB + step // SUB) % 2 * SUB + c
         power_ref[pl.ds(row, 1), lanes] = power * (1.0 / half)
 
     block = min(inputs, 256)
@@ -322,45 +398,55 @@
                 vis_copy(at, part).wait()
 
 
-def products(sizes, first, count, x0, xl, steer, so_far):
+def early_start(first):
+    return 2 * first // 16 * 16
+
+
+def products(sizes, first, count, early, late, steer, so_far):
     n_time, n_input, frame_count, per_dev = sizes
-    inputs = n_input * x0.shape[2]
+    width = early.shape[2]
+    inputs = n_input * width
     beams = steer.shape[0] * steer.shape[2] // 2
-    whole = pl.BlockSpec(memory_space=pltpu.VMEM)
     rows = 2 * n_time * frame_count * SUB
     slots = min(3, count)
+    start = early_start(first)
+    stop = -(-2 * (first + count) // 16) * 16
     cost = pl.CostEstimate(
         flops=count * 2 * rows // SUB * inputs * (2 * inputs + 2 * beams),
         bytes_accessed=count * 4 * inputs * inputs + 4 * inputs * beams,
         transcendentals=0,
     )
-    operands = [x0, xl, steer]
-    specs = [whole] * 2 + [pl.BlockSpec(memory_space=pltpu.HBM)]
+    far = pl.BlockSpec(memory_space=pltpu.HBM)
+    power_spec = pl.BlockSpec((2 * SUB, beams), lambda c: ((first + c) // (2 * SUB), 0))
+    operands = [steer, early, *late]
+    specs = [far] * len(operands)
     aliases = {}
     for at, block in enumerate(so_far):
         aliases[len(operands)] = at
         operands.append(block)
-        specs.append(pl.BlockSpec(memory_space=pl.ANY))
-    return pl.pallas_call(
-        functools.partial(products_kernel, n_time, n_input, frame_count, first, count),
+        specs.append(power_spec if at == 1 else far)
+    return pl.pallas_call(
+        functools.partial(
+            products_kernel, n_time, n_input, frame_count, first, count, len(late)
+        ),
         grid=(count,),
         in_specs=specs,
-        out_specs=[
-            pl.BlockSpec(memory_space=pltpu.HBM),
-            pl.BlockSpec((2 * SUB, beams), lambda c: ((first + c) // (2 * SUB), 0)),
-        ],
+        out_specs=[far, power_spec],
         out_shape=[
             jax.ShapeDtypeStruct((per_dev, 2, inputs, inputs), jnp.bfloat16),
             jax.ShapeDtypeStruct((per_dev, beams), jnp.float32),
         ],
         scratch_shapes=[
-            pltpu.VMEM((rows, inputs), jnp.bfloat16),
+            pltpu.VMEM((n_input, rows, width), jnp.bfloat16),
             pltpu.VMEM((rows, inputs), jnp.bfloat16),
             pltpu.VMEM(steer.shape, jnp.bfloat16),
             pltpu.VMEM((slots, 2, inputs, inputs), jnp.bfloat16),
             pltpu.SemaphoreType.DMA((SUB,)),
             pltpu.SemaphoreType.DMA((slots, 2)),
-        ],
+            pltpu.SemaphoreType.DMA((1 + len(late),)),
+            pltpu.VMEM((n_time * n_input, stop - start, width), jnp.bfloat16),
+        ]
+        + [pltpu.VMEM(block.shape, jnp.bfloat16) for block in late],
         input_output_aliases=aliases,
         compiler_params=pltpu.CompilerParams(vmem_limit_bytes=58 * MIB),
         cost_estimate=cost,
@@ -370,6 +456,13 @@
 
 def exchanged(block):
     return lax.all_to_all(block, AXES, 0, 0, tiled=True)
+
+
+def onward(block, axis, distance):
+    if distance == 0:
+        return block
+    devices = lax.axis_size(axis)
+    return lax.ppermute(block, axis, [(i, (i + distance) % devices) for i in range(devices)])
 
 
 def in_pieces(voltages, input_gain, input_feed, beam_grid):
@@ -378,7 +471,7 @@
     n_input = lax.axis_size("inp")
     dests = n_time * n_input
     per_dev = CH // dests
-    last = per_dev // 2 // (2 * SUB) * (2 * SUB)
+    last = LAST_GROUP
     counts = (per_dev - last, last)
     back = [(i + 1, i) for i in range(n_time - 1)]
 
@@ -388,20 +481,24 @@
 
     widths = ((TAPS - 2) * L, L)
     later = [lax.ppermute(head, "tm", back) for head in heads_of(voltages, widths)]
-    first = first_frame(dests, voltages, gain, window, table)
-    x0 = exchanged(first)
+    early = exchanged(first_frame(dests, voltages, gain, window, table))
+
+    steer = steering(input_feed, beam_grid, jnp.asarray(steer_grid(input_feed.shape[0])), SUB)
     parts = ()
     for frame in range(1, frame_count):
         cuts = [2 * count for count in counts]
-        parts = later_frame(frame, dests, cuts, voltages, later, gain, window, table, parts)
-    steer = steering(input_feed, beam_grid, jnp.asarray(steer_grid(input_feed.shape[0])), SUB)
-    send_a, x0, steer = lax.optimization_barrier((parts[0], x0, steer))
-    xa = exchanged(send_a)
-    send_b, xa = lax.optimization_barrier((parts[1], xa))
-    xb = exchanged(send_b)
+        if frame == frame_count - 1:
+            parts, steer = lax.optimization_barrier((parts, steer))
+        parts = later_frame(frame, 1, dests, cuts, voltages, later, gain, window, table, parts)
+    send, early = lax.optimization_barrier((parts[0], early))
+    arrived = exchanged(send)
+    blocks = [onward(block, "tm", t) for t, block in enumerate(to_tm(n_time, n_input, parts[1]))]
+    onwards = to_inp(blocks)
+    arrived, _ = lax.optimization_barrier((arrived, onwards))
+    onwards = [onward(block, "inp", z) for z, block in enumerate(onwards)]
     sizes = (n_time, n_input, frame_count, per_dev)
-    found = products(sizes, 0, counts[0], x0, xa, steer, ())
-    return products(sizes, counts[0], counts[1], x0, xb, steer, found)
+    found = products(sizes, 0, counts[0], early, [arrived], steer, ())
+    return products(sizes, counts[0], counts[1], early, onwards, steer, found)
 
 
 def whole_channel(spectrum, steer):
@@ -460,7 +557,7 @@
 def on_device(voltages, input_gain, input_feed, beam_grid):
     per_dev = CH // (lax.axis_size("tm") * lax.axis_size("inp"))
     slots = lax.axis_size("tm") * (voltages.shape[1] // L)
-    whole_tiles = per_dev % (4 * SUB) == 0 and slots % 16 == 0 and beam_grid.shape[0] % (SUB * 128) == 0
+    whole_tiles = per_dev % (4 * SUB) == 0 and voltages.shape[1] >= TAPS * L and slots % 16 == 0 and beam_grid.shape[0] % (SUB * 128) == 0
     if whole_tiles and slots & (slots - 1) == 0:
         return in_pieces(voltages, input_gain, input_feed, beam_grid)
     return at_once(voltages, input_gain, input_feed, beam_grid)

time: 101 us -> 96.6 us (0.956)
  blocking collectives: 26.8 us -> 0 us
  starting transfers between devices: 14.6 us -> 30.1 us
  waiting for transfers between devices: 10.6 us -> 16.8 us
  local copies, waits for them, and re-layouts: 1.17 us -> 2.39 us
    all_to_all x1 -> x0, blocking collectives: 26.8 us -> none  [exchanged(): return lax.all_to_all(block, AXES, 0, 0, tiled=True)]
    ppermute x0 -> x10, starting transfers between devices: none -> 12.6 us  [onward(): lax.ppermute(block, axis, [(i, (i + distance) % devices) for i in range(d...]
    ppermute x0 -> x10, waiting for transfers between devices: none -> 11.5 us  [onward(): lax.ppermute(block, axis, [(i, (i + distance) % devices) for i in range(d...]
    all_to_all x2, waiting for transfers between devices: 5.34 us -> 0.01 us  [exchanged(): return lax.all_to_all(block, AXES, 0, 0, tiled=True)]
    all_to_all x2, starting transfers between devices: 10.4 us -> 13.3 us  [exchanged(): return lax.all_to_all(block, AXES, 0, 0, tiled=True)]
    unnamed x18 -> x30, local copies, waits for them, and re-layouts: 0.95 us -> 2.39 us
  transfers between devices with their start and end apart: 4 -> 14, of which waited for: 3 -> 8; matrix products, arithmetic and copies ran while one was open for 0% -> 0% of each run, Pallas kernels for 28% -> 29%
where the time goes in v3:
time: 96.6 us; the launch traced here: 96.1 us
  Pallas kernels  45.9 us (48%)
  starting transfers between devices  30.1 us (31%)
  waiting for transfers between devices  16.8 us (17%)
  local copies, waits for them, and re-layouts  2.39 us (2%)
    pallas_call x2, Pallas kernels, products(): pl.pallas_call(functools.partial(products_kernel, n_time, n_input, frame_...  30 us
    all_to_all x2, starting transfers between devices, exchanged(): return lax.all_to_all(block, AXES, 0, 0, tiled=True)  13.3 us
    ppermute x10, starting transfers between devices, onward(): lax.ppermute(block, axis, [(i, (i + distance) % devices) for i in range(d...  12.6 us
    ppermute x10, waiting for transfers between devices, onward(): lax.ppermute(block, axis, [(i, (i + distance) % devices) for i in range(d...  11.5 us
    pallas_call x3, Pallas kernels, later_frame(): pl.pallas_call(functools.partial(later_kernel, frame, len(later), len(cut...  5.47 us
    ppermute x2, waiting for transfers between devices, in_pieces(): lax.ppermute(head, 'tm', back)  5.32 us
    ppermute x2, starting transfers between devices, in_pieces(): lax.ppermute(head, 'tm', back)  4.26 us
    pallas_call x1, Pallas kernels, first_frame(): pl.pallas_call(first_kernel, in_specs=[far] * 4, out_shape=jax.ShapeDtype...  3.9 us
  transfers between devices with their start and end apart: 14, of which 8 were waited for; matrix products, arithmetic and copies ran while one was open for 0% of the time, Pallas kernels for 29%

profile of v3, /device:TPU:1, one launch (start us, length us, event | category | flops | bytes accessed | tf_op | source)
XLA Modules:
  0.0 96.1 jit_solution(7999205254622881129)
XLA Ops:
  0.6 0.0 copy-start.8
  0.6 0.0 copy-start.7
  0.7 0.0 copy-start.6
  0.7 2.5 %heads.1 = (bf16[256,2048]{1,0:T(8,128)(2,1)}, bf16[256,1024]{1,0:T(8,128)(2,1)}) custom-call(bf16[256,4096]{1,0:T(8,128)(2,1)} %v_ref.9), custom_call_target="tpu_custom_call" | custom-call | bytes 3145728 | tf_op jit(solution)/shard_map/heads/pallas_call | solution.py:92
  3.2 0.0 copy-start.14
  3.2 2.1 %collective-permute-start = (bf16[256,2048]{1,0:T(8,128)(2,1)}, bf16[256,2048]{1,0:T(8,128)(2,1)S(1)}, u32[]{:S(2)}, u32[]{:S(2)}) collective-permute-start(bf16[256,2048]{1,0:T(8,128)(2,1)} %get-tuple-element.30), channel_id=1, source_target_pairs={{4,0},{8,4},{12,8},{16,12},{20,16},{24,20},{28,24},{5,1},{9,5},{13... | collective-permute-start | bytes 3145736 | tf_op jit(solution)/shard_map/ppermute | solution.py:483
  5.3 3.9 %first_frame.1 = bf16[32,32,256]{2,1,0:T(8,128)(2,1)} custom-call(bf16[256,4096]{1,0:T(8,128)(2,1)} %v_ref.9, f32[1,256]{1,0:T(1,128)} %bitcast.3, f32[4,1024]{1,0:T(4,128)} %constant.6.clone.window_ref, bf16[1024,1024]{1,0:T(8,128)(2,1)} %constant.7.clone.table_ref), custom_call_target="tpu_custom_call" | custom-call | flops 536870912 | bytes 4194304 | tf_op jit(solution)/shard_map/first_frame/pallas_call | solution.py:128
  9.2 7.2 %all-to-all-start = ((bf16[32,32,256]{2,1,0:T(8,128)(2,1)}), bf16[32,32,256]{2,1,0:T(8,128)(2,1)S(1)}, u32[]{:S(2)}, u32[]{:S(2)}) async-start(bf16[32,32,256]{2,1,0:T(8,128)(2,1)} %first_frame.1), calls=%async_computation | async-start | bytes 1048576 | tf_op jit(solution)/shard_map/all_to_all | solution.py:458
  16.4 0.0 copy-done.14
  16.4 2.2 %collective-permute-start.1 = (bf16[256,1024]{1,0:T(8,128)(2,1)S(1)}, bf16[256,1024]{1,0:T(8,128)(2,1)S(1)}, u32[]{:S(2)}, u32[]{:S(2)}) collective-permute-start(bf16[256,1024]{1,0:T(8,128)(2,1)S(1)} %copy-done.14), channel_id=1, source_target_pairs={{4,0},{8,4},{12,8},{16,12},{20,16},{24,20},{28,24},{5,1},{9,5},{13... | collective-permute-start | bytes 1572872 | tf_op jit(solution)/shard_map/ppermute | solution.py:483
  18.6 0.0 copy-done.8
  18.6 0.0 copy-done.7
  18.6 0.0 copy-done.6
  18.6 0.0 copy-start
  18.6 0.0 copy-start.1
  18.6 0.0 copy-start.3
  18.7 0.0 copy-start.5
  18.7 3.9 %steering.1.steer_ref = bf16[4,1024,512]{2,1,0:T(8,128)(2,1)S(1)} custom-call(s32[1,1024]{1,0:T(1,128)S(1)} %bitcast.7, s32[1,1024]{1,0:T(1,128)S(1)} %bitcast.8, bf16[2,512,512]{2,1,0:T(8,128)(2,1)S(1)} %copy-done.8), custom_call_target="tpu_custom_call" | custom-call | flops 3221225472 | bytes 4194304 | tf_op jit(solution)/shard_map/steering/pallas_call | solution.py:264
  22.6 0.0 copy-start.2
  22.6 0.6 collective-permute-done.refs_0_
  23.1 0.0 copy-done
  23.2 0.0 copy-done.1
  23.2 0.0 copy-done.3
  23.2 0.0 copy-done.5
  23.2 1.8 %later_frame.3 = (bf16[32,3,16,256]{3,2,1,0:T(8,128)(2,1)}, bf16[32,3,16,256]{3,2,1,0:T(8,128)(2,1)S(1)}) custom-call(bf16[256,4096]{1,0:T(8,128)(2,1)S(1)} %copy-done, f32[1,256]{1,0:T(1,128)S(1)} %bitcast.4, f32[4,1024]{1,0:T(4,128)S(1)} %copy-done.3, bf16[1024,1024]{1,0:T(8,128)(2,1)S(1)} %copy-done.1, bf16[256,2048]{1,0:T(8,128)(2,1)S(1)} %collective-permute-done.refs_0_), custom_call_target="tpu_custom_call" | custom-call | flops 536870912 | bytes 3145728 | tf_op jit(solution)/shard_map/later_frame/pallas_call | solution.py:220
  25.0 1.8 %later_frame.4 = (bf16[32,3,16,256]{3,2,1,0:T(8,128)(2,1)}, bf16[32,3,16,256]{3,2,1,0:T(8,128)(2,1)S(1)}) custom-call(bf16[256,4096]{1,0:T(8,128)(2,1)S(1)} %copy-done, f32[1,256]{1,0:T(1,128)S(1)} %bitcast.5, f32[4,1024]{1,0:T(4,128)S(1)} %copy-done.3, bf16[1024,1024]{1,0:T(8,128)(2,1)S(1)} %copy-done.1, ...), custom_call_target="tpu_custom_call", output_to_operand_aliasing={{0}: (5, {}), {1}: (6, {})} | custom-call | flops 536870912 | bytes 3145728 | tf_op jit(solution)/shard_map/later_frame/pallas_call | solution.py:220
  26.8 0.0 copy-done.2
  26.8 4.7 %collective-permute-done.1.refs_1_ = bf16[256,1024]{1,0:T(8,128)(2,1)S(1)} collective-permute-done((bf16[256,1024]{1,0:T(8,128)(2,1)S(1)}, bf16[256,1024]{1,0:T(8,128)(2,1)S(1)}, u32[]{:S(2)}, u32[]{:S(2)}) %collective-permute-start.1) | collective-permute-done | bytes 524320 | tf_op jit(solution)/shard_map/ppermute | solution.py:483
  31.6 1.8 %later_frame.5 = (bf16[32,3,16,256]{3,2,1,0:T(8,128)(2,1)}, bf16[32,3,16,256]{3,2,1,0:T(8,128)(2,1)S(1)}) custom-call(bf16[256,4096]{1,0:T(8,128)(2,1)S(1)} %copy-done, f32[1,256]{1,0:T(1,128)S(1)} %bitcast.6, f32[4,1024]{1,0:T(4,128)S(1)} %copy-done.3, bf16[1024,1024]{1,0:T(8,128)(2,1)S(1)} %copy-done.1, ...), custom_call_target="tpu_custom_call", output_to_operand_aliasing={{0}: (6, {}), {1}: (7, {})} | custom-call | flops 536870912 | bytes 3145728 | tf_op jit(solution)/shard_map/later_frame/pallas_call | solution.py:220
  33.4 0.0 all-to-all-done.rest_0_
  33.4 6.0 %all-to-all-start.1 = ((bf16[32,3,16,256]{3,2,1,0:T(8,128)(2,1)}), bf16[32,3,16,256]{3,2,1,0:T(8,128)(2,1)S(1)}, u32[]{:S(2)}, u32[]{:S(2)}) async-start(bf16[32,3,16,256]{3,2,1,0:T(8,128)(2,1)} %get-tuple-element.54), calls=%async_computation.1 | async-start | bytes 1572864 | tf_op jit(solution)/shard_map/all_to_all | solution.py:458
  39.4 0.1 to_tm.1
  39.5 1.7 %collective-permute-start.2 = (bf16[4,48,256]{2,1,0:T(8,128)(2,1)S(1)}, bf16[4,48,256]{2,1,0:T(8,128)(2,1)S(1)}, u32[]{:S(2)}, u32[]{:S(2)}) collective-permute-start(bf16[4,48,256]{2,1,0:T(8,128)(2,1)S(1)} %get-tuple-element.43), channel_id=1, source_target_pairs={{0,4},{4,8},{8,12},{12,16},{16,20},{20,24},{24,28},{28,0},{1,5},{5... | collective-permute-start | bytes 294920 | tf_op jit(solution)/shard_map/ppermute | solution.py:465
  41.2 1.2 %collective-permute-start.3 = (bf16[4,48,256]{2,1,0:T(8,128)(2,1)S(1)}, bf16[4,48,256]{2,1,0:T(8,128)(2,1)S(1)}, u32[]{:S(2)}, u32[]{:S(2)}) collective-permute-start(bf16[4,48,256]{2,1,0:T(8,128)(2,1)S(1)} %get-tuple-element.44), channel_id=1, source_target_pairs={{0,8},{4,12},{8,16},{12,20},{16,24},{20,28},{24,0},{28,4},{1,9},{5... | collective-permute-start | bytes 294920 | tf_op jit(solution)/shard_map/ppermute | solution.py:465
  42.4 0.4 collective-permute-start.4
  42.8 0.3 collective-permute-start.5
  43.1 2.3 %collective-permute-start.6 = (bf16[4,48,256]{2,1,0:T(8,128)(2,1)S(1)}, bf16[4,48,256]{2,1,0:T(8,128)(2,1)S(1)}, u32[]{:S(2)}, u32[]{:S(2)}) collective-permute-start(bf16[4,48,256]{2,1,0:T(8,128)(2,1)S(1)} %get-tuple-element.47), channel_id=1, source_target_pairs={{0,20},{4,24},{8,28},{12,0},{16,4},{20,8},{24,12},{28,16},{1,21},{... | collective-permute-start | bytes 294920 | tf_op jit(solution)/shard_map/ppermute | solution.py:465
  45.4 0.9 collective-permute-done.2.refs_1_
  46.2 2.1 %collective-permute-start.7 = (bf16[4,48,256]{2,1,0:T(8,128)(2,1)S(1)}, bf16[4,48,256]{2,1,0:T(8,128)(2,1)S(1)}, u32[]{:S(2)}, u32[]{:S(2)}) collective-permute-start(bf16[4,48,256]{2,1,0:T(8,128)(2,1)S(1)} %get-tuple-element.48), channel_id=1, source_target_pairs={{0,24},{4,28},{8,0},{12,4},{16,8},{20,12},{24,16},{28,20},{1,25},{... | collective-permute-start | bytes 294920 | tf_op jit(solution)/shard_map/ppermute | solution.py:465
  48.3 4.7 %collective-permute-done.3.refs_2_ = bf16[4,48,256]{2,1,0:T(8,128)(2,1)S(1)} collective-permute-done((bf16[4,48,256]{2,1,0:T(8,128)(2,1)S(1)}, bf16[4,48,256]{2,1,0:T(8,128)(2,1)S(1)}, u32[]{:S(2)}, u32[]{:S(2)}) %collective-permute-start.3) | collective-permute-done | bytes 98336 | tf_op jit(solution)/shard_map/ppermute | solution.py:465
  53.0 0.0 collective-permute-start.8
  53.0 1.2 %collective-permute-done.4.refs_3_ = bf16[4,48,256]{2,1,0:T(8,128)(2,1)S(1)} collective-permute-done((bf16[4,48,256]{2,1,0:T(8,128)(2,1)S(1)}, bf16[4,48,256]{2,1,0:T(8,128)(2,1)S(1)}, u32[]{:S(2)}, u32[]{:S(2)}) %collective-permute-start.4) | collective-permute-done | bytes 98336 | tf_op jit(solution)/shard_map/ppermute | solution.py:465
  54.2 4.4 %collective-permute-done.5.refs_4_ = bf16[4,48,256]{2,1,0:T(8,128)(2,1)S(1)} collective-permute-done((bf16[4,48,256]{2,1,0:T(8,128)(2,1)S(1)}, bf16[4,48,256]{2,1,0:T(8,128)(2,1)S(1)}, u32[]{:S(2)}, u32[]{:S(2)}) %collective-permute-start.5) | collective-permute-done | bytes 98336 | tf_op jit(solution)/shard_map/ppermute | solution.py:465
  58.6 0.2 collective-permute-done.6.refs_5_
  58.8 0.0 collective-permute-done.7.refs_6_
  58.8 0.1 collective-permute-done.8.refs_7_
  58.9 0.1 to_inp.1
  59.0 0.0 copy-start.4
  59.0 0.7 copy-done.4
  59.6 2.2 %collective-permute-start.9 = (bf16[8,48,256]{2,1,0:T(8,128)(2,1)S(1)}, bf16[8,48,256]{2,1,0:T(8,128)(2,1)S(1)}, u32[]{:S(2)}, u32[]{:S(2)}) collective-permute-start(bf16[8,48,256]{2,1,0:T(8,128)(2,1)S(1)} %get-tuple-element.51), channel_id=1, source_target_pairs={{0,1},{1,2},{2,3},{3,0},{4,5},{5,6},{6,7},{7,4},{8,9},{9,10},{10,1... | collective-permute-start | bytes 589832 | tf_op jit(solution)/shard_map/ppermute | solution.py:465
  61.8 1.1 %collective-permute-start.10 = (bf16[8,48,256]{2,1,0:T(8,128)(2,1)S(1)}, bf16[8,48,256]{2,1,0:T(8,128)(2,1)S(1)}, u32[]{:S(2)}, u32[]{:S(2)}) collective-permute-start(bf16[8,48,256]{2,1,0:T(8,128)(2,1)S(1)} %get-tuple-element.52), channel_id=1, source_target_pairs={{0,2},{1,3},{2,0},{3,1},{4,6},{5,7},{6,4},{7,5},{8,10},{9,11},{10,... | collective-permute-start | bytes 589832 | tf_op jit(solution)/shard_map/ppermute | solution.py:465
  62.9 1.4 %collective-permute-start.11 = (bf16[8,48,256]{2,1,0:T(8,128)(2,1)S(1)}, bf16[8,48,256]{2,1,0:T(8,128)(2,1)S(1)}, u32[]{:S(2)}, u32[]{:S(2)}) collective-permute-start(bf16[8,48,256]{2,1,0:T(8,128)(2,1)S(1)} %get-tuple-element.53), channel_id=1, source_target_pairs={{0,3},{1,0},{2,1},{3,2},{4,7},{5,4},{6,5},{7,6},{8,11},{9,8},{10,9... | collective-permute-start | bytes 589832 | tf_op jit(solution)/shard_map/ppermute | solution.py:465
  64.3 0.0 all-to-all-done.1.rest_1_
  64.3 0.0 copy-done.9
  64.3 0.9 copy-done.10
  65.2 14.5 %products.2 = (bf16[16,2,1024,1024]{3,2,1,0:T(8,128)(2,1)}, f32[16,1024]{1,0:T(8,128)}) custom-call(bf16[4,1024,512]{2,1,0:T(8,128)(2,1)} %copy-done.2, bf16[32,32,256]{2,1,0:T(8,128)(2,1)} %copy-done.9, bf16[32,3,16,256]{3,2,1,0:T(8,128)(2,1)} %copy-done.10), custom_call_target="tpu_custom_call" | custom-call | flops 4294967296 | bytes 37748736 | tf_op jit(solution)/shard_map/products/pallas_call | solution.py:428
  79.7 0.0 collective-permute-done.9.rest_2_
  79.7 0.0 copy-start.11
  79.7 0.0 collective-permute-done.10.rest_3_
  79.8 0.0 collective-permute-done.11.rest_4_
  79.8 0.6 copy-done.11
  80.4 0.1 copy-done.12
  80.5 0.1 copy-done.13
  80.6 15.5 %products.3 = (bf16[16,2,1024,1024]{3,2,1,0:T(8,128)(2,1)}, f32[16,1024]{1,0:T(8,128)}) custom-call(bf16[4,1024,512]{2,1,0:T(8,128)(2,1)} %copy-done.2, bf16[32,32,256]{2,1,0:T(8,128)(2,1)} %copy-done.9, bf16[8,48,256]{2,1,0:T(8,128)(2,1)} %copy-done.4, bf16[8,48,256]{2,1,0:T(8,128)(2,1)} %copy-done.11, ...), custom_call_target="tpu_custom_call", output_to_operand_aliasing={{0}: (6, {}), {1}: (7, {})} | custom-call | flops 4294967296 | bytes 37748736 | tf_op jit(solution)/shard_map/products/pallas_call | solution.py:428
  (4 shorter events, 0.0 us)
Async XLA Ops:
  0.6 18.0 %copy-start.8 = (bf16[2,512,512]{2,1,0:T(8,128)(2,1)S(1)}, bf16[2,512,512]{2,1,0:T(8,128)(2,1)}, u32[]{:S(2)}) copy-start(bf16[2,512,512]{2,1,0:T(8,128)(2,1)} %constant.8.clone.table_ref) | copy-start | bytes 3145732
  0.6 18.0 %copy-start.7 = (s32[1024]{0:T(1024)S(1)}, s32[1024]{0:T(1024)}, u32[]{:S(2)}) copy-start(s32[1024]{0:T(1024)} %param.10) | copy-start | bytes 12292
  0.7 18.0 %copy-start.6 = (s32[1024]{0:T(1024)S(1)}, s32[1024]{0:T(1024)}, u32[]{:S(2)}) copy-start(s32[1024]{0:T(1024)} %param.9) | copy-start | bytes 12292
  3.2 13.3 %copy-start.14 = (bf16[256,1024]{1,0:T(8,128)(2,1)S(1)}, bf16[256,1024]{1,0:T(8,128)(2,1)}, u32[]{:S(2)}) copy-start(bf16[256,1024]{1,0:T(8,128)(2,1)} %get-tuple-element.36) | copy-start | bytes 1572868
  3.2 20.0 %collective-permute-start = (bf16[256,2048]{1,0:T(8,128)(2,1)}, bf16[256,2048]{1,0:T(8,128)(2,1)S(1)}, u32[]{:S(2)}, u32[]{:S(2)}) collective-permute-start(bf16[256,2048]{1,0:T(8,128)(2,1)} %get-tuple-element.30), channel_id=1, source_target_pairs={{4,0},{8,4},{12,8},{16,12},{20,16},{24,20},{28,24},{5,1},{9,5},{13... | collective-permute-start | bytes 3145736 | tf_op jit(solution)/shard_map/ppermute | solution.py:483
  9.2 24.2 %all-to-all-start = ((bf16[32,32,256]{2,1,0:T(8,128)(2,1)}), bf16[32,32,256]{2,1,0:T(8,128)(2,1)S(1)}, u32[]{:S(2)}, u32[]{:S(2)}) async-start(bf16[32,32,256]{2,1,0:T(8,128)(2,1)} %first_frame.1), calls=%async_computation | async-start | bytes 1048576 | tf_op jit(solution)/shard_map/all_to_all | solution.py:458
  16.4 15.1 %collective-permute-start.1 = (bf16[256,1024]{1,0:T(8,128)(2,1)S(1)}, bf16[256,1024]{1,0:T(8,128)(2,1)S(1)}, u32[]{:S(2)}, u32[]{:S(2)}) collective-permute-start(bf16[256,1024]{1,0:T(8,128)(2,1)S(1)} %copy-done.14), channel_id=1, source_target_pairs={{4,0},{8,4},{12,8},{16,12},{20,16},{24,20},{28,24},{5,1},{9,5},{13... | collective-permute-start | bytes 1572872 | tf_op jit(solution)/shard_map/ppermute | solution.py:483
  18.6 4.5 %copy-start = (bf16[256,4096]{1,0:T(8,128)(2,1)S(1)}, bf16[256,4096]{1,0:T(8,128)(2,1)}, u32[]{:S(2)}) copy-start(bf16[256,4096]{1,0:T(8,128)(2,1)} %v_ref.9) | copy-start | bytes 6291460
  18.6 4.5 %copy-start.1 = (bf16[1024,1024]{1,0:T(8,128)(2,1)S(1)}, bf16[1024,1024]{1,0:T(8,128)(2,1)}, u32[]{:S(2)}) copy-start(bf16[1024,1024]{1,0:T(8,128)(2,1)} %constant.7.clone.table_ref) | copy-start | bytes 6291460
  18.6 4.5 %copy-start.3 = (f32[4,1024]{1,0:T(4,128)S(1)}, f32[4,1024]{1,0:T(4,128)}, u32[]{:S(2)}) copy-start(f32[4,1024]{1,0:T(4,128)} %constant.6.clone.window_ref) | copy-start | bytes 49156
  18.7 4.5 %copy-start.5 = (f32[256]{0:T(256)S(1)}, f32[256]{0:T(256)}, u32[]{:S(2)}) copy-start(f32[256]{0:T(256)} %param.8) | copy-start | bytes 3076
  22.6 4.3 %copy-start.2 = (bf16[4,1024,512]{2,1,0:T(8,128)(2,1)}, bf16[4,1024,512]{2,1,0:T(8,128)(2,1)S(1)}, u32[]{:S(2)}) copy-start(bf16[4,1024,512]{2,1,0:T(8,128)(2,1)S(1)} %steering.1.steer_ref) | copy-start | bytes 12582916
  33.4 30.9 %copy-start.9 = (bf16[32,32,256]{2,1,0:T(8,128)(2,1)}, bf16[32,32,256]{2,1,0:T(8,128)(2,1)S(1)}, u32[]{:S(2)}) copy-start(bf16[32,32,256]{2,1,0:T(8,128)(2,1)S(1)} %all-to-all-done.rest_0_) | copy-start | bytes 1572868
  33.4 30.9 %all-to-all-start.1 = ((bf16[32,3,16,256]{3,2,1,0:T(8,128)(2,1)}), bf16[32,3,16,256]{3,2,1,0:T(8,128)(2,1)S(1)}, u32[]{:S(2)}, u32[]{:S(2)}) async-start(bf16[32,3,16,256]{3,2,1,0:T(8,128)(2,1)} %get-tuple-element.54), calls=%async_computation.1 | async-start | bytes 1572864 | tf_op jit(solution)/shard_map/all_to_all | solution.py:458
  39.5 6.7 %collective-permute-start.2 = (bf16[4,48,256]{2,1,0:T(8,128)(2,1)S(1)}, bf16[4,48,256]{2,1,0:T(8,128)(2,1)S(1)}, u32[]{:S(2)}, u32[]{:S(2)}) collective-permute-start(bf16[4,48,256]{2,1,0:T(8,128)(2,1)S(1)} %get-tuple-element.43), channel_id=1, source_target_pairs={{0,4},{4,8},{8,12},{12,16},{16,20},{20,24},{24,28},{28,0},{1,5},{5... | collective-permute-start | bytes 294920 | tf_op jit(solution)/shard_map/ppermute | solution.py:465
  41.2 11.8 %collective-permute-start.3 = (bf16[4,48,256]{2,1,0:T(8,128)(2,1)S(1)}, bf16[4,48,256]{2,1,0:T(8,128)(2,1)S(1)}, u32[]{:S(2)}, u32[]{:S(2)}) collective-permute-start(bf16[4,48,256]{2,1,0:T(8,128)(2,1)S(1)} %get-tuple-element.44), channel_id=1, source_target_pairs={{0,8},{4,12},{8,16},{12,20},{16,24},{20,28},{24,0},{28,4},{1,9},{5... | collective-permute-start | bytes 294920 | tf_op jit(solution)/shard_map/ppermute | solution.py:465
  42.4 11.8 %collective-permute-start.4 = (bf16[4,48,256]{2,1,0:T(8,128)(2,1)S(1)}, bf16[4,48,256]{2,1,0:T(8,128)(2,1)S(1)}, u32[]{:S(2)}, u32[]{:S(2)}) collective-permute-start(bf16[4,48,256]{2,1,0:T(8,128)(2,1)S(1)} %get-tuple-element.45), channel_id=1, source_target_pairs={{0,12},{4,16},{8,20},{12,24},{16,28},{20,0},{24,4},{28,8},{1,13},{... | collective-permute-start | bytes 294920 | tf_op jit(solution)/shard_map/ppermute | solution.py:465
  42.8 15.8 %collective-permute-start.5 = (bf16[4,48,256]{2,1,0:T(8,128)(2,1)S(1)}, bf16[4,48,256]{2,1,0:T(8,128)(2,1)S(1)}, u32[]{:S(2)}, u32[]{:S(2)}) collective-permute-start(bf16[4,48,256]{2,1,0:T(8,128)(2,1)S(1)} %get-tuple-element.46), channel_id=1, source_target_pairs={{0,16},{4,20},{8,24},{12,28},{16,0},{20,4},{24,8},{28,12},{1,17},{... | collective-permute-start | bytes 294920 | tf_op jit(solution)/shard_map/ppermute | solution.py:465
  43.1 15.7 %collective-permute-start.6 = (bf16[4,48,256]{2,1,0:T(8,128)(2,1)S(1)}, bf16[4,48,256]{2,1,0:T(8,128)(2,1)S(1)}, u32[]{:S(2)}, u32[]{:S(2)}) collective-permute-start(bf16[4,48,256]{2,1,0:T(8,128)(2,1)S(1)} %get-tuple-element.47), channel_id=1, source_target_pairs={{0,20},{4,24},{8,28},{12,0},{16,4},{20,8},{24,12},{28,16},{1,21},{... | collective-permute-start | bytes 294920 | tf_op jit(solution)/shard_map/ppermute | solution.py:465
  46.2 12.6 %collective-permute-start.7 = (bf16[4,48,256]{2,1,0:T(8,128)(2,1)S(1)}, bf16[4,48,256]{2,1,0:T(8,128)(2,1)S(1)}, u32[]{:S(2)}, u32[]{:S(2)}) collective-permute-start(bf16[4,48,256]{2,1,0:T(8,128)(2,1)S(1)} %get-tuple-element.48), channel_id=1, source_target_pairs={{0,24},{4,28},{8,0},{12,4},{16,8},{20,12},{24,16},{28,20},{1,25},{... | collective-permute-start | bytes 294920 | tf_op jit(solution)/shard_map/ppermute | solution.py:465
  53.0 5.9 %collective-permute-start.8 = (bf16[4,48,256]{2,1,0:T(8,128)(2,1)S(1)}, bf16[4,48,256]{2,1,0:T(8,128)(2,1)S(1)}, u32[]{:S(2)}, u32[]{:S(2)}) collective-permute-start(bf16[4,48,256]{2,1,0:T(8,128)(2,1)S(1)} %get-tuple-element.49), channel_id=1, source_target_pairs={{0,28},{4,0},{8,4},{12,8},{16,12},{20,16},{24,20},{28,24},{1,29},{... | collective-permute-start | bytes 294920 | tf_op jit(solution)/shard_map/ppermute | solution.py:465
  59.0 0.7 copy-start.4
  59.6 20.1 %collective-permute-start.9 = (bf16[8,48,256]{2,1,0:T(8,128)(2,1)S(1)}, bf16[8,48,256]{2,1,0:T(8,128)(2,1)S(1)}, u32[]{:S(2)}, u32[]{:S(2)}) collective-permute-start(bf16[8,48,256]{2,1,0:T(8,128)(2,1)S(1)} %get-tuple-element.51), channel_id=1, source_target_pairs={{0,1},{1,2},{2,3},{3,0},{4,5},{5,6},{6,7},{7,4},{8,9},{9,10},{10,1... | collective-permute-start | bytes 589832 | tf_op jit(solution)/shard_map/ppermute | solution.py:465
  61.8 17.9 %collective-permute-start.10 = (bf16[8,48,256]{2,1,0:T(8,128)(2,1)S(1)}, bf16[8,48,256]{2,1,0:T(8,128)(2,1)S(1)}, u32[]{:S(2)}, u32[]{:S(2)}) collective-permute-start(bf16[8,48,256]{2,1,0:T(8,128)(2,1)S(1)} %get-tuple-element.52), channel_id=1, source_target_pairs={{0,2},{1,3},{2,0},{3,1},{4,6},{5,7},{6,4},{7,5},{8,10},{9,11},{10,... | collective-permute-start | bytes 589832 | tf_op jit(solution)/shard_map/ppermute | solution.py:465
  62.9 16.8 %collective-permute-start.11 = (bf16[8,48,256]{2,1,0:T(8,128)(2,1)S(1)}, bf16[8,48,256]{2,1,0:T(8,128)(2,1)S(1)}, u32[]{:S(2)}, u32[]{:S(2)}) collective-permute-start(bf16[8,48,256]{2,1,0:T(8,128)(2,1)S(1)} %get-tuple-element.53), channel_id=1, source_target_pairs={{0,3},{1,0},{2,1},{3,2},{4,7},{5,4},{6,5},{7,6},{8,11},{9,8},{10,9... | collective-permute-start | bytes 589832 | tf_op jit(solution)/shard_map/ppermute | solution.py:465
  64.3 0.9 copy-start.10
  79.7 0.7 copy-start.11
  79.8 0.8 copy-start.12
  79.8 0.8 copy-start.13

commit v4 on v3

--- a/solution.py
+++ b/solution.py
@@ -70,15 +70,16 @@
     return ref[:, frame * L : (frame + 1) * L]
 
 
-def heads_kernel(v_ref, *refs):
-    head_refs, held, sems = refs[:-2], refs[-2], refs[-1]
-    into, out, start = [], [], 0
-    for at, head_ref in enumerate(head_refs):
-        lanes = slice(start, start + head_ref.shape[1])
-        into.append(pltpu.make_async_copy(v_ref.at[:, lanes], held.at[:, lanes], sems.at[0, at]))
-        out.append(pltpu.make_async_copy(held.at[:, lanes], head_ref, sems.at[1, at]))
+def head_kernel(v_ref, head_ref, held, sems):
+    pieces = sems.shape[1]
+    rows = head_ref.shape[0] // pieces
+    into, out = [], []
+    for at in range(pieces):
+        block = pl.ds(at * rows, rows)
+        source = v_ref.at[block, : head_ref.shape[1]]
+        into.append(pltpu.make_async_copy(source, held.at[block], sems.at[0, at]))
+        out.append(pltpu.make_async_copy(held.at[block], head_ref.at[block], sems.at[1, at]))
         into[-1].start()
-        start = lanes.stop
     for first, second in zip(into, out):
         first.wait()
         second.start()
@@ -86,25 +87,28 @@
         copy.wait()
 
 
-def heads_of(voltages, widths):
-    rows, span = voltages.shape[0], sum(widths)
+def head_of(voltages, width):
+    rows = voltages.shape[0]
     far = pl.BlockSpec(memory_space=pltpu.HBM)
-    return pl.pallas_call(
-        heads_kernel,
+    pieces = 4 if rows % 64 == 0 else 1
+    return pl.pallas_call(
+        head_kernel,
         in_specs=[far],
-        out_specs=[far] * len(widths),
-        out_shape=[jax.ShapeDtypeStruct((rows, width), jnp.bfloat16) for width in widths],
+        out_specs=far,
+        out_shape=jax.ShapeDtypeStruct((rows, width), jnp.bfloat16),
         scratch_shapes=[
-            pltpu.VMEM((rows, span), jnp.bfloat16),
-            pltpu.SemaphoreType.DMA((2, len(widths))),
+            pltpu.VMEM((rows, width), jnp.bfloat16),
+            pltpu.SemaphoreType.DMA((2, pieces)),
         ],
         compiler_params=pltpu.CompilerParams(vmem_limit_bytes=58 * MIB),
-        cost_estimate=pl.CostEstimate(flops=0, bytes_accessed=4 * rows * span, transcendentals=0),
-        name="heads",
+        cost_estimate=pl.CostEstimate(flops=0, bytes_accessed=4 * rows * width, transcendentals=0),
+        name="head",
     )(voltages)
 
 
-def first_kernel(v_ref, gain_ref, window_ref, table_ref, out_ref, held, gain, window, table, sems):
+def first_kernel(
+    v_ref, gain_ref, window_ref, table_ref, out_ref, head_ref, held, gain, window, table, sems
+):
     copies = [
         pltpu.make_async_copy(frame_of(v_ref.at, tap), frame_of(held.at, tap), sems.at[tap])
         for tap in range(TAPS)
@@ -117,9 +121,12 @@
     table_copy.start()
     for copy in copies:
         copy.wait()
+    head_copy = pltpu.make_async_copy(frame_of(held.at, TAPS - 2), head_ref, sems.at[TAPS + 3])
+    head_copy.start()
     filtered = filtered_frame([frame_of(held, tap) for tap in range(TAPS)], gain, window)
     table_copy.wait()
     put_spectra(filtered, table, [out_ref])
+    head_copy.wait()
 
 
 def first_frame(dests, voltages, gain, window, table):
@@ -128,13 +135,17 @@
     return pl.pallas_call(
         first_kernel,
         in_specs=[far] * 4,
-        out_shape=jax.ShapeDtypeStruct((dests, 2 * CH // dests, rows), jnp.bfloat16),
+        out_specs=[pl.BlockSpec(memory_space=pltpu.VMEM), far],
+        out_shape=[
+            jax.ShapeDtypeStruct((dests, 2 * CH // dests, rows), jnp.bfloat16),
+            jax.ShapeDtypeStruct((rows, L), jnp.bfloat16),
+        ],
         scratch_shapes=[
             pltpu.VMEM((rows, TAPS * L), jnp.bfloat16),
             pltpu.VMEM(gain.shape, jnp.float32),
             pltpu.VMEM(window.shape, jnp.float32),
             pltpu.VMEM(table.shape, jnp.bfloat16),
-            pltpu.SemaphoreType.DMA((TAPS + 3,)),
+            pltpu.SemaphoreType.DMA((TAPS + 4,)),
         ],
         compiler_params=pltpu.CompilerParams(vmem_limit_bytes=58 * MIB),
         cost_estimate=pl.CostEstimate(
@@ -274,7 +285,8 @@
     n_time, n_input, frame_count, first, count, n_late, steer_ref, *rest
 ):
     early_ref, late_refs, rest = rest[0], rest[1 : n_late + 1], rest[n_late + 1 :]
-    earlier_ref = rest[1] if first else None
+    shared = first % (2 * SUB) != 0
+    earlier_ref = rest[1] if shared else None
     vis_ref, power_ref, arrived, ordered, held, ring, sems, ring_sems, in_sems, early, *late = rest[
         2 if first else 0 :
     ]
@@ -308,7 +320,7 @@
         for copy in copies:
             copy.start()
         steer_copy(0).start()
-        if first:
+        if shared:
             power_ref[...] = earlier_ref[...]
         for copy in copies:
             copy.wait()
@@ -417,14 +429,15 @@
         transcendentals=0,
     )
     far = pl.BlockSpec(memory_space=pltpu.HBM)
+    any_place = pl.BlockSpec(memory_space=pl.ANY)
     power_spec = pl.BlockSpec((2 * SUB, beams), lambda c: ((first + c) // (2 * SUB), 0))
     operands = [steer, early, *late]
-    specs = [far] * len(operands)
+    specs = [far] + [any_place] * (len(operands) - 1)
     aliases = {}
     for at, block in enumerate(so_far):
         aliases[len(operands)] = at
         operands.append(block)
-        specs.append(power_spec if at == 1 else far)
+        specs.append(power_spec if at == 1 and first % (2 * SUB) != 0 else far)
     return pl.pallas_call(
         functools.partial(
             products_kernel, n_time, n_input, frame_count, first, count, len(late)
@@ -448,7 +461,7 @@
         ]
         + [pltpu.VMEM(block.shape, jnp.bfloat16) for block in late],
         input_output_aliases=aliases,
-        compiler_params=pltpu.CompilerParams(vmem_limit_bytes=58 * MIB),
+        compiler_params=pltpu.CompilerParams(vmem_limit_bytes=50 * MIB),
         cost_estimate=cost,
         name="products",
     )(*operands)
@@ -479,9 +492,10 @@
     table = jnp.asarray(dft_rows())
     gain = input_gain.reshape(1, -1)
 
-    widths = ((TAPS - 2) * L, L)
-    later = [lax.ppermute(head, "tm", back) for head in heads_of(voltages, widths)]
-    early = exchanged(first_frame(dests, voltages, gain, window, table))
+    heads = [head_of(voltages, (TAPS - 2) * L)]
+    first, head = first_frame(dests, voltages, gain, window, table)
+    later = [lax.ppermute(block, "tm", back) for block in (*heads, head)]
+    early = exchanged(first)
 
     steer = steering(input_feed, beam_grid, jnp.asarray(steer_grid(input_feed.shape[0])), SUB)
     parts = ()

time: 96.6 us -> 93.1 us (0.964)
  local copies, waits for them, and re-layouts: 2.39 us -> 0.05 us
    unnamed x30 -> x16, local copies, waits for them, and re-layouts: 2.39 us -> 0.05 us
  transfers between devices with their start and end apart: 14 -> 14, of which waited for: 8 -> 8; matrix products, arithmetic and copies ran while one was open for 0% -> 0% of each run, Pallas kernels for 29% -> 30%
where the time goes in v4:
time: 93.1 us; the launch traced here: 92.7 us
  Pallas kernels  45 us (48%)
  starting transfers between devices  30.1 us (32%)
  waiting for transfers between devices  16.8 us (18%)
    pallas_call x2, Pallas kernels, products(): pl.pallas_call(functools.partial(products_kernel, n_time, n_input, frame_...  29.5 us
    all_to_all x2, starting transfers between devices, exchanged(): return lax.all_to_all(block, AXES, 0, 0, tiled=True)  13.3 us
    ppermute x10, starting transfers between devices, onward(): lax.ppermute(block, axis, [(i, (i + distance) % devices) for i in range(d...  12.7 us
    ppermute x10, waiting for transfers between devices, onward(): lax.ppermute(block, axis, [(i, (i + distance) % devices) for i in range(d...  11.5 us
    pallas_call x3, Pallas kernels, later_frame(): pl.pallas_call(functools.partial(later_kernel, frame, len(later), len(cut...  5.47 us
    ppermute x2, waiting for transfers between devices, in_pieces(): later = [lax.ppermute(block, 'tm', back) for block in (*heads, head)]  5.3 us
    ppermute x2, starting transfers between devices, in_pieces(): later = [lax.ppermute(block, 'tm', back) for block in (*heads, head)]  4.13 us
    pallas_call x1, Pallas kernels, first_frame(): pl.pallas_call(first_kernel, in_specs=[far] * 4, out_specs=[pl.BlockSpec(...  3.93 us
  transfers between devices with their start and end apart: 14, of which 8 were waited for; matrix products, arithmetic and copies ran while one was open for 0% of the time, Pallas kernels for 30%

profile of v4, /device:TPU:1, one launch (start us, length us, event | category | flops | bytes accessed | tf_op | source)
XLA Modules:
  0.0 92.7 jit_solution(16248801239844190318)
XLA Ops:
  0.6 0.0 copy-start.7
  0.6 0.0 copy-start.6
  0.7 0.0 copy-start.5
  0.7 2.1 %head.1 = bf16[256,2048]{1,0:T(8,128)(2,1)} custom-call(bf16[256,4096]{1,0:T(8,128)(2,1)} %v_ref.9), custom_call_target="tpu_custom_call" | custom-call | bytes 2097152 | tf_op jit(solution)/shard_map/head/pallas_call | solution.py:94
  2.7 2.0 %collective-permute-start = (bf16[256,2048]{1,0:T(8,128)(2,1)}, bf16[256,2048]{1,0:T(8,128)(2,1)S(1)}, u32[]{:S(2)}, u32[]{:S(2)}) collective-permute-start(bf16[256,2048]{1,0:T(8,128)(2,1)} %head.1), channel_id=1, source_target_pairs={{4,0},{8,4},{12,8},{16,12},{20,16},{24,20},{28,24},{5,1},{9,5},{13... | collective-permute-start | bytes 3145736 | tf_op jit(solution)/shard_map/ppermute | solution.py:497
  4.7 3.9 %first_frame.1 = (bf16[32,32,256]{2,1,0:T(8,128)(2,1)}, bf16[256,1024]{1,0:T(8,128)(2,1)}) custom-call(bf16[256,4096]{1,0:T(8,128)(2,1)} %v_ref.9, f32[1,256]{1,0:T(1,128)} %bitcast.3, f32[4,1024]{1,0:T(4,128)} %constant.6.clone.window_ref, bf16[1024,1024]{1,0:T(8,128)(2,1)} %constant.7.clone.table_ref), custom_call_target="tpu_custom_call" | custom-call | flops 536870912 | bytes 4194304 | tf_op jit(solution)/shard_map/first_frame/pallas_call | solution.py:135
  8.6 7.2 %all-to-all-start = ((bf16[32,32,256]{2,1,0:T(8,128)(2,1)}), bf16[32,32,256]{2,1,0:T(8,128)(2,1)S(1)}, u32[]{:S(2)}, u32[]{:S(2)}) async-start(bf16[32,32,256]{2,1,0:T(8,128)(2,1)} %get-tuple-element.39), calls=%async_computation | async-start | bytes 1048576 | tf_op jit(solution)/shard_map/all_to_all | solution.py:471
  15.9 2.2 %collective-permute-start.1 = (bf16[256,1024]{1,0:T(8,128)(2,1)}, bf16[256,1024]{1,0:T(8,128)(2,1)S(1)}, u32[]{:S(2)}, u32[]{:S(2)}) collective-permute-start(bf16[256,1024]{1,0:T(8,128)(2,1)} %get-tuple-element.35), channel_id=1, source_target_pairs={{4,0},{8,4},{12,8},{16,12},{20,16},{24,20},{28,24},{5,1},{9,5},{13... | collective-permute-start | bytes 1572872 | tf_op jit(solution)/shard_map/ppermute | solution.py:497
  18.0 0.0 copy-done.7
  18.1 0.0 copy-done.6
  18.1 0.0 copy-done.5
  18.1 0.0 copy-start
  18.1 0.0 copy-start.1
  18.1 0.0 copy-start.3
  18.1 0.0 copy-start.4
  18.1 3.9 %steering.1.steer_ref = bf16[4,1024,512]{2,1,0:T(8,128)(2,1)S(1)} custom-call(s32[1,1024]{1,0:T(1,128)S(1)} %bitcast.7, s32[1,1024]{1,0:T(1,128)S(1)} %bitcast.8, bf16[2,512,512]{2,1,0:T(8,128)(2,1)S(1)} %copy-done.7), custom_call_target="tpu_custom_call" | custom-call | flops 3221225472 | bytes 4194304 | tf_op jit(solution)/shard_map/steering/pallas_call | solution.py:275
  22.0 0.0 copy-start.2
  22.0 0.5 collective-permute-done.refs_0_
  22.6 0.0 copy-done
  22.6 0.0 copy-done.1
  22.6 0.0 copy-done.3
  22.6 0.0 copy-done.4
  22.6 1.8 %later_frame.3 = (bf16[32,3,16,256]{3,2,1,0:T(8,128)(2,1)}, bf16[32,3,16,256]{3,2,1,0:T(8,128)(2,1)S(1)}) custom-call(bf16[256,4096]{1,0:T(8,128)(2,1)S(1)} %copy-done, f32[1,256]{1,0:T(1,128)S(1)} %bitcast.4, f32[4,1024]{1,0:T(4,128)S(1)} %copy-done.3, bf16[1024,1024]{1,0:T(8,128)(2,1)S(1)} %copy-done.1, bf16[256,2048]{1,0:T(8,128)(2,1)S(1)} %collective-permute-done.refs_0_), custom_call_target="tpu_custom_call" | custom-call | flops 536870912 | bytes 3145728 | tf_op jit(solution)/shard_map/later_frame/pallas_call | solution.py:231
  24.4 1.8 %later_frame.4 = (bf16[32,3,16,256]{3,2,1,0:T(8,128)(2,1)}, bf16[32,3,16,256]{3,2,1,0:T(8,128)(2,1)S(1)}) custom-call(bf16[256,4096]{1,0:T(8,128)(2,1)S(1)} %copy-done, f32[1,256]{1,0:T(1,128)S(1)} %bitcast.5, f32[4,1024]{1,0:T(4,128)S(1)} %copy-done.3, bf16[1024,1024]{1,0:T(8,128)(2,1)S(1)} %copy-done.1, ...), custom_call_target="tpu_custom_call", output_to_operand_aliasing={{0}: (5, {}), {1}: (6, {})} | custom-call | flops 536870912 | bytes 3145728 | tf_op jit(solution)/shard_map/later_frame/pallas_call | solution.py:231
  26.2 0.0 copy-done.2
  26.2 4.8 %collective-permute-done.1.refs_1_ = bf16[256,1024]{1,0:T(8,128)(2,1)S(1)} collective-permute-done((bf16[256,1024]{1,0:T(8,128)(2,1)}, bf16[256,1024]{1,0:T(8,128)(2,1)S(1)}, u32[]{:S(2)}, u32[]{:S(2)}) %collective-permute-start.1) | collective-permute-done | bytes 524320 | tf_op jit(solution)/shard_map/ppermute | solution.py:497
  31.0 1.8 %later_frame.5 = (bf16[32,3,16,256]{3,2,1,0:T(8,128)(2,1)}, bf16[32,3,16,256]{3,2,1,0:T(8,128)(2,1)S(1)}) custom-call(bf16[256,4096]{1,0:T(8,128)(2,1)S(1)} %copy-done, f32[1,256]{1,0:T(1,128)S(1)} %bitcast.6, f32[4,1024]{1,0:T(4,128)S(1)} %copy-done.3, bf16[1024,1024]{1,0:T(8,128)(2,1)S(1)} %copy-done.1, ...), custom_call_target="tpu_custom_call", output_to_operand_aliasing={{0}: (6, {}), {1}: (7, {})} | custom-call | flops 536870912 | bytes 3145728 | tf_op jit(solution)/shard_map/later_frame/pallas_call | solution.py:231
  32.8 0.0 all-to-all-done.rest_0_
  32.8 6.0 %all-to-all-start.1 = ((bf16[32,3,16,256]{3,2,1,0:T(8,128)(2,1)}), bf16[32,3,16,256]{3,2,1,0:T(8,128)(2,1)S(1)}, u32[]{:S(2)}, u32[]{:S(2)}) async-start(bf16[32,3,16,256]{3,2,1,0:T(8,128)(2,1)} %get-tuple-element.54), calls=%async_computation.1 | async-start | bytes 1572864 | tf_op jit(solution)/shard_map/all_to_all | solution.py:471
  38.9 0.1 to_tm.1
  39.0 1.7 %collective-permute-start.2 = (bf16[4,48,256]{2,1,0:T(8,128)(2,1)S(1)}, bf16[4,48,256]{2,1,0:T(8,128)(2,1)S(1)}, u32[]{:S(2)}, u32[]{:S(2)}) collective-permute-start(bf16[4,48,256]{2,1,0:T(8,128)(2,1)S(1)} %get-tuple-element.43), channel_id=1, source_target_pairs={{0,4},{4,8},{8,12},{12,16},{16,20},{20,24},{24,28},{28,0},{1,5},{5... | collective-permute-start | bytes 294920 | tf_op jit(solution)/shard_map/ppermute | solution.py:478
  40.6 1.2 %collective-permute-start.3 = (bf16[4,48,256]{2,1,0:T(8,128)(2,1)S(1)}, bf16[4,48,256]{2,1,0:T(8,128)(2,1)S(1)}, u32[]{:S(2)}, u32[]{:S(2)}) collective-permute-start(bf16[4,48,256]{2,1,0:T(8,128)(2,1)S(1)} %get-tuple-element.44), channel_id=1, source_target_pairs={{0,8},{4,12},{8,16},{12,20},{16,24},{20,28},{24,0},{28,4},{1,9},{5... | collective-permute-start | bytes 294920 | tf_op jit(solution)/shard_map/ppermute | solution.py:478
  41.8 0.4 collective-permute-start.4
  42.3 0.3 collective-permute-start.5
  42.5 2.3 %collective-permute-start.6 = (bf16[4,48,256]{2,1,0:T(8,128)(2,1)S(1)}, bf16[4,48,256]{2,1,0:T(8,128)(2,1)S(1)}, u32[]{:S(2)}, u32[]{:S(2)}) collective-permute-start(bf16[4,48,256]{2,1,0:T(8,128)(2,1)S(1)} %get-tuple-element.47), channel_id=1, source_target_pairs={{0,20},{4,24},{8,28},{12,0},{16,4},{20,8},{24,12},{28,16},{1,21},{... | collective-permute-start | bytes 294920 | tf_op jit(solution)/shard_map/ppermute | solution.py:478
  44.8 0.9 collective-permute-done.2.refs_1_
  45.7 2.1 %collective-permute-start.7 = (bf16[4,48,256]{2,1,0:T(8,128)(2,1)S(1)}, bf16[4,48,256]{2,1,0:T(8,128)(2,1)S(1)}, u32[]{:S(2)}, u32[]{:S(2)}) collective-permute-start(bf16[4,48,256]{2,1,0:T(8,128)(2,1)S(1)} %get-tuple-element.48), channel_id=1, source_target_pairs={{0,24},{4,28},{8,0},{12,4},{16,8},{20,12},{24,16},{28,20},{1,25},{... | collective-permute-start | bytes 294920 | tf_op jit(solution)/shard_map/ppermute | solution.py:478
  47.7 4.7 %collective-permute-done.3.refs_2_ = bf16[4,48,256]{2,1,0:T(8,128)(2,1)S(1)} collective-permute-done((bf16[4,48,256]{2,1,0:T(8,128)(2,1)S(1)}, bf16[4,48,256]{2,1,0:T(8,128)(2,1)S(1)}, u32[]{:S(2)}, u32[]{:S(2)}) %collective-permute-start.3) | collective-permute-done | bytes 98336 | tf_op jit(solution)/shard_map/ppermute | solution.py:478
  52.4 0.0 collective-permute-start.8
  52.4 1.2 %collective-permute-done.4.refs_3_ = bf16[4,48,256]{2,1,0:T(8,128)(2,1)S(1)} collective-permute-done((bf16[4,48,256]{2,1,0:T(8,128)(2,1)S(1)}, bf16[4,48,256]{2,1,0:T(8,128)(2,1)S(1)}, u32[]{:S(2)}, u32[]{:S(2)}) %collective-permute-start.4) | collective-permute-done | bytes 98336 | tf_op jit(solution)/shard_map/ppermute | solution.py:478
  53.7 4.4 %collective-permute-done.5.refs_4_ = bf16[4,48,256]{2,1,0:T(8,128)(2,1)S(1)} collective-permute-done((bf16[4,48,256]{2,1,0:T(8,128)(2,1)S(1)}, bf16[4,48,256]{2,1,0:T(8,128)(2,1)S(1)}, u32[]{:S(2)}, u32[]{:S(2)}) %collective-permute-start.5) | collective-permute-done | bytes 98336 | tf_op jit(solution)/shard_map/ppermute | solution.py:478
  58.1 0.2 collective-permute-done.6.refs_5_
  58.2 0.0 collective-permute-done.7.refs_6_
  58.2 0.1 collective-permute-done.8.refs_7_
  58.3 0.1 to_inp.1
  58.4 2.2 %collective-permute-start.9 = (bf16[8,48,256]{2,1,0:T(8,128)(2,1)S(1)}, bf16[8,48,256]{2,1,0:T(8,128)(2,1)S(1)}, u32[]{:S(2)}, u32[]{:S(2)}) collective-permute-start(bf16[8,48,256]{2,1,0:T(8,128)(2,1)S(1)} %get-tuple-element.51), channel_id=1, source_target_pairs={{0,1},{1,2},{2,3},{3,0},{4,5},{5,6},{6,7},{7,4},{8,9},{9,10},{10,1... | collective-permute-start | bytes 589832 | tf_op jit(solution)/shard_map/ppermute | solution.py:478
  60.6 1.1 %collective-permute-start.10 = (bf16[8,48,256]{2,1,0:T(8,128)(2,1)S(1)}, bf16[8,48,256]{2,1,0:T(8,128)(2,1)S(1)}, u32[]{:S(2)}, u32[]{:S(2)}) collective-permute-start(bf16[8,48,256]{2,1,0:T(8,128)(2,1)S(1)} %get-tuple-element.52), channel_id=1, source_target_pairs={{0,2},{1,3},{2,0},{3,1},{4,6},{5,7},{6,4},{7,5},{8,10},{9,11},{10,... | collective-permute-start | bytes 589832 | tf_op jit(solution)/shard_map/ppermute | solution.py:478
  61.7 1.4 %collective-permute-start.11 = (bf16[8,48,256]{2,1,0:T(8,128)(2,1)S(1)}, bf16[8,48,256]{2,1,0:T(8,128)(2,1)S(1)}, u32[]{:S(2)}, u32[]{:S(2)}) collective-permute-start(bf16[8,48,256]{2,1,0:T(8,128)(2,1)S(1)} %get-tuple-element.53), channel_id=1, source_target_pairs={{0,3},{1,0},{2,1},{3,2},{4,7},{5,4},{6,5},{7,6},{8,11},{9,8},{10,9... | collective-permute-start | bytes 589832 | tf_op jit(solution)/shard_map/ppermute | solution.py:478
  63.1 0.0 all-to-all-done.1.rest_1_
  63.1 14.2 %products.2 = (bf16[16,2,1024,1024]{3,2,1,0:T(8,128)(2,1)}, f32[16,1024]{1,0:T(8,128)}) custom-call(bf16[4,1024,512]{2,1,0:T(8,128)(2,1)} %copy-done.2, bf16[32,32,256]{2,1,0:T(8,128)(2,1)S(1)} %all-to-all-done.rest_0_, bf16[32,3,16,256]{3,2,1,0:T(8,128)(2,1)S(1)} %all-to-all-done.1.rest_1_), custom_call_target="tpu_custom_call" | custom-call | flops 4294967296 | bytes 37748736 | tf_op jit(solution)/shard_map/products/pallas_call | solution.py:441
  77.4 0.0 collective-permute-done.9.rest_2_
  77.4 0.0 collective-permute-done.10.rest_3_
  77.4 0.0 collective-permute-done.11.rest_4_
  77.4 15.3 %products.3 = (bf16[16,2,1024,1024]{3,2,1,0:T(8,128)(2,1)}, f32[16,1024]{1,0:T(8,128)}) custom-call(bf16[4,1024,512]{2,1,0:T(8,128)(2,1)} %copy-done.2, bf16[32,32,256]{2,1,0:T(8,128)(2,1)S(1)} %all-to-all-done.rest_0_, bf16[8,48,256]{2,1,0:T(8,128)(2,1)S(1)} %get-tuple-element.50.rest_1_, ...), custom_call_target="tpu_custom_call", output_to_operand_aliasing={{0}: (6, {}), {1}: (7, {})} | custom-call | flops 4294967296 | bytes 37748736 | tf_op jit(solution)/shard_map/products/pallas_call | solution.py:441
Async XLA Ops:
  0.6 17.4 %copy-start.7 = (bf16[2,512,512]{2,1,0:T(8,128)(2,1)S(1)}, bf16[2,512,512]{2,1,0:T(8,128)(2,1)}, u32[]{:S(2)}) copy-start(bf16[2,512,512]{2,1,0:T(8,128)(2,1)} %constant.8.clone.table_ref) | copy-start | bytes 3145732
  0.6 17.4 %copy-start.6 = (s32[1024]{0:T(1024)S(1)}, s32[1024]{0:T(1024)}, u32[]{:S(2)}) copy-start(s32[1024]{0:T(1024)} %param.10) | copy-start | bytes 12292
  0.7 17.4 %copy-start.5 = (s32[1024]{0:T(1024)S(1)}, s32[1024]{0:T(1024)}, u32[]{:S(2)}) copy-start(s32[1024]{0:T(1024)} %param.9) | copy-start | bytes 12292
  2.7 19.8 %collective-permute-start = (bf16[256,2048]{1,0:T(8,128)(2,1)}, bf16[256,2048]{1,0:T(8,128)(2,1)S(1)}, u32[]{:S(2)}, u32[]{:S(2)}) collective-permute-start(bf16[256,2048]{1,0:T(8,128)(2,1)} %head.1), channel_id=1, source_target_pairs={{4,0},{8,4},{12,8},{16,12},{20,16},{24,20},{28,24},{5,1},{9,5},{13... | collective-permute-start | bytes 3145736 | tf_op jit(solution)/shard_map/ppermute | solution.py:497
  8.6 24.2 %all-to-all-start = ((bf16[32,32,256]{2,1,0:T(8,128)(2,1)}), bf16[32,32,256]{2,1,0:T(8,128)(2,1)S(1)}, u32[]{:S(2)}, u32[]{:S(2)}) async-start(bf16[32,32,256]{2,1,0:T(8,128)(2,1)} %get-tuple-element.39), calls=%async_computation | async-start | bytes 1048576 | tf_op jit(solution)/shard_map/all_to_all | solution.py:471
  15.9 15.1 %collective-permute-start.1 = (bf16[256,1024]{1,0:T(8,128)(2,1)}, bf16[256,1024]{1,0:T(8,128)(2,1)S(1)}, u32[]{:S(2)}, u32[]{:S(2)}) collective-permute-start(bf16[256,1024]{1,0:T(8,128)(2,1)} %get-tuple-element.35), channel_id=1, source_target_pairs={{4,0},{8,4},{12,8},{16,12},{20,16},{24,20},{28,24},{5,1},{9,5},{13... | collective-permute-start | bytes 1572872 | tf_op jit(solution)/shard_map/ppermute | solution.py:497
  18.1 4.5 %copy-start = (bf16[256,4096]{1,0:T(8,128)(2,1)S(1)}, bf16[256,4096]{1,0:T(8,128)(2,1)}, u32[]{:S(2)}) copy-start(bf16[256,4096]{1,0:T(8,128)(2,1)} %v_ref.9) | copy-start | bytes 6291460
  18.1 4.5 %copy-start.1 = (bf16[1024,1024]{1,0:T(8,128)(2,1)S(1)}, bf16[1024,1024]{1,0:T(8,128)(2,1)}, u32[]{:S(2)}) copy-start(bf16[1024,1024]{1,0:T(8,128)(2,1)} %constant.7.clone.table_ref) | copy-start | bytes 6291460
  18.1 4.5 %copy-start.3 = (f32[4,1024]{1,0:T(4,128)S(1)}, f32[4,1024]{1,0:T(4,128)}, u32[]{:S(2)}) copy-start(f32[4,1024]{1,0:T(4,128)} %constant.6.clone.window_ref) | copy-start | bytes 49156
  18.1 4.5 %copy-start.4 = (f32[256]{0:T(256)S(1)}, f32[256]{0:T(256)}, u32[]{:S(2)}) copy-start(f32[256]{0:T(256)} %param.8) | copy-start | bytes 3076
  22.0 4.2 %copy-start.2 = (bf16[4,1024,512]{2,1,0:T(8,128)(2,1)}, bf16[4,1024,512]{2,1,0:T(8,128)(2,1)S(1)}, u32[]{:S(2)}) copy-start(bf16[4,1024,512]{2,1,0:T(8,128)(2,1)S(1)} %steering.1.steer_ref) | copy-start | bytes 12582916
  32.8 30.3 %all-to-all-start.1 = ((bf16[32,3,16,256]{3,2,1,0:T(8,128)(2,1)}), bf16[32,3,16,256]{3,2,1,0:T(8,128)(2,1)S(1)}, u32[]{:S(2)}, u32[]{:S(2)}) async-start(bf16[32,3,16,256]{3,2,1,0:T(8,128)(2,1)} %get-tuple-element.54), calls=%async_computation.1 | async-start | bytes 1572864 | tf_op jit(solution)/shard_map/all_to_all | solution.py:471
  39.0 6.7 %collective-permute-start.2 = (bf16[4,48,256]{2,1,0:T(8,128)(2,1)S(1)}, bf16[4,48,256]{2,1,0:T(8,128)(2,1)S(1)}, u32[]{:S(2)}, u32[]{:S(2)}) collective-permute-start(bf16[4,48,256]{2,1,0:T(8,128)(2,1)S(1)} %get-tuple-element.43), channel_id=1, source_target_pairs={{0,4},{4,8},{8,12},{12,16},{16,20},{20,24},{24,28},{28,0},{1,5},{5... | collective-permute-start | bytes 294920 | tf_op jit(solution)/shard_map/ppermute | solution.py:478
  40.6 11.8 %collective-permute-start.3 = (bf16[4,48,256]{2,1,0:T(8,128)(2,1)S(1)}, bf16[4,48,256]{2,1,0:T(8,128)(2,1)S(1)}, u32[]{:S(2)}, u32[]{:S(2)}) collective-permute-start(bf16[4,48,256]{2,1,0:T(8,128)(2,1)S(1)} %get-tuple-element.44), channel_id=1, source_target_pairs={{0,8},{4,12},{8,16},{12,20},{16,24},{20,28},{24,0},{28,4},{1,9},{5... | collective-permute-start | bytes 294920 | tf_op jit(solution)/shard_map/ppermute | solution.py:478
  41.8 11.8 %collective-permute-start.4 = (bf16[4,48,256]{2,1,0:T(8,128)(2,1)S(1)}, bf16[4,48,256]{2,1,0:T(8,128)(2,1)S(1)}, u32[]{:S(2)}, u32[]{:S(2)}) collective-permute-start(bf16[4,48,256]{2,1,0:T(8,128)(2,1)S(1)} %get-tuple-element.45), channel_id=1, source_target_pairs={{0,12},{4,16},{8,20},{12,24},{16,28},{20,0},{24,4},{28,8},{1,13},{... | collective-permute-start | bytes 294920 | tf_op jit(solution)/shard_map/ppermute | solution.py:478
  42.3 15.8 %collective-permute-start.5 = (bf16[4,48,256]{2,1,0:T(8,128)(2,1)S(1)}, bf16[4,48,256]{2,1,0:T(8,128)(2,1)S(1)}, u32[]{:S(2)}, u32[]{:S(2)}) collective-permute-start(bf16[4,48,256]{2,1,0:T(8,128)(2,1)S(1)} %get-tuple-element.46), channel_id=1, source_target_pairs={{0,16},{4,20},{8,24},{12,28},{16,0},{20,4},{24,8},{28,12},{1,17},{... | collective-permute-start | bytes 294920 | tf_op jit(solution)/shard_map/ppermute | solution.py:478
  42.5 15.7 %collective-permute-start.6 = (bf16[4,48,256]{2,1,0:T(8,128)(2,1)S(1)}, bf16[4,48,256]{2,1,0:T(8,128)(2,1)S(1)}, u32[]{:S(2)}, u32[]{:S(2)}) collective-permute-start(bf16[4,48,256]{2,1,0:T(8,128)(2,1)S(1)} %get-tuple-element.47), channel_id=1, source_target_pairs={{0,20},{4,24},{8,28},{12,0},{16,4},{20,8},{24,12},{28,16},{1,21},{... | collective-permute-start | bytes 294920 | tf_op jit(solution)/shard_map/ppermute | solution.py:478
  45.7 12.6 %collective-permute-start.7 = (bf16[4,48,256]{2,1,0:T(8,128)(2,1)S(1)}, bf16[4,48,256]{2,1,0:T(8,128)(2,1)S(1)}, u32[]{:S(2)}, u32[]{:S(2)}) collective-permute-start(bf16[4,48,256]{2,1,0:T(8,128)(2,1)S(1)} %get-tuple-element.48), channel_id=1, source_target_pairs={{0,24},{4,28},{8,0},{12,4},{16,8},{20,12},{24,16},{28,20},{1,25},{... | collective-permute-start | bytes 294920 | tf_op jit(solution)/shard_map/ppermute | solution.py:478
  52.4 5.9 %collective-permute-start.8 = (bf16[4,48,256]{2,1,0:T(8,128)(2,1)S(1)}, bf16[4,48,256]{2,1,0:T(8,128)(2,1)S(1)}, u32[]{:S(2)}, u32[]{:S(2)}) collective-permute-start(bf16[4,48,256]{2,1,0:T(8,128)(2,1)S(1)} %get-tuple-element.49), channel_id=1, source_target_pairs={{0,28},{4,0},{8,4},{12,8},{16,12},{20,16},{24,20},{28,24},{1,29},{... | collective-permute-start | bytes 294920 | tf_op jit(solution)/shard_map/ppermute | solution.py:478
  58.4 19.0 %collective-permute-start.9 = (bf16[8,48,256]{2,1,0:T(8,128)(2,1)S(1)}, bf16[8,48,256]{2,1,0:T(8,128)(2,1)S(1)}, u32[]{:S(2)}, u32[]{:S(2)}) collective-permute-start(bf16[8,48,256]{2,1,0:T(8,128)(2,1)S(1)} %get-tuple-element.51), channel_id=1, source_target_pairs={{0,1},{1,2},{2,3},{3,0},{4,5},{5,6},{6,7},{7,4},{8,9},{9,10},{10,1... | collective-permute-start | bytes 589832 | tf_op jit(solution)/shard_map/ppermute | solution.py:478
  60.6 16.7 %collective-permute-start.10 = (bf16[8,48,256]{2,1,0:T(8,128)(2,1)S(1)}, bf16[8,48,256]{2,1,0:T(8,128)(2,1)S(1)}, u32[]{:S(2)}, u32[]{:S(2)}) collective-permute-start(bf16[8,48,256]{2,1,0:T(8,128)(2,1)S(1)} %get-tuple-element.52), channel_id=1, source_target_pairs={{0,2},{1,3},{2,0},{3,1},{4,6},{5,7},{6,4},{7,5},{8,10},{9,11},{10,... | collective-permute-start | bytes 589832 | tf_op jit(solution)/shard_map/ppermute | solution.py:478
  61.7 15.7 %collective-permute-start.11 = (bf16[8,48,256]{2,1,0:T(8,128)(2,1)S(1)}, bf16[8,48,256]{2,1,0:T(8,128)(2,1)S(1)}, u32[]{:S(2)}, u32[]{:S(2)}) collective-permute-start(bf16[8,48,256]{2,1,0:T(8,128)(2,1)S(1)} %get-tuple-element.53), channel_id=1, source_target_pairs={{0,3},{1,0},{2,1},{3,2},{4,7},{5,4},{6,5},{7,6},{8,11},{9,8},{10,9... | collective-permute-start | bytes 589832 | tf_op jit(solution)/shard_map/ppermute | solution.py:478

commit v5 on v4

--- a/solution.py
+++ b/solution.py
@@ -312,6 +312,7 @@
 
     @pl.when(step == 0)
     def _():
+        steer_copy(0).start()
         rows = slice(start, start + early.shape[1])
         copies = [pltpu.make_async_copy(early_ref.at[:, rows], early, in_sems.at[0])]
         copies += [
@@ -319,7 +320,6 @@
         ]
         for copy in copies:
             copy.start()
-        steer_copy(0).start()
         if shared:
             power_ref[...] = earlier_ref[...]
         for copy in copies:

time: 93.1 us -> 92.2 us (level)
    pallas_call x2, Pallas kernels: 29.5 us -> 28.6 us  [products(): pl.pallas_call(functools.partial(products_kernel, n_time, n_input, frame_...]
where the time goes in v5:
time: 92.2 us; the launch traced here: 91.8 us
  Pallas kernels  44.1 us (48%)
  starting transfers between devices  30.1 us (33%)
  waiting for transfers between devices  16.8 us (18%)
    pallas_call x2, Pallas kernels, products(): pl.pallas_call(functools.partial(products_kernel, n_time, n_input, frame_...  28.6 us
    all_to_all x2, starting transfers between devices, exchanged(): return lax.all_to_all(block, AXES, 0, 0, tiled=True)  13.3 us
    ppermute x10, starting transfers between devices, onward(): lax.ppermute(block, axis, [(i, (i + distance) % devices) for i in range(d...  12.7 us
    ppermute x10, waiting for transfers between devices, onward(): lax.ppermute(block, axis, [(i, (i + distance) % devices) for i in range(d...  11.5 us
    pallas_call x3, Pallas kernels, later_frame(): pl.pallas_call(functools.partial(later_kernel, frame, len(later), len(cut...  5.47 us
    ppermute x2, waiting for transfers between devices, in_pieces(): later = [lax.ppermute(block, 'tm', back) for block in (*heads, head)]  5.3 us
    ppermute x2, starting transfers between devices, in_pieces(): later = [lax.ppermute(block, 'tm', back) for block in (*heads, head)]  4.13 us
    pallas_call x1, Pallas kernels, first_frame(): pl.pallas_call(first_kernel, in_specs=[far] * 4, out_specs=[pl.BlockSpec(...  3.93 us
  transfers between devices with their start and end apart: 14, of which 8 were waited for; matrix products, arithmetic and copies ran while one was open for 0% of the time, Pallas kernels for 30%

profile of v5, /device:TPU:1, one launch (start us, length us, event | category | flops | bytes accessed | tf_op | source)
XLA Modules:
  0.0 91.8 jit_solution(3763947346082205922)
XLA Ops:
  0.6 0.0 copy-start.7
  0.6 0.0 copy-start.6
  0.7 0.0 copy-start.5
  0.7 2.1 %head.1 = bf16[256,2048]{1,0:T(8,128)(2,1)} custom-call(bf16[256,4096]{1,0:T(8,128)(2,1)} %v_ref.9), custom_call_target="tpu_custom_call" | custom-call | bytes 2097152 | tf_op jit(solution)/shard_map/head/pallas_call | solution.py:94
  2.7 2.0 %collective-permute-start = (bf16[256,2048]{1,0:T(8,128)(2,1)}, bf16[256,2048]{1,0:T(8,128)(2,1)S(1)}, u32[]{:S(2)}, u32[]{:S(2)}) collective-permute-start(bf16[256,2048]{1,0:T(8,128)(2,1)} %head.1), channel_id=1, source_target_pairs={{4,0},{8,4},{12,8},{16,12},{20,16},{24,20},{28,24},{5,1},{9,5},{13... | collective-permute-start | bytes 3145736 | tf_op jit(solution)/shard_map/ppermute | solution.py:497
  4.7 3.9 %first_frame.1 = (bf16[32,32,256]{2,1,0:T(8,128)(2,1)}, bf16[256,1024]{1,0:T(8,128)(2,1)}) custom-call(bf16[256,4096]{1,0:T(8,128)(2,1)} %v_ref.9, f32[1,256]{1,0:T(1,128)} %bitcast.3, f32[4,1024]{1,0:T(4,128)} %constant.6.clone.window_ref, bf16[1024,1024]{1,0:T(8,128)(2,1)} %constant.7.clone.table_ref), custom_call_target="tpu_custom_call" | custom-call | flops 536870912 | bytes 4194304 | tf_op jit(solution)/shard_map/first_frame/pallas_call | solution.py:135
  8.6 7.2 %all-to-all-start = ((bf16[32,32,256]{2,1,0:T(8,128)(2,1)}), bf16[32,32,256]{2,1,0:T(8,128)(2,1)S(1)}, u32[]{:S(2)}, u32[]{:S(2)}) async-start(bf16[32,32,256]{2,1,0:T(8,128)(2,1)} %get-tuple-element.39), calls=%async_computation | async-start | bytes 1048576 | tf_op jit(solution)/shard_map/all_to_all | solution.py:471
  15.9 2.2 %collective-permute-start.1 = (bf16[256,1024]{1,0:T(8,128)(2,1)}, bf16[256,1024]{1,0:T(8,128)(2,1)S(1)}, u32[]{:S(2)}, u32[]{:S(2)}) collective-permute-start(bf16[256,1024]{1,0:T(8,128)(2,1)} %get-tuple-element.35), channel_id=1, source_target_pairs={{4,0},{8,4},{12,8},{16,12},{20,16},{24,20},{28,24},{5,1},{9,5},{13... | collective-permute-start | bytes 1572872 | tf_op jit(solution)/shard_map/ppermute | solution.py:497
  18.0 0.0 copy-done.7
  18.1 0.0 copy-done.6
  18.1 0.0 copy-done.5
  18.1 0.0 copy-start
  18.1 0.0 copy-start.1
  18.1 0.0 copy-start.3
  18.1 0.0 copy-start.4
  18.1 3.9 %steering.1.steer_ref = bf16[4,1024,512]{2,1,0:T(8,128)(2,1)S(1)} custom-call(s32[1,1024]{1,0:T(1,128)S(1)} %bitcast.7, s32[1,1024]{1,0:T(1,128)S(1)} %bitcast.8, bf16[2,512,512]{2,1,0:T(8,128)(2,1)S(1)} %copy-done.7), custom_call_target="tpu_custom_call" | custom-call | flops 3221225472 | bytes 4194304 | tf_op jit(solution)/shard_map/steering/pallas_call | solution.py:275
  22.0 0.0 copy-start.2
  22.0 0.5 collective-permute-done.refs_0_
  22.6 0.0 copy-done
  22.6 0.0 copy-done.1
  22.6 0.0 copy-done.3
  22.6 0.0 copy-done.4
  22.6 1.8 %later_frame.3 = (bf16[32,3,16,256]{3,2,1,0:T(8,128)(2,1)}, bf16[32,3,16,256]{3,2,1,0:T(8,128)(2,1)S(1)}) custom-call(bf16[256,4096]{1,0:T(8,128)(2,1)S(1)} %copy-done, f32[1,256]{1,0:T(1,128)S(1)} %bitcast.4, f32[4,1024]{1,0:T(4,128)S(1)} %copy-done.3, bf16[1024,1024]{1,0:T(8,128)(2,1)S(1)} %copy-done.1, bf16[256,2048]{1,0:T(8,128)(2,1)S(1)} %collective-permute-done.refs_0_), custom_call_target="tpu_custom_call" | custom-call | flops 536870912 | bytes 3145728 | tf_op jit(solution)/shard_map/later_frame/pallas_call | solution.py:231
  24.4 1.8 %later_frame.4 = (bf16[32,3,16,256]{3,2,1,0:T(8,128)(2,1)}, bf16[32,3,16,256]{3,2,1,0:T(8,128)(2,1)S(1)}) custom-call(bf16[256,4096]{1,0:T(8,128)(2,1)S(1)} %copy-done, f32[1,256]{1,0:T(1,128)S(1)} %bitcast.5, f32[4,1024]{1,0:T(4,128)S(1)} %copy-done.3, bf16[1024,1024]{1,0:T(8,128)(2,1)S(1)} %copy-done.1, ...), custom_call_target="tpu_custom_call", output_to_operand_aliasing={{0}: (5, {}), {1}: (6, {})} | custom-call | flops 536870912 | bytes 3145728 | tf_op jit(solution)/shard_map/later_frame/pallas_call | solution.py:231
  26.2 0.0 copy-done.2
  26.2 4.8 %collective-permute-done.1.refs_1_ = bf16[256,1024]{1,0:T(8,128)(2,1)S(1)} collective-permute-done((bf16[256,1024]{1,0:T(8,128)(2,1)}, bf16[256,1024]{1,0:T(8,128)(2,1)S(1)}, u32[]{:S(2)}, u32[]{:S(2)}) %collective-permute-start.1) | collective-permute-done | bytes 524320 | tf_op jit(solution)/shard_map/ppermute | solution.py:497
  31.0 1.8 %later_frame.5 = (bf16[32,3,16,256]{3,2,1,0:T(8,128)(2,1)}, bf16[32,3,16,256]{3,2,1,0:T(8,128)(2,1)S(1)}) custom-call(bf16[256,4096]{1,0:T(8,128)(2,1)S(1)} %copy-done, f32[1,256]{1,0:T(1,128)S(1)} %bitcast.6, f32[4,1024]{1,0:T(4,128)S(1)} %copy-done.3, bf16[1024,1024]{1,0:T(8,128)(2,1)S(1)} %copy-done.1, ...), custom_call_target="tpu_custom_call", output_to_operand_aliasing={{0}: (6, {}), {1}: (7, {})} | custom-call | flops 536870912 | bytes 3145728 | tf_op jit(solution)/shard_map/later_frame/pallas_call | solution.py:231
  32.8 0.0 all-to-all-done.rest_0_
  32.8 6.0 %all-to-all-start.1 = ((bf16[32,3,16,256]{3,2,1,0:T(8,128)(2,1)}), bf16[32,3,16,256]{3,2,1,0:T(8,128)(2,1)S(1)}, u32[]{:S(2)}, u32[]{:S(2)}) async-start(bf16[32,3,16,256]{3,2,1,0:T(8,128)(2,1)} %get-tuple-element.54), calls=%async_computation.1 | async-start | bytes 1572864 | tf_op jit(solution)/shard_map/all_to_all | solution.py:471
  38.9 0.1 to_tm.1
  39.0 1.7 %collective-permute-start.2 = (bf16[4,48,256]{2,1,0:T(8,128)(2,1)S(1)}, bf16[4,48,256]{2,1,0:T(8,128)(2,1)S(1)}, u32[]{:S(2)}, u32[]{:S(2)}) collective-permute-start(bf16[4,48,256]{2,1,0:T(8,128)(2,1)S(1)} %get-tuple-element.43), channel_id=1, source_target_pairs={{0,4},{4,8},{8,12},{12,16},{16,20},{20,24},{24,28},{28,0},{1,5},{5... | collective-permute-start | bytes 294920 | tf_op jit(solution)/shard_map/ppermute | solution.py:478
  40.6 1.2 %collective-permute-start.3 = (bf16[4,48,256]{2,1,0:T(8,128)(2,1)S(1)}, bf16[4,48,256]{2,1,0:T(8,128)(2,1)S(1)}, u32[]{:S(2)}, u32[]{:S(2)}) collective-permute-start(bf16[4,48,256]{2,1,0:T(8,128)(2,1)S(1)} %get-tuple-element.44), channel_id=1, source_target_pairs={{0,8},{4,12},{8,16},{12,20},{16,24},{20,28},{24,0},{28,4},{1,9},{5... | collective-permute-start | bytes 294920 | tf_op jit(solution)/shard_map/ppermute | solution.py:478
  41.8 0.4 collective-permute-start.4
  42.3 0.3 collective-permute-start.5
  42.5 2.3 %collective-permute-start.6 = (bf16[4,48,256]{2,1,0:T(8,128)(2,1)S(1)}, bf16[4,48,256]{2,1,0:T(8,128)(2,1)S(1)}, u32[]{:S(2)}, u32[]{:S(2)}) collective-permute-start(bf16[4,48,256]{2,1,0:T(8,128)(2,1)S(1)} %get-tuple-element.47), channel_id=1, source_target_pairs={{0,20},{4,24},{8,28},{12,0},{16,4},{20,8},{24,12},{28,16},{1,21},{... | collective-permute-start | bytes 294920 | tf_op jit(solution)/shard_map/ppermute | solution.py:478
  44.8 0.9 collective-permute-done.2.refs_1_
  45.7 2.1 %collective-permute-start.7 = (bf16[4,48,256]{2,1,0:T(8,128)(2,1)S(1)}, bf16[4,48,256]{2,1,0:T(8,128)(2,1)S(1)}, u32[]{:S(2)}, u32[]{:S(2)}) collective-permute-start(bf16[4,48,256]{2,1,0:T(8,128)(2,1)S(1)} %get-tuple-element.48), channel_id=1, source_target_pairs={{0,24},{4,28},{8,0},{12,4},{16,8},{20,12},{24,16},{28,20},{1,25},{... | collective-permute-start | bytes 294920 | tf_op jit(solution)/shard_map/ppermute | solution.py:478
  47.7 4.7 %collective-permute-done.3.refs_2_ = bf16[4,48,256]{2,1,0:T(8,128)(2,1)S(1)} collective-permute-done((bf16[4,48,256]{2,1,0:T(8,128)(2,1)S(1)}, bf16[4,48,256]{2,1,0:T(8,128)(2,1)S(1)}, u32[]{:S(2)}, u32[]{:S(2)}) %collective-permute-start.3) | collective-permute-done | bytes 98336 | tf_op jit(solution)/shard_map/ppermute | solution.py:478
  52.4 0.0 collective-permute-start.8
  52.4 1.2 %collective-permute-done.4.refs_3_ = bf16[4,48,256]{2,1,0:T(8,128)(2,1)S(1)} collective-permute-done((bf16[4,48,256]{2,1,0:T(8,128)(2,1)S(1)}, bf16[4,48,256]{2,1,0:T(8,128)(2,1)S(1)}, u32[]{:S(2)}, u32[]{:S(2)}) %collective-permute-start.4) | collective-permute-done | bytes 98336 | tf_op jit(solution)/shard_map/ppermute | solution.py:478
  53.7 4.4 %collective-permute-done.5.refs_4_ = bf16[4,48,256]{2,1,0:T(8,128)(2,1)S(1)} collective-permute-done((bf16[4,48,256]{2,1,0:T(8,128)(2,1)S(1)}, bf16[4,48,256]{2,1,0:T(8,128)(2,1)S(1)}, u32[]{:S(2)}, u32[]{:S(2)}) %collective-permute-start.5) | collective-permute-done | bytes 98336 | tf_op jit(solution)/shard_map/ppermute | solution.py:478
  58.1 0.2 collective-permute-done.6.refs_5_
  58.2 0.0 collective-permute-done.7.refs_6_
  58.2 0.1 collective-permute-done.8.refs_7_
  58.3 0.1 to_inp.1
  58.4 2.2 %collective-permute-start.9 = (bf16[8,48,256]{2,1,0:T(8,128)(2,1)S(1)}, bf16[8,48,256]{2,1,0:T(8,128)(2,1)S(1)}, u32[]{:S(2)}, u32[]{:S(2)}) collective-permute-start(bf16[8,48,256]{2,1,0:T(8,128)(2,1)S(1)} %get-tuple-element.51), channel_id=1, source_target_pairs={{0,1},{1,2},{2,3},{3,0},{4,5},{5,6},{6,7},{7,4},{8,9},{9,10},{10,1... | collective-permute-start | bytes 589832 | tf_op jit(solution)/shard_map/ppermute | solution.py:478
  60.6 1.1 %collective-permute-start.10 = (bf16[8,48,256]{2,1,0:T(8,128)(2,1)S(1)}, bf16[8,48,256]{2,1,0:T(8,128)(2,1)S(1)}, u32[]{:S(2)}, u32[]{:S(2)}) collective-permute-start(bf16[8,48,256]{2,1,0:T(8,128)(2,1)S(1)} %get-tuple-element.52), channel_id=1, source_target_pairs={{0,2},{1,3},{2,0},{3,1},{4,6},{5,7},{6,4},{7,5},{8,10},{9,11},{10,... | collective-permute-start | bytes 589832 | tf_op jit(solution)/shard_map/ppermute | solution.py:478
  61.7 1.4 %collective-permute-start.11 = (bf16[8,48,256]{2,1,0:T(8,128)(2,1)S(1)}, bf16[8,48,256]{2,1,0:T(8,128)(2,1)S(1)}, u32[]{:S(2)}, u32[]{:S(2)}) collective-permute-start(bf16[8,48,256]{2,1,0:T(8,128)(2,1)S(1)} %get-tuple-element.53), channel_id=1, source_target_pairs={{0,3},{1,0},{2,1},{3,2},{4,7},{5,4},{6,5},{7,6},{8,11},{9,8},{10,9... | collective-permute-start | bytes 589832 | tf_op jit(solution)/shard_map/ppermute | solution.py:478
  63.1 0.0 all-to-all-done.1.rest_1_
  63.1 14.1 %products.2 = (bf16[16,2,1024,1024]{3,2,1,0:T(8,128)(2,1)}, f32[16,1024]{1,0:T(8,128)}) custom-call(bf16[4,1024,512]{2,1,0:T(8,128)(2,1)} %copy-done.2, bf16[32,32,256]{2,1,0:T(8,128)(2,1)S(1)} %all-to-all-done.rest_0_, bf16[32,3,16,256]{3,2,1,0:T(8,128)(2,1)S(1)} %all-to-all-done.1.rest_1_), custom_call_target="tpu_custom_call" | custom-call | flops 4294967296 | bytes 37748736 | tf_op jit(solution)/shard_map/products/pallas_call | solution.py:441
  77.3 0.0 collective-permute-done.9.rest_2_
  77.3 0.0 collective-permute-done.10.rest_3_
  77.3 0.0 collective-permute-done.11.rest_4_
  77.3 14.5 %products.3 = (bf16[16,2,1024,1024]{3,2,1,0:T(8,128)(2,1)}, f32[16,1024]{1,0:T(8,128)}) custom-call(bf16[4,1024,512]{2,1,0:T(8,128)(2,1)} %copy-done.2, bf16[32,32,256]{2,1,0:T(8,128)(2,1)S(1)} %all-to-all-done.rest_0_, bf16[8,48,256]{2,1,0:T(8,128)(2,1)S(1)} %get-tuple-element.50.rest_1_, ...), custom_call_target="tpu_custom_call", output_to_operand_aliasing={{0}: (6, {}), {1}: (7, {})} | custom-call | flops 4294967296 | bytes 37748736 | tf_op jit(solution)/shard_map/products/pallas_call | solution.py:441
Async XLA Ops:
  0.6 17.4 %copy-start.7 = (bf16[2,512,512]{2,1,0:T(8,128)(2,1)S(1)}, bf16[2,512,512]{2,1,0:T(8,128)(2,1)}, u32[]{:S(2)}) copy-start(bf16[2,512,512]{2,1,0:T(8,128)(2,1)} %constant.8.clone.table_ref) | copy-start | bytes 3145732
  0.6 17.4 %copy-start.6 = (s32[1024]{0:T(1024)S(1)}, s32[1024]{0:T(1024)}, u32[]{:S(2)}) copy-start(s32[1024]{0:T(1024)} %param.10) | copy-start | bytes 12292
  0.7 17.4 %copy-start.5 = (s32[1024]{0:T(1024)S(1)}, s32[1024]{0:T(1024)}, u32[]{:S(2)}) copy-start(s32[1024]{0:T(1024)} %param.9) | copy-start | bytes 12292
  2.7 19.8 %collective-permute-start = (bf16[256,2048]{1,0:T(8,128)(2,1)}, bf16[256,2048]{1,0:T(8,128)(2,1)S(1)}, u32[]{:S(2)}, u32[]{:S(2)}) collective-permute-start(bf16[256,2048]{1,0:T(8,128)(2,1)} %head.1), channel_id=1, source_target_pairs={{4,0},{8,4},{12,8},{16,12},{20,16},{24,20},{28,24},{5,1},{9,5},{13... | collective-permute-start | bytes 3145736 | tf_op jit(solution)/shard_map/ppermute | solution.py:497
  8.6 24.2 %all-to-all-start = ((bf16[32,32,256]{2,1,0:T(8,128)(2,1)}), bf16[32,32,256]{2,1,0:T(8,128)(2,1)S(1)}, u32[]{:S(2)}, u32[]{:S(2)}) async-start(bf16[32,32,256]{2,1,0:T(8,128)(2,1)} %get-tuple-element.39), calls=%async_computation | async-start | bytes 1048576 | tf_op jit(solution)/shard_map/all_to_all | solution.py:471
  15.9 15.1 %collective-permute-start.1 = (bf16[256,1024]{1,0:T(8,128)(2,1)}, bf16[256,1024]{1,0:T(8,128)(2,1)S(1)}, u32[]{:S(2)}, u32[]{:S(2)}) collective-permute-start(bf16[256,1024]{1,0:T(8,128)(2,1)} %get-tuple-element.35), channel_id=1, source_target_pairs={{4,0},{8,4},{12,8},{16,12},{20,16},{24,20},{28,24},{5,1},{9,5},{13... | collective-permute-start | bytes 1572872 | tf_op jit(solution)/shard_map/ppermute | solution.py:497
  18.1 4.5 %copy-start = (bf16[256,4096]{1,0:T(8,128)(2,1)S(1)}, bf16[256,4096]{1,0:T(8,128)(2,1)}, u32[]{:S(2)}) copy-start(bf16[256,4096]{1,0:T(8,128)(2,1)} %v_ref.9) | copy-start | bytes 6291460
  18.1 4.5 %copy-start.1 = (bf16[1024,1024]{1,0:T(8,128)(2,1)S(1)}, bf16[1024,1024]{1,0:T(8,128)(2,1)}, u32[]{:S(2)}) copy-start(bf16[1024,1024]{1,0:T(8,128)(2,1)} %constant.7.clone.table_ref) | copy-start | bytes 6291460
  18.1 4.5 %copy-start.3 = (f32[4,1024]{1,0:T(4,128)S(1)}, f32[4,1024]{1,0:T(4,128)}, u32[]{:S(2)}) copy-start(f32[4,1024]{1,0:T(4,128)} %constant.6.clone.window_ref) | copy-start | bytes 49156
  18.1 4.5 %copy-start.4 = (f32[256]{0:T(256)S(1)}, f32[256]{0:T(256)}, u32[]{:S(2)}) copy-start(f32[256]{0:T(256)} %param.8) | copy-start | bytes 3076
  22.0 4.2 %copy-start.2 = (bf16[4,1024,512]{2,1,0:T(8,128)(2,1)}, bf16[4,1024,512]{2,1,0:T(8,128)(2,1)S(1)}, u32[]{:S(2)}) copy-start(bf16[4,1024,512]{2,1,0:T(8,128)(2,1)S(1)} %steering.1.steer_ref) | copy-start | bytes 12582916
  32.8 30.3 %all-to-all-start.1 = ((bf16[32,3,16,256]{3,2,1,0:T(8,128)(2,1)}), bf16[32,3,16,256]{3,2,1,0:T(8,128)(2,1)S(1)}, u32[]{:S(2)}, u32[]{:S(2)}) async-start(bf16[32,3,16,256]{3,2,1,0:T(8,128)(2,1)} %get-tuple-element.54), calls=%async_computation.1 | async-start | bytes 1572864 | tf_op jit(solution)/shard_map/all_to_all | solution.py:471
  39.0 6.7 %collective-permute-start.2 = (bf16[4,48,256]{2,1,0:T(8,128)(2,1)S(1)}, bf16[4,48,256]{2,1,0:T(8,128)(2,1)S(1)}, u32[]{:S(2)}, u32[]{:S(2)}) collective-permute-start(bf16[4,48,256]{2,1,0:T(8,128)(2,1)S(1)} %get-tuple-element.43), channel_id=1, source_target_pairs={{0,4},{4,8},{8,12},{12,16},{16,20},{20,24},{24,28},{28,0},{1,5},{5... | collective-permute-start | bytes 294920 | tf_op jit(solution)/shard_map/ppermute | solution.py:478
  40.6 11.8 %collective-permute-start.3 = (bf16[4,48,256]{2,1,0:T(8,128)(2,1)S(1)}, bf16[4,48,256]{2,1,0:T(8,128)(2,1)S(1)}, u32[]{:S(2)}, u32[]{:S(2)}) collective-permute-start(bf16[4,48,256]{2,1,0:T(8,128)(2,1)S(1)} %get-tuple-element.44), channel_id=1, source_target_pairs={{0,8},{4,12},{8,16},{12,20},{16,24},{20,28},{24,0},{28,4},{1,9},{5... | collective-permute-start | bytes 294920 | tf_op jit(solution)/shard_map/ppermute | solution.py:478
  41.8 11.8 %collective-permute-start.4 = (bf16[4,48,256]{2,1,0:T(8,128)(2,1)S(1)}, bf16[4,48,256]{2,1,0:T(8,128)(2,1)S(1)}, u32[]{:S(2)}, u32[]{:S(2)}) collective-permute-start(bf16[4,48,256]{2,1,0:T(8,128)(2,1)S(1)} %get-tuple-element.45), channel_id=1, source_target_pairs={{0,12},{4,16},{8,20},{12,24},{16,28},{20,0},{24,4},{28,8},{1,13},{... | collective-permute-start | bytes 294920 | tf_op jit(solution)/shard_map/ppermute | solution.py:478
  42.3 15.8 %collective-permute-start.5 = (bf16[4,48,256]{2,1,0:T(8,128)(2,1)S(1)}, bf16[4,48,256]{2,1,0:T(8,128)(2,1)S(1)}, u32[]{:S(2)}, u32[]{:S(2)}) collective-permute-start(bf16[4,48,256]{2,1,0:T(8,128)(2,1)S(1)} %get-tuple-element.46), channel_id=1, source_target_pairs={{0,16},{4,20},{8,24},{12,28},{16,0},{20,4},{24,8},{28,12},{1,17},{... | collective-permute-start | bytes 294920 | tf_op jit(solution)/shard_map/ppermute | solution.py:478
  42.5 15.7 %collective-permute-start.6 = (bf16[4,48,256]{2,1,0:T(8,128)(2,1)S(1)}, bf16[4,48,256]{2,1,0:T(8,128)(2,1)S(1)}, u32[]{:S(2)}, u32[]{:S(2)}) collective-permute-start(bf16[4,48,256]{2,1,0:T(8,128)(2,1)S(1)} %get-tuple-element.47), channel_id=1, source_target_pairs={{0,20},{4,24},{8,28},{12,0},{16,4},{20,8},{24,12},{28,16},{1,21},{... | collective-permute-start | bytes 294920 | tf_op jit(solution)/shard_map/ppermute | solution.py:478
  45.7 12.6 %collective-permute-start.7 = (bf16[4,48,256]{2,1,0:T(8,128)(2,1)S(1)}, bf16[4,48,256]{2,1,0:T(8,128)(2,1)S(1)}, u32[]{:S(2)}, u32[]{:S(2)}) collective-permute-start(bf16[4,48,256]{2,1,0:T(8,128)(2,1)S(1)} %get-tuple-element.48), channel_id=1, source_target_pairs={{0,24},{4,28},{8,0},{12,4},{16,8},{20,12},{24,16},{28,20},{1,25},{... | collective-permute-start | bytes 294920 | tf_op jit(solution)/shard_map/ppermute | solution.py:478
  52.4 5.9 %collective-permute-start.8 = (bf16[4,48,256]{2,1,0:T(8,128)(2,1)S(1)}, bf16[4,48,256]{2,1,0:T(8,128)(2,1)S(1)}, u32[]{:S(2)}, u32[]{:S(2)}) collective-permute-start(bf16[4,48,256]{2,1,0:T(8,128)(2,1)S(1)} %get-tuple-element.49), channel_id=1, source_target_pairs={{0,28},{4,0},{8,4},{12,8},{16,12},{20,16},{24,20},{28,24},{1,29},{... | collective-permute-start | bytes 294920 | tf_op jit(solution)/shard_map/ppermute | solution.py:478
  58.4 18.9 %collective-permute-start.9 = (bf16[8,48,256]{2,1,0:T(8,128)(2,1)S(1)}, bf16[8,48,256]{2,1,0:T(8,128)(2,1)S(1)}, u32[]{:S(2)}, u32[]{:S(2)}) collective-permute-start(bf16[8,48,256]{2,1,0:T(8,128)(2,1)S(1)} %get-tuple-element.51), channel_id=1, source_target_pairs={{0,1},{1,2},{2,3},{3,0},{4,5},{5,6},{6,7},{7,4},{8,9},{9,10},{10,1... | collective-permute-start | bytes 589832 | tf_op jit(solution)/shard_map/ppermute | solution.py:478
  60.6 16.7 %collective-permute-start.10 = (bf16[8,48,256]{2,1,0:T(8,128)(2,1)S(1)}, bf16[8,48,256]{2,1,0:T(8,128)(2,1)S(1)}, u32[]{:S(2)}, u32[]{:S(2)}) collective-permute-start(bf16[8,48,256]{2,1,0:T(8,128)(2,1)S(1)} %get-tuple-element.52), channel_id=1, source_target_pairs={{0,2},{1,3},{2,0},{3,1},{4,6},{5,7},{6,4},{7,5},{8,10},{9,11},{10,... | collective-permute-start | bytes 589832 | tf_op jit(solution)/shard_map/ppermute | solution.py:478
  61.7 15.6 %collective-permute-start.11 = (bf16[8,48,256]{2,1,0:T(8,128)(2,1)S(1)}, bf16[8,48,256]{2,1,0:T(8,128)(2,1)S(1)}, u32[]{:S(2)}, u32[]{:S(2)}) collective-permute-start(bf16[8,48,256]{2,1,0:T(8,128)(2,1)S(1)} %get-tuple-element.53), channel_id=1, source_target_pairs={{0,3},{1,0},{2,1},{3,2},{4,7},{5,4},{6,5},{7,6},{8,11},{9,8},{10,9... | collective-permute-start | bytes 589832 | tf_op jit(solution)/shard_map/ppermute | solution.py:478
